TPU v7x, 32 devices: a whole 2x2x4 slice. The times are simulated.
32 devices in a mesh: tile: 16 (over z, y, x), plane: 2 (over core).
Axes of the slice: x: 2, y: 2, z: 4, core: 2. Of those that a mesh axis runs over, the one named last changes fastest.
Arguments:
- ref_feat: bfloat16 [32, 4, 4096], P(None, None, 'tile'), may hold values from -6 to 6
- src_feat: bfloat16 [4, 32, 4, 4096], P(None, 'plane', None, 'tile'), may hold values from -6 to 6
- shifts: int32 [4, 16], P(None, 'plane'), may hold values from 0 to 128, as said below
- conv_one: bfloat16 [8, 8, 3, 3, 3], replicated, may hold values from -0.4375 to 0.4375
- bias_one: float32 [8], replicated, may hold values from -0.5 to 0.5
- conv_two: bfloat16 [8, 8, 3, 3, 3], replicated, may hold values from -0.4375 to 0.4375
- bias_two: float32 [8], replicated, may hold values from -0.5 to 0.5
- view_head: float32 [8], replicated, may hold values from -2 to 2
Outputs:
- joined: bfloat16 [8, 16, 4, 4096], P(None, 'plane', None, 'tile')
Inputs may be any that keep to these rules, and one draw needn't show every extreme that they name: `shifts`: for every view the shift never falls from one plane to the next; it is 0 at plane 0 and 128 at plane 16 - 1.
All inputs are finite; a program needn't handle non-finite values.
Results may differ from a plain program's by a relative error of at most 0.0053.
Values may be sent and summed in bfloat16 or wider, within the bound.
No kernel may reach another device: no remote copies, remote signals or barrier semaphores. Data moves between devices by JAX's collectives and lax.ppermute only.
A program may use at most 64 MiB of HBM per device.

v0:
```python
import jax
import jax.numpy as jnp
from jax import lax
from jax.sharding import PartitionSpec as P

CHANNELS = 32
GROUPS = 8
VIEWS = 4
MAX_SHIFT = 128


def padded(cells, sides, width):
    for axis, dim in sides:
        count = lax.axis_size(axis)
        ends = count - 1
        head = lax.slice_in_dim(cells, 0, width, axis=dim)
        tail = lax.slice_in_dim(cells, cells.shape[dim] - width, cells.shape[dim], axis=dim)
        cells = jnp.concatenate(
            [
                lax.ppermute(tail, axis, [(i, (i + 1) % count) for i in range(ends)]),
                cells,
                lax.ppermute(head, axis, [((i + 1) % count, i) for i in range(ends)]),
            ],
            axis=dim,
        )
    return cells


def from_behind(value, axis, by):
    peers = lax.axis_size(axis)
    pairs = [(i, i + by) for i in range(peers) if 0 <= i + by < peers]
    return lax.ppermute(value, axis, pairs)


def convolve_valid(volume, kernel):
    return lax.conv_general_dilated(
        volume[None],
        kernel,
        (1, 1, 1),
        "VALID",
        dimension_numbers=("NCDHW", "OIDHW", "NCDHW"),
        preferred_element_type=jnp.float32,
    )[0]


def margin_single(volume):
    return padded(volume, (("tile", 3), ("plane", 1)), 1)


def pad_rows(volume, depth):
    return jnp.pad(volume, ((0, 0), (0, 0), (depth, depth), (0, 0)))


def per_device(ref_feat, src_feat, shifts, conv_one, bias_one, conv_two, bias_two, view_head):
    tile_cols = ref_feat.shape[2]
    row_count = ref_feat.shape[1]
    planes = shifts.shape[1]
    gathered_all = lax.all_gather(src_feat, "plane", axis=1, tiled=True)
    before = from_behind(gathered_all[:, :, :, tile_cols - MAX_SHIFT :], "tile", 1)
    gathered = jnp.concatenate([before, gathered_all], axis=3)
    ref_wide = ref_feat.astype(jnp.float32)
    weighted = jnp.zeros((GROUPS, planes, row_count, tile_cols), jnp.float32)
    total_weight = jnp.zeros((planes, row_count, tile_cols), jnp.float32)
    for view_idx in range(VIEWS):
        source = gathered[view_idx]

        def one_plane(offset):
            start = MAX_SHIFT - offset
            shifted = lax.dynamic_slice_in_dim(source, start, tile_cols, 2).astype(jnp.float32)
            products = (ref_wide * shifted).reshape(
                GROUPS, CHANNELS // GROUPS, row_count, tile_cols
            )
            return jnp.mean(products, axis=1)

        matches = jnp.transpose(lax.map(one_plane, shifts[view_idx]), (1, 0, 2, 3)).astype(
            jnp.bfloat16
        )
        first_raw = convolve_valid(pad_rows(margin_single(matches), 1), conv_one)
        first_core = jax.nn.relu(first_raw + bias_one[:, None, None, None]).astype(jnp.bfloat16)
        first_out = pad_rows(margin_single(first_core), 1)
        second_out = jax.nn.relu(
            convolve_valid(first_out, conv_two) + bias_two[:, None, None, None]
        )
        scores = jnp.einsum("c,cdhw->dhw", view_head, second_out)
        weight = jax.nn.sigmoid(scores)
        weighted = weighted + weight[None] * matches.astype(jnp.float32)
        total_weight = total_weight + weight
    return (weighted / total_weight[None]).astype(jnp.bfloat16)


def solution(mesh):
    placed = (
        P(None, None, "tile"),
        P(None, "plane", None, "tile"),
        P(None, "plane"),
        P(),
        P(),
        P(),
        P(),
        P(),
    )
    return jax.shard_map(
        per_device,
        mesh=mesh,
        in_specs=placed,
        out_specs=P(None, "plane", None, "tile"),
        check_vma=False,
    )
```

profile of v0, /device:TPU:25, one launch (start us, length us, event | category | flops | bytes accessed | tf_op | source)
XLA Modules:
  0.0 338.8 jit_solution(13270971516612633139)
XLA Ops:
  0.0 2.7 all_gather.3
  2.8 3.1 collective-permute-start
  7.6 3.6 %collective-permute-done = bf16[4,32,4,128]{3,2,1,0:T(4,128)(2,1)S(1)} collective-permute-done((bf16[4,32,4,128]{3,2,1,0:T(4,128)(2,1)S(1)}, bf16[4,32,4,128]{3,2,1,0:T(4,128)(2,1)S(1)}, u32[]{:S(2)}, u32[]{:S(2)}) %collective-permute-start) | collective-permute-done | bytes 131104 | tf_op jit(solution)/shard_map/ppermute | solution.py:32
  11.6 16.5 %while.48 = (s32[]{:T(128)}, bf16[8,8,4,256]{3,2,0,1:T(4,128)(2,1)S(1)}, s32[8]{0:T(128)S(1)}, bf16[32,4,384]{2,1,0:T(4,128)(2,1)S(1)}, f32[32,4,256]{2,1,0:T(4,...) while((s32[]{:T(128)}, bf16[8,8,4,256]{3,2,0,1:T(4,128)(2,1)S(1)}, s32[8]{0:T(128)S(1)}, ...), condition=%wide.region_2.3_spmd, body=%wide.region_0.2_spmd.sunk | while | flops 98310 | bytes 295071 | solution.py:75
  30.2 5.2 %collective-permute-start.2 = (bf16[8,8,4,1]{3,2,1,0:T(4,128)(2,1)S(1)}, bf16[8,8,4,1]{3,2,1,0:T(4,128)(2,1)S(1)}, u32[]{:S(2)}, u32[]{:S(2)}) collective-permute-start(bf16[8,8,4,1]{3,2,1,0:T(4,128)(2,1)S(1)} %get-tuple-element.404), channel_id=1, source_target_pairs={{2,0},{4,2},{6,4},{8,6},{10,8},{12,10},{14,12},{16,14},{18,16},{20... | collective-permute-start | bytes 1544 | tf_op jit(solution)/shard_map/ppermute | solution.py:22
  35.4 16.5 %while.50 = (s32[]{:T(128)}, bf16[8,8,4,256]{3,2,0,1:T(4,128)(2,1)S(1)}, s32[8]{0:T(128)S(1)}, bf16[32,4,384]{2,1,0:T(4,128)(2,1)S(1)}, f32[32,4,256]{2,1,0:T(4,...) while((s32[]{:T(128)}, bf16[8,8,4,256]{3,2,0,1:T(4,128)(2,1)S(1)}, s32[8]{0:T(128)S(1)}, ...), condition=%wide.region_8.9_spmd, body=%wide.region_6.8_spmd.sunk | while | flops 98310 | bytes 295071 | solution.py:75
  54.0 5.2 %collective-permute-start.18 = (bf16[8,8,4,1]{3,2,1,0:T(4,128)(2,1)S(1)}, bf16[8,8,4,1]{3,2,1,0:T(4,128)(2,1)S(1)}, u32[]{:S(2)}, u32[]{:S(2)}) collective-permute-start(bf16[8,8,4,1]{3,2,1,0:T(4,128)(2,1)S(1)} %get-tuple-element.396), channel_id=1, source_target_pairs={{2,0},{4,2},{6,4},{8,6},{10,8},{12,10},{14,12},{16,14},{18,16},{20... | collective-permute-start | bytes 1544 | tf_op jit(solution)/shard_map/ppermute | solution.py:22
  59.2 15.0 %while.49 = (s32[]{:T(128)}, bf16[8,8,4,256]{3,2,0,1:T(4,128)(2,1)S(1)}, s32[8]{0:T(128)S(1)}, bf16[32,4,384]{2,1,0:T(4,128)(2,1)S(1)}, f32[32,4,256]{2,1,0:T(4,...) while((s32[]{:T(128)}, bf16[8,8,4,256]{3,2,0,1:T(4,128)(2,1)S(1)}, s32[8]{0:T(128)S(1)}, ...), condition=%wide.region_5.6_spmd, body=%wide.region_3.5_spmd.sunk | while | flops 98310 | bytes 295071 | solution.py:75
  76.3 16.7 %while.51 = (s32[]{:T(128)}, bf16[8,8,4,256]{3,2,0,1:T(4,128)(2,1)S(1)}, s32[8]{0:T(128)S(1)}, bf16[32,4,384]{2,1,0:T(4,128)(2,1)S(1)}, f32[32,4,256]{2,1,0:T(4,...) while((s32[]{:T(128)}, bf16[8,8,4,256]{3,2,0,1:T(4,128)(2,1)S(1)}, s32[8]{0:T(128)S(1)}, ...), condition=%wide.region_11.12_spmd, body=%wide.region_9.11_spmd.sunk | while | flops 98310 | bytes 295071 | solution.py:75
  93.1 3.4 collective-permute-start.9
  96.4 1.9 collective-permute-start.25
  98.5 5.2 %collective-permute-start.26 = (bf16[8,8,4,1]{3,2,1,0:T(4,128)(2,1)S(1)}, bf16[8,8,4,1]{3,2,1,0:T(4,128)(2,1)S(1)}, u32[]{:S(2)}, u32[]{:S(2)}) collective-permute-start(bf16[8,8,4,1]{3,2,1,0:T(4,128)(2,1)S(1)} %get-tuple-element.392), channel_id=1, source_target_pairs={{2,0},{4,2},{6,4},{8,6},{10,8},{12,10},{14,12},{16,14},{18,16},{20... | collective-permute-start | bytes 1544 | tf_op jit(solution)/shard_map/ppermute | solution.py:22
  105.1 5.3 %collective-permute-start.4 = (bf16[8,1,4,258]{3,2,1,0:T(4,128)(2,1)S(1)}, bf16[8,1,4,258]{3,2,1,0:T(4,128)(2,1)S(1)}, u32[]{:S(2)}, u32[]{:S(2)}) collective-permute-start(bf16[8,1,4,258]{3,2,1,0:T(4,128)(2,1)S(1)} %get-tuple-element.388), channel_id=1, source_target_pairs={{1,0},{3,2},{5,4},{7,6},{9,8},{11,10},{13,12},{15,14},{17,16},{19,... | collective-permute-start | bytes 49544 | tf_op jit(solution)/shard_map/ppermute | solution.py:22
  111.9 3.0 collective-permute-start.20
  116.3 3.0 collective-permute-start.12
  122.2 4.7 %copy.97 = bf16[8,10,6,1,8,33]{0,4,5,2,1,3:T(8,128)(2,1)} copy(bf16[8,10,6,1,8,33]{5,4,2,1,0,3:T(8,128)(2,1)S(1)} %reshape.199) | data formatting | bytes 506880 | tf_op jit(solution)/shard_map/conv_general_dilated | solution.py:36
  127.9 3.6 %collective-permute-start.28 = (bf16[8,1,4,258]{3,2,1,0:T(4,128)(2,1)S(1)}, bf16[8,1,4,258]{3,2,1,0:T(4,128)(2,1)S(1)}, u32[]{:S(2)}, u32[]{:S(2)}) collective-permute-start(bf16[8,1,4,258]{3,2,1,0:T(4,128)(2,1)S(1)} %get-tuple-element.376), channel_id=1, source_target_pairs={{1,0},{3,2},{5,4},{7,6},{9,8},{11,10},{13,12},{15,14},{17,16},{19,... | collective-permute-start | bytes 49544 | tf_op jit(solution)/shard_map/ppermute | solution.py:22
  132.9 4.7 %copy.115 = bf16[8,10,6,1,8,33]{0,4,5,2,1,3:T(8,128)(2,1)} copy(bf16[8,10,6,1,8,33]{5,4,2,1,0,3:T(8,128)(2,1)S(1)} %reshape.201) | data formatting | bytes 506880 | tf_op jit(solution)/shard_map/conv_general_dilated | solution.py:36
  138.6 9.9 %broadcast_select_fusion.7 = f32[8,4,8,33,8]{4,2,3,1,0:T(8,128)} fusion(pred[8,33]{0,1:T(8,128)(4,1)S(1)} %copy-done.11, bf16[8,8,3,3,3]{1,0,4,3,2:T(8,128)(2,1)S(1)} %copy-done, bf16[8,10,6,1,7,2]{0,4,5,2,1,3:T(8,128)(2,1)S(1)} %slice.184, bf16[8,10,6,1,8,33]{0,4,5,2,1,3:T(8,128)(2,1)} %copy.97), kind=kOutput, calls=%fused_computation.76 | convolution fusion | flops 30070272 | bytes 540936 | tf_op jit(solution)/shard_map/conv_general_dilated | solution.py:36
  148.6 7.4 %broadcast_select_fusion.3 = f32[8,4,8,33,8]{4,2,3,1,0:T(8,128)} fusion(pred[8,33]{0,1:T(8,128)(4,1)S(1)} %copy-done.11, bf16[8,8,3,3,3]{1,0,4,3,2:T(8,128)(2,1)S(1)} %copy-done, bf16[8,10,6,1,7,2]{0,4,5,2,1,3:T(8,128)(2,1)S(1)} %slice.202, bf16[8,10,6,1,8,33]{0,4,5,2,1,3:T(8,128)(2,1)S(1)} %copy-done.2), kind=kOutput, calls=%fused_computation.72 | convolution fusion | flops 30070272 | bytes 540936 | tf_op jit(solution)/shard_map/conv_general_dilated | solution.py:36
  157.5 4.6 %copy.106 = bf16[8,10,6,1,8,33]{0,4,5,2,1,3:T(8,128)(2,1)} copy(bf16[8,10,6,1,8,33]{5,4,2,1,0,3:T(8,128)(2,1)S(1)} %reshape.200) | data formatting | bytes 506880 | tf_op jit(solution)/shard_map/conv_general_dilated | solution.py:36
  163.1 10.1 %broadcast_select_fusion.5 = f32[8,4,8,33,8]{4,2,3,1,0:T(8,128)} fusion(pred[8,33]{0,1:T(8,128)(4,1)S(1)} %copy-done.11, bf16[8,8,3,3,3]{1,0,4,3,2:T(8,128)(2,1)S(1)} %copy-done, bf16[8,10,6,1,7,2]{0,4,5,2,1,3:T(8,128)(2,1)S(1)} %slice.193, bf16[8,10,6,1,8,33]{0,4,5,2,1,3:T(8,128)(2,1)} %copy.106), kind=kOutput, calls=%fused_computation.74 | convolution fusion | flops 30070272 | bytes 540936 | tf_op jit(solution)/shard_map/conv_general_dilated | solution.py:36
  173.2 3.5 %copy.98 = f32[8,4,8,33,8]{3,2,4,1,0:T(8,128)S(1)} copy(f32[8,4,8,33,8]{4,2,3,1,0:T(8,128)} %broadcast_select_fusion.7) | data formatting | bytes 540672 | tf_op jit(solution)/shard_map/conv_general_dilated | solution.py:36
  176.9 3.5 %copy.116 = f32[8,4,8,33,8]{3,2,4,1,0:T(8,128)S(1)} copy(f32[8,4,8,33,8]{4,2,3,1,0:T(8,128)} %broadcast_select_fusion.3) | data formatting | bytes 540672 | tf_op jit(solution)/shard_map/conv_general_dilated | solution.py:36
  180.7 3.5 %copy.107 = f32[8,4,8,33,8]{3,2,4,1,0:T(8,128)S(1)} copy(f32[8,4,8,33,8]{4,2,3,1,0:T(8,128)} %broadcast_select_fusion.5) | data formatting | bytes 540672 | tf_op jit(solution)/shard_map/conv_general_dilated | solution.py:36
  186.0 4.7 %copy.124 = bf16[8,10,6,1,8,33]{0,4,5,2,1,3:T(8,128)(2,1)} copy(bf16[8,10,6,1,8,33]{5,4,2,1,0,3:T(8,128)(2,1)S(1)} %reshape.202) | data formatting | bytes 506880 | tf_op jit(solution)/shard_map/conv_general_dilated | solution.py:36
  191.7 9.8 %broadcast_select_fusion.1 = f32[8,4,8,33,8]{4,2,3,1,0:T(8,128)} fusion(pred[8,33]{0,1:T(8,128)(4,1)S(1)} %copy-done.11, bf16[8,8,3,3,3]{1,0,4,3,2:T(8,128)(2,1)S(1)} %copy-done, bf16[8,10,6,1,7,2]{0,4,5,2,1,3:T(8,128)(2,1)S(1)} %slice.211, bf16[8,10,6,1,8,33]{0,4,5,2,1,3:T(8,128)(2,1)} %copy.124), kind=kOutput, calls=%fused_computation.70 | convolution fusion | flops 30070272 | bytes 540936 | tf_op jit(solution)/shard_map/conv_general_dilated | solution.py:36
  201.5 3.7 %copy.125 = f32[8,4,8,33,8]{3,2,4,1,0:T(8,128)S(1)} copy(f32[8,4,8,33,8]{4,2,3,1,0:T(8,128)} %broadcast_select_fusion.1) | data formatting | bytes 540672 | tf_op jit(solution)/shard_map/conv_general_dilated | solution.py:36
  209.4 5.2 %collective-permute-start.14 = (bf16[8,8,4,1]{3,0,2,1:T(8,128)(2,1)S(1)}, bf16[8,8,4,1]{3,0,2,1:T(8,128)(2,1)S(1)}, u32[]{:S(2)}, u32[]{:S(2)}) collective-permute-start(bf16[8,8,4,1]{3,0,2,1:T(8,128)(2,1)S(1)} %get-tuple-element.398), channel_id=1, source_target_pairs={{2,0},{4,2},{6,4},{8,6},{10,8},{12,10},{14,12},{16,14},{18,16},{20... | collective-permute-start | bytes 1544 | tf_op jit(solution)/shard_map/ppermute | solution.py:22
  216.6 5.2 %collective-permute-start.22 = (bf16[8,8,4,1]{3,0,2,1:T(8,128)(2,1)S(1)}, bf16[8,8,4,1]{3,0,2,1:T(8,128)(2,1)S(1)}, u32[]{:S(2)}, u32[]{:S(2)}) collective-permute-start(bf16[8,8,4,1]{3,0,2,1:T(8,128)(2,1)S(1)} %get-tuple-element.394), channel_id=1, source_target_pairs={{2,0},{4,2},{6,4},{8,6},{10,8},{12,10},{14,12},{16,14},{18,16},{20... | collective-permute-start | bytes 1544 | tf_op jit(solution)/shard_map/ppermute | solution.py:22
  223.9 5.2 %collective-permute-start.30 = (bf16[8,8,4,1]{3,0,2,1:T(8,128)(2,1)S(1)}, bf16[8,8,4,1]{3,0,2,1:T(8,128)(2,1)S(1)}, u32[]{:S(2)}, u32[]{:S(2)}) collective-permute-start(bf16[8,8,4,1]{3,0,2,1:T(8,128)(2,1)S(1)} %get-tuple-element.390), channel_id=1, source_target_pairs={{2,0},{4,2},{6,4},{8,6},{10,8},{12,10},{14,12},{16,14},{18,16},{20... | collective-permute-start | bytes 1544 | tf_op jit(solution)/shard_map/ppermute | solution.py:22
  231.1 5.2 %collective-permute-start.6 = (bf16[8,8,4,1]{3,0,2,1:T(8,128)(2,1)S(1)}, bf16[8,8,4,1]{3,0,2,1:T(8,128)(2,1)S(1)}, u32[]{:S(2)}, u32[]{:S(2)}) collective-permute-start(bf16[8,8,4,1]{3,0,2,1:T(8,128)(2,1)S(1)} %get-tuple-element.402), channel_id=1, source_target_pairs={{2,0},{4,2},{6,4},{8,6},{10,8},{12,10},{14,12},{16,14},{18,16},{20... | collective-permute-start | bytes 1544 | tf_op jit(solution)/shard_map/ppermute | solution.py:22
  237.7 3.5 %collective-permute-start.16 = (bf16[8,1,4,258]{3,0,2,1:T(8,128)(2,1)S(1)}, bf16[8,1,4,258]{3,0,2,1:T(8,128)(2,1)S(1)}, u32[]{:S(2)}, u32[]{:S(2)}) collective-permute-start(bf16[8,1,4,258]{3,0,2,1:T(8,128)(2,1)S(1)} %get-tuple-element.382), channel_id=1, source_target_pairs={{1,0},{3,2},{5,4},{7,6},{9,8},{11,10},{13,12},{15,14},{17,16},{19,... | collective-permute-start | bytes 49544 | tf_op jit(solution)/shard_map/ppermute | solution.py:22
  242.6 3.0 collective-permute-start.24
  247.2 3.0 collective-permute-start.32
  252.6 4.7 %copy.109 = bf16[8,10,6,1,8,33]{0,4,5,2,1,3:T(8,128)(2,1)} copy(bf16[8,10,6,1,8,33]{5,4,0,2,1,3:T(8,128)(2,1)S(1)} %reshape.118) | data formatting | bytes 506880 | tf_op jit(solution)/shard_map/conv_general_dilated | solution.py:36
  258.3 9.8 %broadcast_select_fusion.4 = f32[8,4,8,33,8]{4,2,3,1,0:T(8,128)} fusion(pred[8,33]{0,1:T(8,128)(4,1)S(1)} %copy-done.11, bf16[8,8,3,3,3]{1,0,4,3,2:T(8,128)(2,1)S(1)} %copy-done.10, bf16[8,10,6,1,7,2]{0,4,5,2,1,3:T(8,128)(2,1)S(1)} %slice.197, bf16[8,10,6,1,8,33]{0,4,5,2,1,3:T(8,128)(2,1)} %copy.109), kind=kOutput, calls=%fused_computation.73 | convolution fusion | flops 30070272 | bytes 540936 | tf_op jit(solution)/shard_map/conv_general_dilated | solution.py:36
  268.1 3.5 %copy.110 = f32[8,4,8,33,8]{3,2,4,1,0:T(8,128)S(1)} copy(f32[8,4,8,33,8]{4,2,3,1,0:T(8,128)} %broadcast_select_fusion.4) | data formatting | bytes 540672 | tf_op jit(solution)/shard_map/conv_general_dilated | solution.py:36
  271.9 3.0 collective-permute-start.8
  275.9 4.9 %copy.118 = bf16[8,10,6,1,8,33]{0,4,5,2,1,3:T(8,128)(2,1)} copy(bf16[8,10,6,1,8,33]{5,4,0,2,1,3:T(8,128)(2,1)S(1)} %reshape.132) | data formatting | bytes 506880 | tf_op jit(solution)/shard_map/conv_general_dilated | solution.py:36
  281.9 9.8 %broadcast_select_fusion.2 = f32[8,4,8,33,8]{4,2,3,1,0:T(8,128)} fusion(pred[8,33]{0,1:T(8,128)(4,1)S(1)} %copy-done.11, bf16[8,8,3,3,3]{1,0,4,3,2:T(8,128)(2,1)S(1)} %copy-done.10, bf16[8,10,6,1,7,2]{0,4,5,2,1,3:T(8,128)(2,1)S(1)} %slice.206, bf16[8,10,6,1,8,33]{0,4,5,2,1,3:T(8,128)(2,1)} %copy.118), kind=kOutput, calls=%fused_computation.71 | convolution fusion | flops 30070272 | bytes 540936 | tf_op jit(solution)/shard_map/conv_general_dilated | solution.py:36
  291.6 3.5 %copy.119 = f32[8,4,8,33,8]{3,2,4,1,0:T(8,128)S(1)} copy(f32[8,4,8,33,8]{4,2,3,1,0:T(8,128)} %broadcast_select_fusion.2) | data formatting | bytes 540672 | tf_op jit(solution)/shard_map/conv_general_dilated | solution.py:36
  297.0 4.7 %copy.127 = bf16[8,10,6,1,8,33]{0,4,5,2,1,3:T(8,128)(2,1)} copy(bf16[8,10,6,1,8,33]{5,4,0,2,1,3:T(8,128)(2,1)S(1)} %reshape.146) | data formatting | bytes 506880 | tf_op jit(solution)/shard_map/conv_general_dilated | solution.py:36
  302.6 9.8 %broadcast_select_fusion = f32[8,4,8,33,8]{4,2,3,1,0:T(8,128)} fusion(pred[8,33]{0,1:T(8,128)(4,1)S(1)} %copy-done.11, bf16[8,8,3,3,3]{1,0,4,3,2:T(8,128)(2,1)S(1)} %copy-done.10, bf16[8,10,6,1,7,2]{0,4,5,2,1,3:T(8,128)(2,1)S(1)} %slice.215, bf16[8,10,6,1,8,33]{0,4,5,2,1,3:T(8,128)(2,1)} %copy.127), kind=kOutput, calls=%fused_computation.69 | convolution fusion | flops 30070272 | bytes 540936 | tf_op jit(solution)/shard_map/conv_general_dilated | solution.py:36
  312.4 3.5 %copy.128 = f32[8,4,8,33,8]{3,2,4,1,0:T(8,128)S(1)} copy(f32[8,4,8,33,8]{4,2,3,1,0:T(8,128)} %broadcast_select_fusion) | data formatting | bytes 540672 | tf_op jit(solution)/shard_map/conv_general_dilated | solution.py:36
  317.5 4.7 %copy.100 = bf16[8,10,6,1,8,33]{0,4,5,2,1,3:T(8,128)(2,1)} copy(bf16[8,10,6,1,8,33]{5,4,0,2,1,3:T(8,128)(2,1)S(1)} %reshape.104) | data formatting | bytes 506880 | tf_op jit(solution)/shard_map/conv_general_dilated | solution.py:36
  323.2 10.1 %broadcast_select_fusion.6 = f32[8,4,8,33,8]{4,2,3,1,0:T(8,128)} fusion(pred[8,33]{0,1:T(8,128)(4,1)S(1)} %copy-done.11, bf16[8,8,3,3,3]{1,0,4,3,2:T(8,128)(2,1)S(1)} %copy-done.10, bf16[8,10,6,1,7,2]{0,4,5,2,1,3:T(8,128)(2,1)S(1)} %slice.188, bf16[8,10,6,1,8,33]{0,4,5,2,1,3:T(8,128)(2,1)} %copy.100), kind=kOutput, calls=%fused_computation.75 | convolution fusion | flops 30070272 | bytes 540936 | tf_op jit(solution)/shard_map/conv_general_dilated | solution.py:36
  333.2 3.5 %copy.101 = f32[8,4,8,33,8]{3,2,4,1,0:T(8,128)S(1)} copy(f32[8,4,8,33,8]{4,2,3,1,0:T(8,128)} %broadcast_select_fusion.6) | data formatting | bytes 540672 | tf_op jit(solution)/shard_map/conv_general_dilated | solution.py:36
  (240 shorter events, 76.2 us)
Async XLA Ops:
  0.0 138.6 %copy-start = (bf16[8,8,3,3,3]{1,0,4,3,2:T(8,128)(2,1)S(1)}, bf16[8,8,3,3,3]{1,0,4,3,2:T(8,128)(2,1)}, u32[]{:S(2)}) copy-start(bf16[8,8,3,3,3]{1,0,4,3,2:T(8,128)(2,1)} %param.19) | copy-start | bytes 10372
  2.8 8.4 %collective-permute-start = (bf16[4,32,4,128]{3,2,1,0:T(4,128)(2,1)S(1)}, bf16[4,32,4,128]{3,2,1,0:T(4,128)(2,1)S(1)}, u32[]{:S(2)}, u32[]{:S(2)}) collective-permute-start(bf16[4,32,4,128]{3,2,1,0:T(4,128)(2,1)S(1)} %slice.180), channel_id=1, source_target_pairs={{0,2},{2,4},{4,6},{6,8},{8,10},{10,12},{12,14},{14,16},{16,18},{18... | collective-permute-start | bytes 393224 | tf_op jit(solution)/shard_map/ppermute | solution.py:32
  28.1 93.0 %copy-start.3 = (bf16[8,8,4,256]{3,2,0,1:T(4,128)(2,1)}, bf16[8,8,4,256]{3,2,0,1:T(4,128)(2,1)S(1)}, u32[]{:S(2)}) copy-start(bf16[8,8,4,256]{3,2,0,1:T(4,128)(2,1)S(1)} %get-tuple-element.265) | copy-start | bytes 393220
  28.3 64.8 %collective-permute-start.1 = (bf16[8,8,4,1]{3,2,1,0:T(4,128)(2,1)S(1)}, bf16[8,8,4,1]{3,2,1,0:T(4,128)(2,1)S(1)}, u32[]{:S(2)}, u32[]{:S(2)}) collective-permute-start(bf16[8,8,4,1]{3,2,1,0:T(4,128)(2,1)S(1)} %get-tuple-element.403), channel_id=1, source_target_pairs={{0,2},{2,4},{4,6},{6,8},{8,10},{10,12},{12,14},{14,16},{16,18},{18... | collective-permute-start | bytes 1544 | tf_op jit(solution)/shard_map/ppermute | solution.py:20
  30.2 66.2 %collective-permute-start.2 = (bf16[8,8,4,1]{3,2,1,0:T(4,128)(2,1)S(1)}, bf16[8,8,4,1]{3,2,1,0:T(4,128)(2,1)S(1)}, u32[]{:S(2)}, u32[]{:S(2)}) collective-permute-start(bf16[8,8,4,1]{3,2,1,0:T(4,128)(2,1)S(1)} %get-tuple-element.404), channel_id=1, source_target_pairs={{2,0},{4,2},{6,4},{8,6},{10,8},{12,10},{14,12},{16,14},{18,16},{20... | collective-permute-start | bytes 1544 | tf_op jit(solution)/shard_map/ppermute | solution.py:22
  51.9 79.5 %copy-start.5 = (bf16[8,8,4,256]{3,2,0,1:T(4,128)(2,1)}, bf16[8,8,4,256]{3,2,0,1:T(4,128)(2,1)S(1)}, u32[]{:S(2)}) copy-start(bf16[8,8,4,256]{3,2,0,1:T(4,128)(2,1)S(1)} %get-tuple-element.267) | copy-start | bytes 393220
  52.1 46.4 %collective-permute-start.17 = (bf16[8,8,4,1]{3,2,1,0:T(4,128)(2,1)S(1)}, bf16[8,8,4,1]{3,2,1,0:T(4,128)(2,1)S(1)}, u32[]{:S(2)}, u32[]{:S(2)}) collective-permute-start(bf16[8,8,4,1]{3,2,1,0:T(4,128)(2,1)S(1)} %get-tuple-element.395), channel_id=1, source_target_pairs={{0,2},{2,4},{4,6},{6,8},{8,10},{10,12},{12,14},{14,16},{16,18},{18... | collective-permute-start | bytes 1544 | tf_op jit(solution)/shard_map/ppermute | solution.py:20
  54.0 49.7 %collective-permute-start.18 = (bf16[8,8,4,1]{3,2,1,0:T(4,128)(2,1)S(1)}, bf16[8,8,4,1]{3,2,1,0:T(4,128)(2,1)S(1)}, u32[]{:S(2)}, u32[]{:S(2)}) collective-permute-start(bf16[8,8,4,1]{3,2,1,0:T(4,128)(2,1)S(1)} %get-tuple-element.396), channel_id=1, source_target_pairs={{2,0},{4,2},{6,4},{8,6},{10,8},{12,10},{14,12},{16,14},{18,16},{20... | collective-permute-start | bytes 1544 | tf_op jit(solution)/shard_map/ppermute | solution.py:22
  74.3 30.8 %collective-permute-start.10 = (bf16[8,8,4,1]{3,2,1,0:T(4,128)(2,1)S(1)}, bf16[8,8,4,1]{3,2,1,0:T(4,128)(2,1)S(1)}, u32[]{:S(2)}, u32[]{:S(2)}) collective-permute-start(bf16[8,8,4,1]{3,2,1,0:T(4,128)(2,1)S(1)} %get-tuple-element.400), channel_id=1, source_target_pairs={{2,0},{4,2},{6,4},{8,6},{10,8},{12,10},{14,12},{16,14},{18,16},{20... | collective-permute-start | bytes 1544 | tf_op jit(solution)/shard_map/ppermute | solution.py:22
  93.1 17.4 %collective-permute-start.9 = (bf16[8,8,4,1]{3,2,1,0:T(4,128)(2,1)S(1)}, bf16[8,8,4,1]{3,2,1,0:T(4,128)(2,1)S(1)}, u32[]{:S(2)}, u32[]{:S(2)}) collective-permute-start(bf16[8,8,4,1]{3,2,1,0:T(4,128)(2,1)S(1)} %get-tuple-element.399), channel_id=1, source_target_pairs={{0,2},{2,4},{4,6},{6,8},{8,10},{10,12},{12,14},{14,16},{16,18},{18... | collective-permute-start | bytes 1544 | tf_op jit(solution)/shard_map/ppermute | solution.py:20
  96.4 15.4 %collective-permute-start.25 = (bf16[8,8,4,1]{3,2,1,0:T(4,128)(2,1)S(1)}, bf16[8,8,4,1]{3,2,1,0:T(4,128)(2,1)S(1)}, u32[]{:S(2)}, u32[]{:S(2)}) collective-permute-start(bf16[8,8,4,1]{3,2,1,0:T(4,128)(2,1)S(1)} %get-tuple-element.391), channel_id=1, source_target_pairs={{0,2},{2,4},{4,6},{6,8},{8,10},{10,12},{12,14},{14,16},{16,18},{18... | collective-permute-start | bytes 1544 | tf_op jit(solution)/shard_map/ppermute | solution.py:20
  98.5 16.4 %collective-permute-start.26 = (bf16[8,8,4,1]{3,2,1,0:T(4,128)(2,1)S(1)}, bf16[8,8,4,1]{3,2,1,0:T(4,128)(2,1)S(1)}, u32[]{:S(2)}, u32[]{:S(2)}) collective-permute-start(bf16[8,8,4,1]{3,2,1,0:T(4,128)(2,1)S(1)} %get-tuple-element.392), channel_id=1, source_target_pairs={{2,0},{4,2},{6,4},{8,6},{10,8},{12,10},{14,12},{16,14},{18,16},{20... | collective-permute-start | bytes 1544 | tf_op jit(solution)/shard_map/ppermute | solution.py:22
  103.7 12.6 %collective-permute-start.3 = (bf16[8,1,4,258]{3,2,1,0:T(4,128)(2,1)S(1)}, bf16[8,1,4,258]{3,2,1,0:T(4,128)(2,1)S(1)}, u32[]{:S(2)}, u32[]{:S(2)}) collective-permute-start(bf16[8,1,4,258]{3,2,1,0:T(4,128)(2,1)S(1)} %get-tuple-element.387), channel_id=1, source_target_pairs={{0,1},{2,3},{4,5},{6,7},{8,9},{10,11},{12,13},{14,15},{16,17},{18,... | collective-permute-start | bytes 49544 | tf_op jit(solution)/shard_map/ppermute | solution.py:20
  105.1 14.3 %collective-permute-start.4 = (bf16[8,1,4,258]{3,2,1,0:T(4,128)(2,1)S(1)}, bf16[8,1,4,258]{3,2,1,0:T(4,128)(2,1)S(1)}, u32[]{:S(2)}, u32[]{:S(2)}) collective-permute-start(bf16[8,1,4,258]{3,2,1,0:T(4,128)(2,1)S(1)} %get-tuple-element.388), channel_id=1, source_target_pairs={{1,0},{3,2},{5,4},{7,6},{9,8},{11,10},{13,12},{15,14},{17,16},{19,... | collective-permute-start | bytes 49544 | tf_op jit(solution)/shard_map/ppermute | solution.py:22
  110.4 17.4 %collective-permute-start.19 = (bf16[8,1,4,258]{3,2,1,0:T(4,128)(2,1)S(1)}, bf16[8,1,4,258]{3,2,1,0:T(4,128)(2,1)S(1)}, u32[]{:S(2)}, u32[]{:S(2)}) collective-permute-start(bf16[8,1,4,258]{3,2,1,0:T(4,128)(2,1)S(1)} %get-tuple-element.379), channel_id=1, source_target_pairs={{0,1},{2,3},{4,5},{6,7},{8,9},{10,11},{12,13},{14,15},{16,17},{18,... | collective-permute-start | bytes 49544 | tf_op jit(solution)/shard_map/ppermute | solution.py:20
  111.9 19.6 %collective-permute-start.20 = (bf16[8,1,4,258]{3,2,1,0:T(4,128)(2,1)S(1)}, bf16[8,1,4,258]{3,2,1,0:T(4,128)(2,1)S(1)}, u32[]{:S(2)}, u32[]{:S(2)}) collective-permute-start(bf16[8,1,4,258]{3,2,1,0:T(4,128)(2,1)S(1)} %get-tuple-element.380), channel_id=1, source_target_pairs={{1,0},{3,2},{5,4},{7,6},{9,8},{11,10},{13,12},{15,14},{17,16},{19,... | collective-permute-start | bytes 49544 | tf_op jit(solution)/shard_map/ppermute | solution.py:22
  114.9 41.1 %collective-permute-start.11 = (bf16[8,1,4,258]{3,2,1,0:T(4,128)(2,1)S(1)}, bf16[8,1,4,258]{3,2,1,0:T(4,128)(2,1)S(1)}, u32[]{:S(2)}, u32[]{:S(2)}) collective-permute-start(bf16[8,1,4,258]{3,2,1,0:T(4,128)(2,1)S(1)} %get-tuple-element.383), channel_id=1, source_target_pairs={{0,1},{2,3},{4,5},{6,7},{8,9},{10,11},{12,13},{14,15},{16,17},{18,... | collective-permute-start | bytes 49544 | tf_op jit(solution)/shard_map/ppermute | solution.py:20
  116.3 39.7 %collective-permute-start.12 = (bf16[8,1,4,258]{3,2,1,0:T(4,128)(2,1)S(1)}, bf16[8,1,4,258]{3,2,1,0:T(4,128)(2,1)S(1)}, u32[]{:S(2)}, u32[]{:S(2)}) collective-permute-start(bf16[8,1,4,258]{3,2,1,0:T(4,128)(2,1)S(1)} %get-tuple-element.384), channel_id=1, source_target_pairs={{1,0},{3,2},{5,4},{7,6},{9,8},{11,10},{13,12},{15,14},{17,16},{19,... | collective-permute-start | bytes 49544 | tf_op jit(solution)/shard_map/ppermute | solution.py:22
  119.4 65.1 %collective-permute-start.27 = (bf16[8,1,4,258]{3,2,1,0:T(4,128)(2,1)S(1)}, bf16[8,1,4,258]{3,2,1,0:T(4,128)(2,1)S(1)}, u32[]{:S(2)}, u32[]{:S(2)}) collective-permute-start(bf16[8,1,4,258]{3,2,1,0:T(4,128)(2,1)S(1)} %get-tuple-element.375), channel_id=1, source_target_pairs={{0,1},{2,3},{4,5},{6,7},{8,9},{10,11},{12,13},{14,15},{16,17},{18,... | collective-permute-start | bytes 49544 | tf_op jit(solution)/shard_map/ppermute | solution.py:20
  127.9 10.8 %copy-start.11 = (pred[8,33]{0,1:T(8,128)(4,1)S(1)}, pred[8,33]{0,1:T(8,128)(4,1)}, u32[]{:S(2)}) copy-start(pred[8,33]{0,1:T(8,128)(4,1)} %constant.226) | copy-start | bytes 796
  127.9 56.7 %collective-permute-start.28 = (bf16[8,1,4,258]{3,2,1,0:T(4,128)(2,1)S(1)}, bf16[8,1,4,258]{3,2,1,0:T(4,128)(2,1)S(1)}, u32[]{:S(2)}, u32[]{:S(2)}) collective-permute-start(bf16[8,1,4,258]{3,2,1,0:T(4,128)(2,1)S(1)} %get-tuple-element.376), channel_id=1, source_target_pairs={{1,0},{3,2},{5,4},{7,6},{9,8},{11,10},{13,12},{15,14},{17,16},{19,... | collective-permute-start | bytes 49544 | tf_op jit(solution)/shard_map/ppermute | solution.py:22
  138.6 9.9 %copy-start.2 = (bf16[8,10,6,1,8,33]{0,4,5,2,1,3:T(8,128)(2,1)S(1)}, bf16[8,10,6,1,8,33]{0,4,5,2,1,3:T(8,128)(2,1)}, u32[]{:S(2)}) copy-start(bf16[8,10,6,1,8,33]{0,4,5,2,1,3:T(8,128)(2,1)} %copy.115) | copy-start | bytes 760324
  201.5 4.8 %copy-start.9 = (f32[8]{0:T(128)S(1)}, f32[8]{0:T(128)}, u32[]{:S(2)}) copy-start(f32[8]{0:T(128)} %param.20) | copy-start | bytes 100
  207.5 16.4 %collective-permute-start.13 = (bf16[8,8,4,1]{3,0,2,1:T(8,128)(2,1)S(1)}, bf16[8,8,4,1]{3,0,2,1:T(8,128)(2,1)S(1)}, u32[]{:S(2)}, u32[]{:S(2)}) collective-permute-start(bf16[8,8,4,1]{3,0,2,1:T(8,128)(2,1)S(1)} %get-tuple-element.397), channel_id=1, source_target_pairs={{0,2},{2,4},{4,6},{6,8},{8,10},{10,12},{12,14},{14,16},{16,18},{18... | collective-permute-start | bytes 1544 | tf_op jit(solution)/shard_map/ppermute | solution.py:20
  209.4 19.7 %collective-permute-start.14 = (bf16[8,8,4,1]{3,0,2,1:T(8,128)(2,1)S(1)}, bf16[8,8,4,1]{3,0,2,1:T(8,128)(2,1)S(1)}, u32[]{:S(2)}, u32[]{:S(2)}) collective-permute-start(bf16[8,8,4,1]{3,0,2,1:T(8,128)(2,1)S(1)} %get-tuple-element.398), channel_id=1, source_target_pairs={{2,0},{4,2},{6,4},{8,6},{10,8},{12,10},{14,12},{16,14},{18,16},{20... | collective-permute-start | bytes 1544 | tf_op jit(solution)/shard_map/ppermute | solution.py:22
  214.7 16.4 %collective-permute-start.21 = (bf16[8,8,4,1]{3,0,2,1:T(8,128)(2,1)S(1)}, bf16[8,8,4,1]{3,0,2,1:T(8,128)(2,1)S(1)}, u32[]{:S(2)}, u32[]{:S(2)}) collective-permute-start(bf16[8,8,4,1]{3,0,2,1:T(8,128)(2,1)S(1)} %get-tuple-element.393), channel_id=1, source_target_pairs={{0,2},{2,4},{4,6},{6,8},{8,10},{10,12},{12,14},{14,16},{16,18},{18... | collective-permute-start | bytes 1544 | tf_op jit(solution)/shard_map/ppermute | solution.py:20
  216.6 19.7 %collective-permute-start.22 = (bf16[8,8,4,1]{3,0,2,1:T(8,128)(2,1)S(1)}, bf16[8,8,4,1]{3,0,2,1:T(8,128)(2,1)S(1)}, u32[]{:S(2)}, u32[]{:S(2)}) collective-permute-start(bf16[8,8,4,1]{3,0,2,1:T(8,128)(2,1)S(1)} %get-tuple-element.394), channel_id=1, source_target_pairs={{2,0},{4,2},{6,4},{8,6},{10,8},{12,10},{14,12},{16,14},{18,16},{20... | collective-permute-start | bytes 1544 | tf_op jit(solution)/shard_map/ppermute | solution.py:22
  221.9 15.8 %collective-permute-start.29 = (bf16[8,8,4,1]{3,0,2,1:T(8,128)(2,1)S(1)}, bf16[8,8,4,1]{3,0,2,1:T(8,128)(2,1)S(1)}, u32[]{:S(2)}, u32[]{:S(2)}) collective-permute-start(bf16[8,8,4,1]{3,0,2,1:T(8,128)(2,1)S(1)} %get-tuple-element.389), channel_id=1, source_target_pairs={{0,2},{2,4},{4,6},{6,8},{8,10},{10,12},{12,14},{14,16},{16,18},{18... | collective-permute-start | bytes 1544 | tf_op jit(solution)/shard_map/ppermute | solution.py:20
  223.9 17.3 %collective-permute-start.30 = (bf16[8,8,4,1]{3,0,2,1:T(8,128)(2,1)S(1)}, bf16[8,8,4,1]{3,0,2,1:T(8,128)(2,1)S(1)}, u32[]{:S(2)}, u32[]{:S(2)}) collective-permute-start(bf16[8,8,4,1]{3,0,2,1:T(8,128)(2,1)S(1)} %get-tuple-element.390), channel_id=1, source_target_pairs={{2,0},{4,2},{6,4},{8,6},{10,8},{12,10},{14,12},{16,14},{18,16},{20... | collective-permute-start | bytes 1544 | tf_op jit(solution)/shard_map/ppermute | solution.py:22
  229.1 13.6 %collective-permute-start.5 = (bf16[8,8,4,1]{3,0,2,1:T(8,128)(2,1)S(1)}, bf16[8,8,4,1]{3,0,2,1:T(8,128)(2,1)S(1)}, u32[]{:S(2)}, u32[]{:S(2)}) collective-permute-start(bf16[8,8,4,1]{3,0,2,1:T(8,128)(2,1)S(1)} %get-tuple-element.401), channel_id=1, source_target_pairs={{0,2},{2,4},{4,6},{6,8},{8,10},{10,12},{12,14},{14,16},{16,18},{18... | collective-permute-start | bytes 1544 | tf_op jit(solution)/shard_map/ppermute | solution.py:20
  231.1 14.6 %collective-permute-start.6 = (bf16[8,8,4,1]{3,0,2,1:T(8,128)(2,1)S(1)}, bf16[8,8,4,1]{3,0,2,1:T(8,128)(2,1)S(1)}, u32[]{:S(2)}, u32[]{:S(2)}) collective-permute-start(bf16[8,8,4,1]{3,0,2,1:T(8,128)(2,1)S(1)} %get-tuple-element.402), channel_id=1, source_target_pairs={{2,0},{4,2},{6,4},{8,6},{10,8},{12,10},{14,12},{16,14},{18,16},{20... | collective-permute-start | bytes 1544 | tf_op jit(solution)/shard_map/ppermute | solution.py:22
  236.3 10.9 %collective-permute-start.15 = (bf16[8,1,4,258]{3,0,2,1:T(8,128)(2,1)S(1)}, bf16[8,1,4,258]{3,0,2,1:T(8,128)(2,1)S(1)}, u32[]{:S(2)}, u32[]{:S(2)}) collective-permute-start(bf16[8,1,4,258]{3,0,2,1:T(8,128)(2,1)S(1)} %get-tuple-element.381), channel_id=1, source_target_pairs={{0,1},{2,3},{4,5},{6,7},{8,9},{10,11},{12,13},{14,15},{16,17},{18,... | collective-permute-start | bytes 49544 | tf_op jit(solution)/shard_map/ppermute | solution.py:20
  237.7 12.6 %collective-permute-start.16 = (bf16[8,1,4,258]{3,0,2,1:T(8,128)(2,1)S(1)}, bf16[8,1,4,258]{3,0,2,1:T(8,128)(2,1)S(1)}, u32[]{:S(2)}, u32[]{:S(2)}) collective-permute-start(bf16[8,1,4,258]{3,0,2,1:T(8,128)(2,1)S(1)} %get-tuple-element.382), channel_id=1, source_target_pairs={{1,0},{3,2},{5,4},{7,6},{9,8},{11,10},{13,12},{15,14},{17,16},{19,... | collective-permute-start | bytes 49544 | tf_op jit(solution)/shard_map/ppermute | solution.py:22
  241.2 30.6 %collective-permute-start.23 = (bf16[8,1,4,258]{3,0,2,1:T(8,128)(2,1)S(1)}, bf16[8,1,4,258]{3,0,2,1:T(8,128)(2,1)S(1)}, u32[]{:S(2)}, u32[]{:S(2)}) collective-permute-start(bf16[8,1,4,258]{3,0,2,1:T(8,128)(2,1)S(1)} %get-tuple-element.377), channel_id=1, source_target_pairs={{0,1},{2,3},{4,5},{6,7},{8,9},{10,11},{12,13},{14,15},{16,17},{18,... | collective-permute-start | bytes 49544 | tf_op jit(solution)/shard_map/ppermute | solution.py:20
  242.6 32.3 %collective-permute-start.24 = (bf16[8,1,4,258]{3,0,2,1:T(8,128)(2,1)S(1)}, bf16[8,1,4,258]{3,0,2,1:T(8,128)(2,1)S(1)}, u32[]{:S(2)}, u32[]{:S(2)}) collective-permute-start(bf16[8,1,4,258]{3,0,2,1:T(8,128)(2,1)S(1)} %get-tuple-element.378), channel_id=1, source_target_pairs={{1,0},{3,2},{5,4},{7,6},{9,8},{11,10},{13,12},{15,14},{17,16},{19,... | collective-permute-start | bytes 49544 | tf_op jit(solution)/shard_map/ppermute | solution.py:22
  245.7 12.6 %copy-start.10 = (bf16[8,8,3,3,3]{1,0,4,3,2:T(8,128)(2,1)S(1)}, bf16[8,8,3,3,3]{1,0,4,3,2:T(8,128)(2,1)}, u32[]{:S(2)}) copy-start(bf16[8,8,3,3,3]{1,0,4,3,2:T(8,128)(2,1)} %param.21) | copy-start | bytes 10372
  245.7 50.2 %collective-permute-start.31 = (bf16[8,1,4,258]{3,0,2,1:T(8,128)(2,1)S(1)}, bf16[8,1,4,258]{3,0,2,1:T(8,128)(2,1)S(1)}, u32[]{:S(2)}, u32[]{:S(2)}) collective-permute-start(bf16[8,1,4,258]{3,0,2,1:T(8,128)(2,1)S(1)} %get-tuple-element.373), channel_id=1, source_target_pairs={{0,1},{2,3},{4,5},{6,7},{8,9},{10,11},{12,13},{14,15},{16,17},{18,... | collective-permute-start | bytes 49544 | tf_op jit(solution)/shard_map/ppermute | solution.py:20
  247.2 48.7 %collective-permute-start.32 = (bf16[8,1,4,258]{3,0,2,1:T(8,128)(2,1)S(1)}, bf16[8,1,4,258]{3,0,2,1:T(8,128)(2,1)S(1)}, u32[]{:S(2)}, u32[]{:S(2)}) collective-permute-start(bf16[8,1,4,258]{3,0,2,1:T(8,128)(2,1)S(1)} %get-tuple-element.374), channel_id=1, source_target_pairs={{1,0},{3,2},{5,4},{7,6},{9,8},{11,10},{13,12},{15,14},{17,16},{19,... | collective-permute-start | bytes 49544 | tf_op jit(solution)/shard_map/ppermute | solution.py:22
  250.3 66.2 %collective-permute-start.7 = (bf16[8,1,4,258]{3,0,2,1:T(8,128)(2,1)S(1)}, bf16[8,1,4,258]{3,0,2,1:T(8,128)(2,1)S(1)}, u32[]{:S(2)}, u32[]{:S(2)}) collective-permute-start(bf16[8,1,4,258]{3,0,2,1:T(8,128)(2,1)S(1)} %get-tuple-element.385), channel_id=1, source_target_pairs={{0,1},{2,3},{4,5},{6,7},{8,9},{10,11},{12,13},{14,15},{16,17},{18,... | collective-permute-start | bytes 49544 | tf_op jit(solution)/shard_map/ppermute | solution.py:20
  271.9 44.6 %collective-permute-start.8 = (bf16[8,1,4,258]{3,0,2,1:T(8,128)(2,1)S(1)}, bf16[8,1,4,258]{3,0,2,1:T(8,128)(2,1)S(1)}, u32[]{:S(2)}, u32[]{:S(2)}) collective-permute-start(bf16[8,1,4,258]{3,0,2,1:T(8,128)(2,1)S(1)} %get-tuple-element.386), channel_id=1, source_target_pairs={{1,0},{3,2},{5,4},{7,6},{9,8},{11,10},{13,12},{15,14},{17,16},{19,... | collective-permute-start | bytes 49544 | tf_op jit(solution)/shard_map/ppermute | solution.py:22
  291.6 3.8 %copy-start.7 = (f32[8]{0:T(128)S(1)}, f32[8]{0:T(128)}, u32[]{:S(2)}) copy-start(f32[8]{0:T(128)} %param.22) | copy-start | bytes 100
  291.6 3.8 %copy-start.8 = (f32[8]{0:T(128)S(1)}, f32[8]{0:T(128)}, u32[]{:S(2)}) copy-start(f32[8]{0:T(128)} %param.23) | copy-start | bytes 100
  323.2 15.2 %copy-start.1 = (bf16[8,8,3,3,3]{1,0,4,3,2:T(8,128)(2,1)S(1)}, bf16[8,8,3,3,3]{1,0,4,3,2:T(8,128)(2,1)}, u32[]{:S(2)}) copy-start(bf16[8,8,3,3,3]{1,0,4,3,2:T(8,128)(2,1)} %param.19) | copy-start | bytes 10372
  333.2 4.2 %copy-start.4 = (bf16[8,8,4,256]{3,2,0,1:T(4,128)(2,1)S(1)}, bf16[8,8,4,256]{3,2,0,1:T(4,128)(2,1)}, u32[]{:S(2)}) copy-start(bf16[8,8,4,256]{3,2,0,1:T(4,128)(2,1)} %copy-done.3) | copy-start | bytes 393220
  333.2 4.2 %copy-start.6 = (bf16[8,8,4,256]{3,2,0,1:T(4,128)(2,1)S(1)}, bf16[8,8,4,256]{3,2,0,1:T(4,128)(2,1)}, u32[]{:S(2)}) copy-start(bf16[8,8,4,256]{3,2,0,1:T(4,128)(2,1)} %copy-done.5) | copy-start | bytes 393220
where the time goes:
time: 344 us; the launch traced here: 339 us
  local copies, waits for them, and re-layouts  106 us (31%)
  starting transfers between devices  96 us (28%)
  matrix products  77.5 us (23%)
  loops' own time  40.7 us (12%)
  other arithmetic  10.8 us (3%)
  waiting for transfers between devices  3.7 us (1%)
    conv_general_dilated x40, local copies, waits for them, and re-layouts, convolve_valid(): lax.conv_general_dilated(volume[None], kernel, (1, 1, 1), 'VALID', dimens...  83.6 us
    conv_general_dilated x8, matrix products, convolve_valid(): lax.conv_general_dilated(volume[None], kernel, (1, 1, 1), 'VALID', dimens...  76.6 us
    ppermute x16, starting transfers between devices, padded(): lax.ppermute(head, axis, [((i + 1) % count, i) for i in range(ends)])  65.6 us
    another operation x4, loops' own time, per_device(): lax.map(one_plane, shifts[view_idx])  40.7 us
    ppermute x16, starting transfers between devices, padded(): lax.ppermute(tail, axis, [(i, (i + 1) % count) for i in range(ends)])  27.3 us
    dynamic_slice x32, local copies, waits for them, and re-layouts, per_device(): lax.map(one_plane, shifts[view_idx])  19.5 us
  transfers between devices with their start and end apart: 33, of which 1 were waited for; matrix products, arithmetic and copies ran while one was open for 42% of the time, Pallas kernels for 0%

commit v1 on v0

v1 whole, which is shorter than its diff:
```python
import jax
import jax.numpy as jnp
from jax import lax
from jax.experimental import pallas as pl
from jax.experimental.pallas import tpu as pltpu
from jax.sharding import PartitionSpec as P

GROUPS = 8
MAX_SHIFT = 128
LEAD = MAX_SHIFT + 16
EDGE = 16
FAR = -3.0e38


def iota(shape, dim):
    return lax.broadcasted_iota(jnp.int32, shape, dim)


def dot(left, right):
    return jnp.dot(left, right, preferred_element_type=jnp.float32)


def dot_nt(left, right):
    return lax.dot_general(
        left, right, (((1,), (1,)), ((), ())), preferred_element_type=jnp.float32
    )


def pack_body(place, own_ref, other_ref, ref_ref, cols_ref, ref_cols_ref, packet_ref):
    views, half, rows, width = own_ref.shape
    lanes = 2 * half * rows
    inner = lanes // (GROUPS * rows)
    role, order = place[0], place[1]
    eye = (iota((width, width), 0) == iota((width, width), 1)).astype(jnp.bfloat16)
    to = iota((lanes, lanes), 0)
    k, g, h = to // (GROUPS * rows), (to // rows) % GROUPS, to % rows
    perm = ((g * inner + k) * rows + h == iota((lanes, lanes), 1)).astype(jnp.bfloat16)

    def turned(block):
        ordered = dot(perm, block).astype(jnp.bfloat16)
        return dot_nt(eye, ordered).astype(jnp.bfloat16)

    for v in range(views):
        own = own_ref[v].reshape(half * rows, width)
        other = other_ref[v].reshape(half * rows, width)
        low = jnp.where(order == 0, own, other)
        high = jnp.where(order == 0, other, own)
        cols_ref[v] = turned(jnp.concatenate([low, high], axis=0))
    ref_cols_ref[...] = turned(ref_ref[...].reshape(lanes, width))
    for v in range(views):
        start = pl.multiple_of(jnp.where(role == 0, width - LEAD, 0), 16)
        packet_ref[v * LEAD : (v + 1) * LEAD] = cols_ref[v, pl.ds(start, LEAD)]
    start = pl.multiple_of(jnp.where(role == 0, width - EDGE, 0), 16)
    packet_ref[views * LEAD :] = ref_cols_ref[pl.ds(start, EDGE)]


def lane_table(values_ref, rows, lane):
    which = (lane // rows) % GROUPS
    table = jnp.zeros(lane.shape, jnp.float32)
    for o in range(GROUPS):
        table = jnp.where(which == o, values_ref[o], table)
    return table


def build_band(taps_ref, which, band_ref, rows):
    block = GROUPS * rows
    spread = iota((3 * GROUPS, 128), 1) // rows == iota((3 * GROUPS, 128), 0)
    wide = dot(taps_ref[which], spread.astype(jnp.bfloat16)).astype(jnp.bfloat16)
    stretch = (iota((block, GROUPS), 0) // rows == iota((block, GROUPS), 1)).astype(jnp.bfloat16)
    lane = iota((block, 128), 1)
    gap = iota((block, 128), 0) % rows - lane % rows + 1
    depth, out_lanes = band_ref.shape[0] // 3, band_ref.shape[1]
    per_tile = 128 // block
    zero = jnp.zeros((block, 128), jnp.bfloat16)
    for e in range(3):
        base = jnp.zeros((block, 128), jnp.float32)
        for b in range(3):
            at = (b * 3 + e) * GROUPS
            base = jnp.where(gap == b, dot(stretch, wide[at : at + GROUPS]), base)
        for j in range(depth // block):
            offset = j - 2
            first, turn = offset // per_tile, offset % per_tile
            moved = pltpu.roll(base, turn * block, 1) if turn else base
            for t in range(out_lanes // 128):
                if t == first:
                    part = jnp.where(lane >= turn * block, moved, 0.0).astype(jnp.bfloat16)
                elif t == first + 1 and turn > per_tile - 3:
                    part = jnp.where(lane < turn * block, moved, 0.0).astype(jnp.bfloat16)
                else:
                    part = zero
                at = e * depth + j * block
                band_ref[at : at + block, t * 128 : (t + 1) * 128] = part


def main_body(
    place,
    shifts,
    before,
    after,
    bias_one,
    bias_two,
    view_head,
    cols_ref,
    ref_cols_ref,
    got_ref,
    swapped_ref,
    taps_ref,
    out_ref,
    src,
    ref_wide,
    match,
    first,
    band_one,
    band_two,
):
    views, width, lanes = cols_ref.shape
    groups, planes, rows, _ = out_ref.shape
    block = groups * rows
    span = (planes + 4) * block
    tall = match.shape[1] - 8
    order = place[1]
    is_first_tile, is_last_tile = place[2], place[3]
    is_first_plane, is_last_plane = place[4], place[5]

    build_band(taps_ref, 0, band_one, rows)
    build_band(taps_ref, 1, band_two, rows)

    row_which = (iota((block, 128), 0) // rows) % groups
    head = jnp.zeros((block, 128), jnp.float32)
    for o in range(groups):
        head = jnp.where(row_which == o, view_head[o], head)
    lane = iota((block, 128), 1)
    head = jnp.where(iota((block, 128), 0) % rows == lane % rows, head, 0.0)
    head_high = head.astype(jnp.bfloat16).astype(jnp.float32)
    head_low = head - head_high

    def diagonal(part):
        pieces = []
        for j in range(planes):
            row = []
            for t in range(planes * block // 128):
                here = lane // block + t * (128 // block) == j
                row.append(jnp.where(here, part, 0.0).astype(jnp.bfloat16))
            pieces.append(jnp.concatenate(row, axis=1))
        return jnp.concatenate(pieces, axis=0)

    high = diagonal(head_high)
    head_all = jnp.concatenate([high, high, diagonal(head_low)], axis=0)

    left = jnp.where(order == 0, got_ref[...], swapped_ref[...])
    right = jnp.where(order == 0, swapped_ref[...], got_ref[...])
    for v in range(views):
        src[v, 0:LEAD] = left[v * LEAD : (v + 1) * LEAD].astype(jnp.float32)
        src[v, LEAD : LEAD + width] = cols_ref[v].astype(jnp.float32)
        src[v, LEAD + width :] = right[v * LEAD : v * LEAD + EDGE].astype(jnp.float32)
    ref_wide[0:EDGE] = left[views * LEAD :].astype(jnp.float32)
    ref_wide[EDGE : EDGE + width] = ref_cols_ref[...].astype(jnp.float32)
    ref_wide[EDGE + width :] = right[views * LEAD : views * LEAD + EDGE].astype(jnp.float32)

    span_lane = iota((1, span), 1) // block
    outside = ((span_lane < 2) & (is_first_plane == 1)) | (
        (span_lane >= planes + 2) & (is_last_plane == 1)
    )
    scale = jnp.where(outside, 0.0, 1.0 / (lanes // block))
    base_one = lane_table(bias_one, rows, iota((1, span), 1))
    outside = ((span_lane == 0) & (is_first_plane == 1)) | (
        (span_lane == planes + 1) & (is_last_plane == 1)
    )
    base_one = jnp.where(outside, FAR, base_one)
    base_two = lane_table(bias_two, rows, iota((1, planes * block), 1))

    def shift_of(v, d):
        if d < 0:
            return before[v, planes + d]
        return shifts[v, d] if d < planes else after[v, d - planes]

    chunk = tall // 3
    quarter = iota((chunk, 128), 1) // block
    lower, middle, even = quarter < 2, (quarter == 1) | (quarter == 2), quarter % 2 == 0
    weighted = jnp.zeros((width, planes * block), jnp.float32)
    total = jnp.zeros((width, planes * block), jnp.float32)
    for v in range(views):
        for q in range(span // 128):
            for r in range(0, tall, chunk):
                here = ref_wide[EDGE - 2 + r : EDGE - 2 + r + chunk]

                def product(j):
                    start = LEAD - 2 + r - shift_of(v, q * 4 + j - 2)
                    return src[v, pl.ds(start, chunk)] * here

                a, c, b, d = (product(j) for j in range(4))
                x = jnp.where(lower, a, b) + pltpu.roll(jnp.where(lower, b, a), 64, 1)
                z = jnp.where(middle, c, d) + pltpu.roll(jnp.where(middle, d, c), 64, 1)
                y = jnp.where(even, x, z) + pltpu.roll(jnp.where(even, z, x), 96, 1)
                y = y * scale[:, q * 128 : (q + 1) * 128]
                match[v, r : r + chunk, q * 128 : (q + 1) * 128] = y.astype(jnp.bfloat16).astype(
                    jnp.float32
                )
        moved = [match[v, e : e + tall].astype(jnp.bfloat16) for e in range(3)]
        raw = dot(jnp.concatenate(moved, axis=1), band_one[...])
        wide_out = raw.shape[1]
        raw = jnp.maximum(raw + base_one[:, :wide_out], 0.0)
        first[v, 0:tall, 0:wide_out] = raw.astype(jnp.bfloat16).astype(jnp.float32)
        rest = span - wide_out
        raw = sum(
            dot(moved[e][:, wide_out:], band_one[e * span : e * span + rest, 0:rest])
            for e in range(3)
        )
        raw = jnp.maximum(raw + base_one[:, wide_out:], 0.0)
        first[v, 0:tall, wide_out:] = raw.astype(jnp.bfloat16).astype(jnp.float32)

        @pl.when(is_first_tile == 1)
        def _():
            first[v, 0:1] = jnp.zeros((1, span), jnp.float32)

        @pl.when(is_last_tile == 1)
        def _():
            first[v, width + 1 : width + 2] = jnp.zeros((1, span), jnp.float32)

        moved = [first[v, e : e + width].astype(jnp.bfloat16) for e in range(3)]
        second = dot(jnp.concatenate(moved, axis=1), band_two[...])
        second = jnp.maximum(second + base_two, 0.0)
        upper = second.astype(jnp.bfloat16)
        under = (second - upper.astype(jnp.float32)).astype(jnp.bfloat16)
        score = dot(jnp.concatenate([upper, under, upper], axis=1), head_all)
        weight = 1.0 / (1.0 + jnp.exp(-score))
        total = total + weight
        weighted = weighted + weight * match[v, 2 : 2 + width, 2 * block : (planes + 2) * block]
    joined = (weighted / total).astype(jnp.bfloat16)
    size = planes * block
    to = iota((size, size), 0)
    g, j, h = to // (planes * rows), (to // rows) % planes, to % rows
    perm = ((j * groups + g) * rows + h == iota((size, size), 1)).astype(jnp.bfloat16)
    turned = dot_nt(perm, joined).astype(jnp.bfloat16)
    out_ref[...] = turned.reshape(groups, planes, rows, width)


def whole(memory):
    return pl.BlockSpec(memory_space=memory)


def per_device(ref_feat, src_feat, shifts, conv_one, bias_one, conv_two, bias_two, view_head):
    views, _, rows, width = src_feat.shape
    planes = shifts.shape[1]
    lanes = ref_feat.shape[0] * rows
    tiles, sides = lax.axis_size("tile"), lax.axis_size("plane")
    tile, plane = lax.axis_index("tile"), lax.axis_index("plane")
    if sides == 2:
        swap = [(0, 1), (1, 0)]
        own, other, order = src_feat, lax.ppermute(src_feat, "plane", swap), plane
        before = after = lax.ppermute(shifts, "plane", swap)
    else:
        full = lax.all_gather(src_feat, "plane", axis=1, tiled=True)
        half = full.shape[1] // 2
        own, other, order = full[:, :half], full[:, half:], 0 * plane
        before = lax.ppermute(shifts, "plane", [(i, i + 1) for i in range(sides - 1)])
        after = lax.ppermute(shifts, "plane", [(i + 1, i) for i in range(sides - 1)])
    ends = [tile == 0, tile == tiles - 1, plane == 0, plane == sides - 1]
    place = jnp.stack([jnp.minimum(plane, 1), order] + [e.astype(jnp.int32) for e in ends])

    packet_rows = views * LEAD + EDGE
    bf16 = jnp.bfloat16
    vmem, smem = pltpu.VMEM, pltpu.SMEM
    cols, ref_cols, packet = pl.pallas_call(
        pack_body,
        out_shape=[
            jax.ShapeDtypeStruct((views, width, lanes), bf16),
            jax.ShapeDtypeStruct((width, lanes), bf16),
            jax.ShapeDtypeStruct((packet_rows, lanes), bf16),
        ],
        in_specs=[whole(smem)] + [whole(vmem)] * 3,
        out_specs=[whole(vmem)] * 3,
        name="pack_columns",
    )(place, own, other, ref_feat)

    pairs = [(sides * i, sides * (i + 1)) for i in range(tiles - 1)]
    pairs += [(sides * (i + 1) + 1, sides * i + 1) for i in range(tiles - 1)]
    got = lax.ppermute(packet, ("tile", "plane"), pairs)
    if sides == 2:
        swapped = lax.ppermute(got, "plane", [(0, 1), (1, 0)])
    else:
        both = lax.all_gather(got, "plane", axis=0)
        got, swapped = both[0], both[1]

    def taps(kernel):
        flipped = jnp.flip(kernel, axis=2)
        return jnp.transpose(flipped, (3, 4, 1, 2, 0)).reshape(9 * GROUPS, 3 * GROUPS)

    both_taps = jnp.stack([taps(conv_one), taps(conv_two)])
    span = (planes + 4) * GROUPS * rows
    out_lanes = planes * GROUPS * rows
    tall = width + 8
    return pl.pallas_call(
        main_body,
        out_shape=jax.ShapeDtypeStruct((GROUPS, planes, rows, width), bf16),
        in_specs=[whole(smem)] * 7 + [whole(vmem)] * 5,
        out_specs=whole(vmem),
        scratch_shapes=[
            pltpu.VMEM((views, LEAD + width + EDGE, lanes), jnp.float32),
            pltpu.VMEM((EDGE + width + EDGE, lanes), jnp.float32),
            pltpu.VMEM((views, tall + 8, span), jnp.float32),
            pltpu.VMEM((views, tall + 8, span), jnp.float32),
            pltpu.VMEM((3 * span, out_lanes), bf16),
            pltpu.VMEM((3 * span, out_lanes), bf16),
        ],
        compiler_params=pltpu.CompilerParams(vmem_limit_bytes=48 * 1024 * 1024),
        name="cost_volume",
    )(
        place,
        shifts,
        before,
        after,
        bias_one,
        bias_two,
        view_head,
        cols,
        ref_cols,
        got,
        swapped,
        both_taps,
    )


def solution(mesh):
    placed = (
        P(None, None, "tile"),
        P(None, "plane", None, "tile"),
        P(None, "plane"),
        P(),
        P(),
        P(),
        P(),
        P(),
    )
    return jax.shard_map(
        per_device,
        mesh=mesh,
        in_specs=placed,
        out_specs=P(None, "plane", None, "tile"),
        check_vma=False,
    )
```

time: 344 us -> 23.6 us (0.07); the launches traced: 339 us -> 23.3 us
  local copies, waits for them, and re-layouts: 106 us -> 2.34 us
  starting transfers between devices: 96 us -> 7.87 us
  matrix products: 77.5 us -> 0 us
  loops' own time: 40.7 us -> 0 us
  other arithmetic: 10.8 us -> 0.01 us
  Pallas kernels: 0 us -> 9.51 us
    ppermute x33 -> x4, starting transfers between devices: 96 us -> 7.87 us  [the longest x1 4.08 us: per_device(): got = lax.ppermute(packet, ('tile', 'plane'), pairs)]
    conv_general_dilated x40 -> x0, local copies, waits for them, and re-layouts: 83.6 us -> none  [convolve_valid(): lax.conv_general_dilated(volume[None], kernel, (1, 1, 1), 'VALID', dimens...]
    conv_general_dilated x8 -> x0, matrix products: 76.6 us -> none  [convolve_valid(): lax.conv_general_dilated(volume[None], kernel, (1, 1, 1), 'VALID', dimens...]
    another operation x4 -> x0, loops' own time: 40.7 us -> none  [per_device(): lax.map(one_plane, shifts[view_idx])]
    dynamic_slice x32 -> x0, local copies, waits for them, and re-layouts: 19.5 us -> none  [per_device(): lax.map(one_plane, shifts[view_idx])]
    pallas_call x0 -> x2, Pallas kernels: none -> 9.51 us  [the longest x1 6.98 us: per_device(): pl.pallas_call(main_body, out_shape=jax.ShapeDtypeStruct((GROUPS, planes,...]
    reduce_sum x32 -> x0, other arithmetic: 3.86 us -> none  [one_plane(): return jnp.mean(products, axis=1)]
  transfers between devices with their start and end apart: 33 -> 4, of which waited for: 1 -> 3; matrix products, arithmetic and copies ran while one was open for 42% -> 4% of each run, Pallas kernels for 0% -> 0%
where the time goes in v1:
time: 23.6 us; the launch traced here: 23.3 us
  Pallas kernels  9.51 us (40%)
  starting transfers between devices  7.87 us (33%)
  waiting for transfers between devices  3.5 us (15%)
  local copies, waits for them, and re-layouts  2.34 us (10%)
    pallas_call x1, Pallas kernels, per_device(): pl.pallas_call(main_body, out_shape=jax.ShapeDtypeStruct((GROUPS, planes,...  6.98 us
    ppermute x1, starting transfers between devices, per_device(): got = lax.ppermute(packet, ('tile', 'plane'), pairs)  4.08 us
    ppermute x1, starting transfers between devices, per_device(): swapped = lax.ppermute(got, 'plane', [(0, 1), (1, 0)])  3.04 us
    pallas_call x1, Pallas kernels, per_device(): pl.pallas_call(pack_body, out_shape=[jax.ShapeDtypeStruct((views, width,...  2.54 us
    ppermute x1, waiting for transfers between devices, per_device(): got = lax.ppermute(packet, ('tile', 'plane'), pairs)  2.36 us
    unnamed x20, local copies, waits for them, and re-layouts  1.35 us
    ppermute x1, starting transfers between devices, per_device(): own, other, order = (src_feat, lax.ppermute(src_feat, 'plane', swap), plane)  0.68 us
    another operation x1, local copies, waits for them, and re-layouts, per_device(): jnp.stack([jnp.minimum(plane, 1), order] + [e.astype(jnp.int32) for e in...  0.61 us
  transfers between devices with their start and end apart: 4, of which 3 were waited for; matrix products, arithmetic and copies ran while one was open for 4% of the time, Pallas kernels for 0%

profile of v1, /device:TPU:25, one launch (start us, length us, event | category | flops | bytes accessed | tf_op | source)
XLA Modules:
  0.0 23.3 jit_solution(1252435012123291800)
XLA Ops:
  0.0 0.7 %collective-permute-start.1 = (bf16[4,16,4,256]{3,2,1,0:T(4,128)(2,1)}, bf16[4,16,4,256]{3,2,1,0:T(4,128)(2,1)S(1)}, u32[]{:S(2)}, u32[]{:S(2)}) collective-permute-start(bf16[4,16,4,256]{3,2,1,0:T(4,128)(2,1)} %own_ref.1), channel_id=1, source_target_pairs={{0,1},{1,0},{2,3},{3,2},{4,5},{5,4},{6,7},{7,6},{8,9},{9,8},{10,11... | collective-permute-start | bytes 393224 | tf_op jit(solution)/shard_map/ppermute | solution.py:250
  0.7 0.6 %stack.46.place = s32[6]{0:T(128)} concatenate(s32[1]{0:T(128)} %bitcast, s32[1]{0:T(128)} %bitcast.1, s32[1]{0:T(128)} %bitcast.2, s32[1]{0:T(128)} %bitcast.3, s32[1]{0:T(128)} %bitcast.4, s32[1]{0:T(128)} %bitcast.5), dimensions={0} | concatenate | bytes 48 | tf_op jit(solution)/shard_map/stack | solution.py:259
  1.3 0.0 copy-start.3
  1.3 0.0 copy-start.8
  1.3 0.6 %collective-permute-done.1.other_ref = bf16[4,16,4,256]{3,2,1,0:T(4,128)(2,1)S(1)} collective-permute-done((bf16[4,16,4,256]{3,2,1,0:T(4,128)(2,1)}, bf16[4,16,4,256]{3,2,1,0:T(4,128)(2,1)S(1)}, u32[]{:S(2)}, u32[]{:S(2)}) %collective-permute-start.1) | collective-permute-done | bytes 131104 | tf_op jit(solution)/shard_map/ppermute | solution.py:250
  1.9 0.0 copy-start.7
  1.9 0.7 %copy-done.7 = bf16[4,16,4,256]{3,2,1,0:T(4,128)(2,1)} copy-done((bf16[4,16,4,256]{3,2,1,0:T(4,128)(2,1)}, bf16[4,16,4,256]{3,2,1,0:T(4,128)(2,1)S(1)}, u32[]{:S(2)}) %copy-start.7) | copy-done | bytes 131096
  2.5 2.5 %pack_columns.1 = (bf16[4,256,128]{2,1,0:T(8,128)(2,1)}, bf16[256,128]{1,0:T(8,128)(2,1)}, bf16[592,128]{1,0:T(8,128)(2,1)}) custom-call(s32[6]{0:T(128)} %stack.46.place, bf16[4,16,4,256]{3,2,1,0:T(4,128)(2,1)} %own_ref.1, bf16[4,16,4,256]{3,2,1,0:T(4,128)(2,1)} %copy-done.7, bf16[32,4,256]{2,1,0:T(4,128)(2,1)} %ref_ref.1), custom_call_target="tpu_custom_call" | custom-call | tf_op jit(solution)/shard_map/pack_columns/pallas_call | solution.py:264
  5.1 0.0 copy-start.9
  5.1 4.1 %collective-permute-start.2 = (bf16[592,128]{1,0:T(8,128)(2,1)}, bf16[592,128]{1,0:T(8,128)(2,1)S(1)}, u32[]{:S(2)}, u32[]{:S(2)}) collective-permute-start(bf16[592,128]{1,0:T(8,128)(2,1)} %get-tuple-element.10), channel_id=1, source_target_pairs={{0,2},{2,4},{4,6},{6,8},{8,10},{10,12},{12,14},{14,16},{16,18},{18... | collective-permute-start | bytes 454664 | tf_op jit(solution)/shard_map/ppermute | solution.py:278
  9.2 0.0 copy-done.3
  9.2 0.1 collective-permute-start
  9.2 0.0 copy-done.8
  9.3 2.4 %collective-permute-done.2.got_ref = bf16[592,128]{1,0:T(8,128)(2,1)S(1)} collective-permute-done((bf16[592,128]{1,0:T(8,128)(2,1)}, bf16[592,128]{1,0:T(8,128)(2,1)S(1)}, u32[]{:S(2)}, u32[]{:S(2)}) %collective-permute-start.2) | collective-permute-done | bytes 151584 | tf_op jit(solution)/shard_map/ppermute | solution.py:278
  11.6 3.0 %collective-permute-start.3 = (bf16[592,128]{1,0:T(8,128)(2,1)S(1)}, bf16[592,128]{1,0:T(8,128)(2,1)S(1)}, u32[]{:S(2)}, u32[]{:S(2)}) collective-permute-start(bf16[592,128]{1,0:T(8,128)(2,1)S(1)} %collective-permute-done.2.got_ref), channel_id=1, source_target_pairs={{0,1},{1,0},{2,3},{3,2},{4,5},{5,4},{6,7},{7,6},{8,9},{9,8},{10,11... | collective-permute-start | bytes 454664 | tf_op jit(solution)/shard_map/ppermute | solution.py:280
  14.7 0.0 copy-done.9
  14.7 0.0 copy-start
  14.7 0.1 stack_reshape.6
  14.9 0.0 copy-start.1
  14.9 0.1 stack_reshape.7
  15.0 0.0 copy-start.6
  15.0 0.1 copy.17.taps_ref
  15.1 0.0 collective-permute-done.before.after
  15.1 0.6 %collective-permute-done.3.swapped_ref = bf16[592,128]{1,0:T(8,128)(2,1)S(1)} collective-permute-done((bf16[592,128]{1,0:T(8,128)(2,1)S(1)}, bf16[592,128]{1,0:T(8,128)(2,1)S(1)}, u32[]{:S(2)}, u32[]{:S(2)}) %collective-permute-start.3) | collective-permute-done | bytes 151584 | tf_op jit(solution)/shard_map/ppermute | solution.py:280
  15.7 0.0 copy-start.2
  15.7 0.0 copy-start.4
  15.7 0.0 copy-start.5
  15.7 0.0 copy-done
  15.7 0.0 copy-done.1
  15.7 0.0 copy-done.6
  15.7 0.6 %copy-done.2 = s32[6]{0:T(128)S(1)} copy-done((s32[6]{0:T(128)S(1)}, s32[6]{0:T(128)}, u32[]{:S(2)}) %copy-start.2) | copy-done | bytes 48
  16.3 0.1 copy-done.4
  16.3 0.0 copy-done.5
  16.4 7.0 %cost_volume.1 = bf16[8,8,4,256]{3,2,1,0:T(4,128)(2,1)} custom-call(s32[6]{0:T(128)S(1)} %copy-done.2, s32[4,8]{1,0:T(4,128)S(1)} %copy-done.3, s32[4,8]{1,0:T(4,128)S(1)} %collective-permute-done.before.after, s32[4,8]{1,0:T(4,128)S(1)} %collective-permute-done.before.after, f32[8]{0:T(128)S(1)} %copy-done.4, f32[8]{0:T(128)S(1)} %copy-done.5, ...), custom_call_target="tpu_custom_call" | custom-call | tf_op jit(solution)/shard_map/cost_volume/pallas_call | solution.py:293
  (5 shorter events, 0.1 us)
Async XLA Ops:
  0.0 1.9 %collective-permute-start.1 = (bf16[4,16,4,256]{3,2,1,0:T(4,128)(2,1)}, bf16[4,16,4,256]{3,2,1,0:T(4,128)(2,1)S(1)}, u32[]{:S(2)}, u32[]{:S(2)}) collective-permute-start(bf16[4,16,4,256]{3,2,1,0:T(4,128)(2,1)} %own_ref.1), channel_id=1, source_target_pairs={{0,1},{1,0},{2,3},{3,2},{4,5},{5,4},{6,7},{7,6},{8,9},{9,8},{10,11... | collective-permute-start | bytes 393224 | tf_op jit(solution)/shard_map/ppermute | solution.py:250
  1.3 7.9 %copy-start.3 = (s32[4,8]{1,0:T(4,128)S(1)}, s32[4,8]{1,0:T(4,128)}, u32[]{:S(2)}) copy-start(s32[4,8]{1,0:T(4,128)} %shifts.1) | copy-start | bytes 388
  1.3 8.0 %copy-start.8 = (bf16[8,8,3,3,3]{1,0,4,3,2:T(8,128)(2,1)S(1)}, bf16[8,8,3,3,3]{1,0,4,3,2:T(8,128)(2,1)}, u32[]{:S(2)}) copy-start(bf16[8,8,3,3,3]{1,0,4,3,2:T(8,128)(2,1)} %param.11) | copy-start | bytes 10372
  1.9 0.7 %copy-start.7 = (bf16[4,16,4,256]{3,2,1,0:T(4,128)(2,1)}, bf16[4,16,4,256]{3,2,1,0:T(4,128)(2,1)S(1)}, u32[]{:S(2)}) copy-start(bf16[4,16,4,256]{3,2,1,0:T(4,128)(2,1)S(1)} %collective-permute-done.1.other_ref) | copy-start | bytes 393220
  5.1 9.6 %copy-start.9 = (bf16[8,8,3,3,3]{1,0,4,3,2:T(8,128)(2,1)S(1)}, bf16[8,8,3,3,3]{1,0,4,3,2:T(8,128)(2,1)}, u32[]{:S(2)}) copy-start(bf16[8,8,3,3,3]{1,0,4,3,2:T(8,128)(2,1)} %param.13) | copy-start | bytes 10372
  5.1 6.6 %collective-permute-start.2 = (bf16[592,128]{1,0:T(8,128)(2,1)}, bf16[592,128]{1,0:T(8,128)(2,1)S(1)}, u32[]{:S(2)}, u32[]{:S(2)}) collective-permute-start(bf16[592,128]{1,0:T(8,128)(2,1)} %get-tuple-element.10), channel_id=1, source_target_pairs={{0,2},{2,4},{4,6},{6,8},{8,10},{10,12},{12,14},{14,16},{16,18},{18... | collective-permute-start | bytes 454664 | tf_op jit(solution)/shard_map/ppermute | solution.py:278
  9.2 6.0 %collective-permute-start = (s32[4,8]{1,0:T(4,128)S(1)}, s32[4,8]{1,0:T(4,128)S(1)}, u32[]{:S(2)}, u32[]{:S(2)}) collective-permute-start(s32[4,8]{1,0:T(4,128)S(1)} %copy-done.3), channel_id=1, source_target_pairs={{0,1},{1,0},{2,3},{3,2},{4,5},{5,4},{6,7},{7,6},{8,9},{9,8},{10,11... | collective-permute-start | bytes 392 | tf_op jit(solution)/shard_map/ppermute | solution.py:251
  11.6 4.1 %collective-permute-start.3 = (bf16[592,128]{1,0:T(8,128)(2,1)S(1)}, bf16[592,128]{1,0:T(8,128)(2,1)S(1)}, u32[]{:S(2)}, u32[]{:S(2)}) collective-permute-start(bf16[592,128]{1,0:T(8,128)(2,1)S(1)} %collective-permute-done.2.got_ref), channel_id=1, source_target_pairs={{0,1},{1,0},{2,3},{3,2},{4,5},{5,4},{6,7},{7,6},{8,9},{9,8},{10,11... | collective-permute-start | bytes 454664 | tf_op jit(solution)/shard_map/ppermute | solution.py:280
  14.7 1.0 %copy-start = (bf16[4,256,128]{2,1,0:T(8,128)(2,1)S(1)}, bf16[4,256,128]{2,1,0:T(8,128)(2,1)}, u32[]{:S(2)}) copy-start(bf16[4,256,128]{2,1,0:T(8,128)(2,1)} %get-tuple-element.8.cols_ref) | copy-start | bytes 786436
  14.9 0.9 %copy-start.1 = (bf16[256,128]{1,0:T(8,128)(2,1)S(1)}, bf16[256,128]{1,0:T(8,128)(2,1)}, u32[]{:S(2)}) copy-start(bf16[256,128]{1,0:T(8,128)(2,1)} %get-tuple-element.9.ref_cols_ref) | copy-start | bytes 196612
  15.0 0.7 %copy-start.6 = (f32[8]{0:T(128)S(1)}, f32[8]{0:T(128)}, u32[]{:S(2)}) copy-start(f32[8]{0:T(128)} %view_head.1) | copy-start | bytes 100
  15.7 0.6 %copy-start.2 = (s32[6]{0:T(128)S(1)}, s32[6]{0:T(128)}, u32[]{:S(2)}) copy-start(s32[6]{0:T(128)} %stack.46.place) | copy-start | bytes 76
  15.7 0.7 %copy-start.4 = (f32[8]{0:T(128)S(1)}, f32[8]{0:T(128)}, u32[]{:S(2)}) copy-start(f32[8]{0:T(128)} %bias_one.1) | copy-start | bytes 100
  15.7 0.7 %copy-start.5 = (f32[8]{0:T(128)S(1)}, f32[8]{0:T(128)}, u32[]{:S(2)}) copy-start(f32[8]{0:T(128)} %bias_two.1) | copy-start | bytes 100

commit v2 on v1

v2 whole, which is shorter than its diff:
```python
import jax
import jax.numpy as jnp
from jax import lax
from jax.experimental import pallas as pl
from jax.experimental.pallas import tpu as pltpu
from jax.sharding import PartitionSpec as P

GROUPS = 8
MAX_SHIFT = 128
LEAD = MAX_SHIFT + 16
EDGE = 16
FAR = -3.0e38


def iota(shape, dim):
    return lax.broadcasted_iota(jnp.int32, shape, dim)


def dot(left, right):
    return jnp.dot(left, right, preferred_element_type=jnp.float32)


def dot_nt(left, right):
    return lax.dot_general(
        left, right, (((1,), (1,)), ((), ())), preferred_element_type=jnp.float32
    )


def turning(own_ref, other_ref, order, pick):
    _, half, rows, width = own_ref.shape
    lanes = 2 * half * rows
    inner = 2 * half // GROUPS
    to = iota((lanes, lanes), 1)
    k, g, h = to // (GROUPS * rows), (to // rows) % GROUPS, to % rows
    place = (g * inner + k - half * order + 2 * half) % (2 * half)
    perm = (place * rows + h == iota((lanes, lanes), 0)).astype(jnp.bfloat16)
    plain = ((g * inner + k) * rows + h == iota((lanes, lanes), 0)).astype(jnp.bfloat16)

    def turned(own, other=None):
        block = own if other is None else jnp.concatenate([own, other], axis=0)
        block = block.reshape(lanes, width)
        columns = dot_nt(pick, block).astype(jnp.bfloat16)
        return dot(columns, plain if other is None else perm).astype(jnp.bfloat16)

    return turned


def pack_body(own_ref, other_ref, ref_ref, packet_ref):
    views, _, _, width = own_ref.shape
    role, order, *_ = position()
    start = jnp.where(role == 0, width - LEAD, 0)
    pick = (iota((LEAD, width), 0) + start == iota((LEAD, width), 1)).astype(jnp.bfloat16)
    turned = turning(own_ref, other_ref, order, pick)
    for v in range(views):
        packet_ref[v * LEAD : (v + 1) * LEAD] = turned(own_ref[v], other_ref[v])
    start = jnp.where(role == 0, width - EDGE, 0)
    pick = (iota((EDGE, width), 0) + start == iota((EDGE, width), 1)).astype(jnp.bfloat16)
    turned = turning(own_ref, other_ref, order, pick)
    packet_ref[views * LEAD :] = turned(ref_ref[...])


def position():
    tile, plane = lax.axis_index("tile"), lax.axis_index("plane")
    tiles, sides = lax.axis_size("tile"), lax.axis_size("plane")
    order = plane if sides == 2 else 0 * plane
    role = jnp.minimum(plane, 1)
    return role, order, tile == 0, tile == tiles - 1, plane == 0, plane == sides - 1


def lane_table(values_ref, rows, lane):
    which = (lane // rows) % GROUPS
    table = jnp.zeros(lane.shape, jnp.float32)
    for o in range(GROUPS):
        table = jnp.where(which == o, values_ref[o], table)
    return table


def build_band(taps_ref, which, band_ref, rows):
    block = GROUPS * rows
    spread = iota((3 * GROUPS, 128), 1) // rows == iota((3 * GROUPS, 128), 0)
    wide = dot(taps_ref[which], spread.astype(jnp.bfloat16)).astype(jnp.bfloat16)
    stretch = (iota((block, GROUPS), 0) // rows == iota((block, GROUPS), 1)).astype(jnp.bfloat16)
    lane = iota((block, 128), 1)
    gap = iota((block, 128), 0) % rows - lane % rows + 1
    depth, out_lanes = band_ref.shape[0] // 3, band_ref.shape[1]
    per_tile = 128 // block
    zero = jnp.zeros((block, 128), jnp.bfloat16)
    for e in range(3):
        base = jnp.zeros((block, 128), jnp.float32)
        for b in range(3):
            at = (b * 3 + e) * GROUPS
            base = jnp.where(gap == b, dot(stretch, wide[at : at + GROUPS]), base)
        for j in range(depth // block):
            offset = j - 2
            first, turn = offset // per_tile, offset % per_tile
            moved = pltpu.roll(base, turn * block, 1) if turn else base
            for t in range(out_lanes // 128):
                if t == first:
                    part = jnp.where(lane >= turn * block, moved, 0.0).astype(jnp.bfloat16)
                elif t == first + 1 and turn > per_tile - 3:
                    part = jnp.where(lane < turn * block, moved, 0.0).astype(jnp.bfloat16)
                else:
                    part = zero
                at = e * depth + j * block
                band_ref[at : at + block, t * 128 : (t + 1) * 128] = part


def volume(sizes, shift_refs, bias_refs, view_head, taps_ref, src, wide, match, first, band_one, band_two, ends):
    planes, rows, inner = sizes
    block = GROUPS * rows
    span = (planes + 4) * block
    out_lanes = planes * block
    shifts, before, after = shift_refs
    bias_one, bias_two = bias_refs
    is_first_plane, is_last_plane = ends
    build_band(taps_ref, 0, band_one, rows)
    build_band(taps_ref, 1, band_two, rows)

    row, lane = iota((out_lanes, out_lanes), 0), iota((out_lanes, out_lanes), 1)
    same = (row // block == lane // block) & (row % rows == lane % rows)
    spread = same.astype(jnp.bfloat16)
    spread = jnp.concatenate([spread, spread], axis=0)

    span_lane = iota((1, span), 1) // block
    outside = ((span_lane < 2) & is_first_plane) | ((span_lane >= planes + 2) & is_last_plane)
    scale = jnp.where(outside, 0.0, 1.0 / inner)
    base_one = lane_table(bias_one, rows, iota((1, span), 1))
    outside = ((span_lane == 0) & is_first_plane) | ((span_lane == planes + 1) & is_last_plane)
    base_one = jnp.where(outside, FAR, base_one)
    base_two = lane_table(bias_two, rows, iota((1, out_lanes), 1))
    head = lane_table(view_head, rows, iota((1, out_lanes), 1))

    def shift_of(v, d):
        if d < 0:
            return before[v, planes + d]
        return shifts[v, d] if d < planes else after[v, d - planes]

    def fill(v, pieces):
        for at, src_at, wide_at, count in pieces:
            quarter = iota((count, 128), 1) // block
            lower, middle, even = quarter < 2, (quarter == 1) | (quarter == 2), quarter % 2 == 0
            here = wide[wide_at : wide_at + count]
            for q in range(span // 128):

                def product(j):
                    return src[v, pl.ds(src_at - shift_of(v, q * 4 + j - 2), count)] * here

                a, c, b, d = (product(j) for j in range(4))
                x = jnp.where(lower, a, b) + pltpu.roll(jnp.where(lower, b, a), 64, 1)
                z = jnp.where(middle, c, d) + pltpu.roll(jnp.where(middle, d, c), 64, 1)
                y = jnp.where(even, x, z) + pltpu.roll(jnp.where(even, z, x), 96, 1)
                y = y * scale[:, q * 128 : (q + 1) * 128]
                y = y.astype(jnp.bfloat16).astype(jnp.float32)
                match[v, at : at + count, q * 128 : (q + 1) * 128] = y

    def weigh(v, tall, out_rows, mend):
        moved = [match[v, e : e + tall].astype(jnp.bfloat16) for e in range(3)]
        raw = dot(jnp.concatenate(moved, axis=1), band_one[...])
        raw = jnp.maximum(raw + base_one[:, :out_lanes], 0.0)
        first[v, 0:tall, 0:out_lanes] = raw.astype(jnp.bfloat16).astype(jnp.float32)
        rest = span - out_lanes
        raw = sum(
            dot(moved[e][:, out_lanes:], band_one[e * span : e * span + rest, 0:rest])
            for e in range(3)
        )
        raw = jnp.maximum(raw + base_one[:, out_lanes:], 0.0)
        first[v, 0:tall, out_lanes:] = raw.astype(jnp.bfloat16).astype(jnp.float32)
        mend(v)
        moved = [first[v, e : e + out_rows].astype(jnp.bfloat16) for e in range(3)]
        second = dot(jnp.concatenate(moved, axis=1), band_two[...])
        second = jnp.maximum(second + base_two, 0.0) * head
        upper = second.astype(jnp.bfloat16)
        under = (second - upper.astype(jnp.float32)).astype(jnp.bfloat16)
        score = dot(jnp.concatenate([upper, under], axis=1), spread)
        weight = 1.0 / (1.0 + jnp.exp(-score))
        return weight, weight * match[v, 2 : 2 + out_rows, 2 * block : (planes + 2) * block]

    return fill, weigh


def inner_body(
    shifts,
    before,
    after,
    bias_one,
    bias_two,
    view_head,
    own_ref,
    other_ref,
    ref_ref,
    taps_ref,
    cols_ref,
    ref_cols_ref,
    late_ref,
    src,
    wide,
    match,
    first,
    band_one,
    band_two,
):
    views, half, rows, width = own_ref.shape
    planes = shifts.shape[1]
    _, order, _, _, *ends = position()
    pick = (iota((width, width), 0) == iota((width, width), 1)).astype(jnp.bfloat16)
    turned = turning(own_ref, other_ref, order, pick)
    lanes = 2 * half * rows
    none = jnp.zeros((8, lanes), jnp.float32)
    columns = turned(ref_ref[...])
    ref_cols_ref[...] = columns
    wide[0:width] = columns.astype(jnp.float32)
    wide[width:] = none
    for v in range(views):
        columns = turned(own_ref[v], other_ref[v])
        cols_ref[v] = columns
        src[v, 0:8] = none
        src[v, 8 : 8 + width] = columns.astype(jnp.float32)
        src[v, 8 + width :] = none
    sizes = (planes, rows, 2 * half // GROUPS)
    fill, weigh = volume(
        sizes,
        (shifts, before, after),
        (bias_one, bias_two),
        view_head,
        taps_ref,
        src,
        wide,
        match,
        first,
        band_one,
        band_two,
        ends,
    )
    out_rows = width - MAX_SHIFT
    tall = out_rows + 8
    base = MAX_SHIFT - 2
    total = weighted = 0.0
    for v in range(views):
        fill(v, [(r, 8 + base + r, base + r, min(48, tall - r)) for r in range(0, tall, 48)])
        weight, part = weigh(v, tall, out_rows, lambda v: None)
        total, weighted = total + weight, weighted + part
    late_ref[...] = (weighted / total).astype(jnp.bfloat16)


def outer_body(
    shifts,
    before,
    after,
    bias_one,
    bias_two,
    view_head,
    cols_ref,
    ref_cols_ref,
    late_ref,
    got_ref,
    swapped_ref,
    taps_ref,
    out_ref,
    src,
    wide,
    match,
    first,
    band_one,
    band_two,
    joined,
):
    views, width, lanes = cols_ref.shape
    groups, planes, rows, _ = out_ref.shape
    block = groups * rows
    _, order, is_first_tile, is_last_tile, *ends = position()

    left = jnp.where(order == 0, got_ref[...], swapped_ref[...])
    right = jnp.where(order == 0, swapped_ref[...], got_ref[...])
    for v in range(views):
        src[v, 0:LEAD] = left[v * LEAD : (v + 1) * LEAD].astype(jnp.float32)
        src[v, LEAD : LEAD + width] = cols_ref[v].astype(jnp.float32)
        src[v, LEAD + width :] = right[v * LEAD : v * LEAD + EDGE].astype(jnp.float32)
    wide[0:EDGE] = left[views * LEAD :].astype(jnp.float32)
    wide[EDGE : EDGE + width] = ref_cols_ref[...].astype(jnp.float32)
    wide[EDGE + width :] = right[views * LEAD : views * LEAD + EDGE].astype(jnp.float32)
    fill, weigh = volume(
        (planes, rows, lanes // block),
        (shifts, before, after),
        (bias_one, bias_two),
        view_head,
        taps_ref,
        src,
        wide,
        match,
        first,
        band_one,
        band_two,
        ends,
    )
    main = MAX_SHIFT + 8
    tall = main + 8
    pieces = [(r, LEAD - 2 + r, EDGE - 2 + r, min(48, main - r)) for r in range(0, main, 48)]
    pieces += [(main, LEAD + width - 4, EDGE + width - 4, 8)]
    none = jnp.zeros((1, match.shape[2]), jnp.float32)

    def mend(v):
        @pl.when(is_first_tile)
        def _():
            first[v, 0:1] = none

        @pl.when(is_last_tile)
        def _():
            first[v, main + 3 : main + 4] = none

    total = weighted = 0.0
    for v in range(views):
        fill(v, pieces)
        weight, part = weigh(v, tall, tall, mend)
        total, weighted = total + weight, weighted + part
    part = weighted / total
    joined[0:MAX_SHIFT] = part[0:MAX_SHIFT]
    joined[MAX_SHIFT:] = late_ref[...].astype(jnp.float32)
    joined[MAX_SHIFT : MAX_SHIFT + 2] = part[MAX_SHIFT : MAX_SHIFT + 2]
    joined[width - 2 :] = part[main : main + 2]
    size = planes * block
    to = iota((size, size), 0)
    g, j, h = to // (planes * rows), (to // rows) % planes, to % rows
    perm = ((j * groups + g) * rows + h == iota((size, size), 1)).astype(jnp.bfloat16)
    turned = dot_nt(perm, joined[...].astype(jnp.bfloat16)).astype(jnp.bfloat16)
    out_ref[...] = turned.reshape(groups, planes, rows, width)


def whole(memory):
    return pl.BlockSpec(memory_space=memory)


def swap_planes(value):
    return lax.ppermute(value, "plane", [(0, 1), (1, 0)])


def per_device(ref_feat, src_feat, shifts, conv_one, bias_one, conv_two, bias_two, view_head):
    views, _, rows, width = src_feat.shape
    planes = shifts.shape[1]
    lanes = ref_feat.shape[0] * rows
    tiles, sides = lax.axis_size("tile"), lax.axis_size("plane")
    if sides == 2:
        own, other = src_feat, swap_planes(src_feat)
        before = after = swap_planes(shifts)
    else:
        full = lax.all_gather(src_feat, "plane", axis=1, tiled=True)
        half = full.shape[1] // 2
        own, other = full[:, :half], full[:, half:]
        before = lax.ppermute(shifts, "plane", [(i, i + 1) for i in range(sides - 1)])
        after = lax.ppermute(shifts, "plane", [(i + 1, i) for i in range(sides - 1)])

    bf16, f32 = jnp.bfloat16, jnp.float32
    vmem, smem = pltpu.VMEM, pltpu.SMEM
    packet = pl.pallas_call(
        pack_body,
        out_shape=jax.ShapeDtypeStruct((views * LEAD + EDGE, lanes), bf16),
        in_specs=[whole(vmem)] * 3,
        out_specs=whole(vmem),
        compiler_params=pltpu.CompilerParams(vmem_limit_bytes=8 * 1024 * 1024),
        name="pack_edges",
    )(own, other, ref_feat)

    pairs = [(sides * i, sides * (i + 1)) for i in range(tiles - 1)]
    pairs += [(sides * (i + 1) + 1, sides * i + 1) for i in range(tiles - 1)]
    got = lax.ppermute(packet, ("tile", "plane"), pairs)
    if sides == 2:
        swapped = swap_planes(got)
    else:
        both = lax.all_gather(got, "plane", axis=0)
        got, swapped = both[0], both[1]

    def taps(kernel):
        flipped = jnp.flip(kernel, axis=2)
        return jnp.transpose(flipped, (3, 4, 1, 2, 0)).reshape(9 * GROUPS, 3 * GROUPS)

    both_taps = jnp.stack([taps(conv_one), taps(conv_two)])
    own, other, before, after, both_taps, packet = lax.optimization_barrier(
        (own, other, before, after, both_taps, packet)
    )
    del packet
    span = (planes + 4) * GROUPS * rows
    out_lanes = planes * GROUPS * rows
    late_rows = width - MAX_SHIFT
    scalars = (shifts, before, after, bias_one, bias_two, view_head)
    bands = [pltpu.VMEM((3 * span, out_lanes), bf16)] * 2
    params = pltpu.CompilerParams(vmem_limit_bytes=24 * 1024 * 1024)
    cols, ref_cols, late = pl.pallas_call(
        inner_body,
        out_shape=[
            jax.ShapeDtypeStruct((views, width, lanes), bf16),
            jax.ShapeDtypeStruct((width, lanes), bf16),
            jax.ShapeDtypeStruct((late_rows, out_lanes), bf16),
        ],
        in_specs=[whole(smem)] * 6 + [whole(vmem)] * 4,
        out_specs=[whole(vmem)] * 3,
        scratch_shapes=[
            pltpu.VMEM((views, width + 16, lanes), f32),
            pltpu.VMEM((width + 8, lanes), f32),
            pltpu.VMEM((views, late_rows + 16, span), f32),
            pltpu.VMEM((views, late_rows + 16, span), f32),
        ]
        + bands,
        compiler_params=params,
        cost_estimate=pl.CostEstimate(
            flops=5 * 10**9, bytes_accessed=10**6, transcendentals=10**5
        ),
        name="inner_columns",
    )(*scalars, own, other, ref_feat, both_taps)
    return pl.pallas_call(
        outer_body,
        out_shape=jax.ShapeDtypeStruct((GROUPS, planes, rows, width), bf16),
        in_specs=[whole(smem)] * 6 + [whole(vmem)] * 6,
        out_specs=whole(vmem),
        scratch_shapes=[
            pltpu.VMEM((views, LEAD + width + EDGE, lanes), f32),
            pltpu.VMEM((EDGE + width + EDGE, lanes), f32),
            pltpu.VMEM((views, MAX_SHIFT + 24, span), f32),
            pltpu.VMEM((views, MAX_SHIFT + 24, span), f32),
        ]
        + bands
        + [pltpu.VMEM((width, out_lanes), f32)],
        compiler_params=params,
        name="outer_columns",
    )(*scalars, cols, ref_cols, late, got, swapped, both_taps)


def solution(mesh):
    placed = (
        P(None, None, "tile"),
        P(None, "plane", None, "tile"),
        P(None, "plane"),
        P(),
        P(),
        P(),
        P(),
        P(),
    )
    return jax.shard_map(
        per_device,
        mesh=mesh,
        in_specs=placed,
        out_specs=P(None, "plane", None, "tile"),
        check_vma=False,
    )
```

time: 23.6 us -> 23 us (0.975)
  waiting for transfers between devices: 3.5 us -> 1.97 us
  Pallas kernels: 9.51 us -> 10.7 us
    pallas_call x2 -> x3, Pallas kernels: 9.51 us -> 10.7 us  [the longest x1 5.24 us: per_device(): pl.pallas_call(outer_body, out_shape=jax.ShapeDtypeStruct((GROUPS, planes...]
    ppermute x3, waiting for transfers between devices: 1.14 us -> 0.32 us  [swap_planes(): return lax.ppermute(value, 'plane', [(0, 1), (1, 0)])]
    transpose x4, local copies, waits for them, and re-layouts: 0.07 us -> 0.89 us  [taps(): jnp.transpose(flipped, (3, 4, 1, 2, 0)).reshape(9 * GROUPS, 3 * GROUPS)]
    ppermute x1, waiting for transfers between devices: 2.36 us -> 1.66 us  [per_device(): got = lax.ppermute(packet, ('tile', 'plane'), pairs)]
    another operation x1 -> x0, local copies, waits for them, and re-layouts: 0.61 us -> none  [per_device(): jnp.stack([jnp.minimum(plane, 1), order] + [e.astype(jnp.int32) for e in...]
    unnamed x20 -> x16, local copies, waits for them, and re-layouts: 1.35 us -> 0.94 us
  transfers between devices with their start and end apart: 4 -> 4, of which waited for: 3 -> 2; matrix products, arithmetic and copies ran while one was open for 4% -> 5% of each run, Pallas kernels for 0% -> 24%
where the time goes in v2:
time: 23 us; the launch traced here: 22.8 us
  Pallas kernels  10.7 us (47%)
  starting transfers between devices  7.81 us (34%)
  local copies, waits for them, and re-layouts  2.14 us (9%)
  waiting for transfers between devices  1.97 us (9%)
    pallas_call x1, Pallas kernels, per_device(): pl.pallas_call(outer_body, out_shape=jax.ShapeDtypeStruct((GROUPS, planes...  5.24 us
    pallas_call x1, Pallas kernels, per_device(): pl.pallas_call(inner_body, out_shape=[jax.ShapeDtypeStruct((views, width,...  4.95 us
    ppermute x1, starting transfers between devices, per_device(): got = lax.ppermute(packet, ('tile', 'plane'), pairs)  3.96 us
    ppermute x3, starting transfers between devices, swap_planes(): return lax.ppermute(value, 'plane', [(0, 1), (1, 0)])  3.85 us
    ppermute x1, waiting for transfers between devices, per_device(): got = lax.ppermute(packet, ('tile', 'plane'), pairs)  1.66 us
    unnamed x16, local copies, waits for them, and re-layouts  0.94 us
    transpose x4, local copies, waits for them, and re-layouts, taps(): jnp.transpose(flipped, (3, 4, 1, 2, 0)).reshape(9 * GROUPS, 3 * GROUPS)  0.89 us
    pallas_call x1, Pallas kernels, per_device(): pl.pallas_call(pack_body, out_shape=jax.ShapeDtypeStruct((views * LEAD +...  0.53 us
  transfers between devices with their start and end apart: 4, of which 2 were waited for; matrix products, arithmetic and copies ran while one was open for 5% of the time, Pallas kernels for 24%

profile of v2, /device:TPU:25, one launch (start us, length us, event | category | flops | bytes accessed | tf_op | source)
XLA Modules:
  0.0 22.8 jit_solution(4142870553573384275)
XLA Ops:
  0.0 0.0 copy-start.2
  0.0 0.7 %collective-permute-start = (bf16[4,16,4,256]{3,2,1,0:T(4,128)(2,1)}, bf16[4,16,4,256]{3,2,1,0:T(4,128)(2,1)S(1)}, u32[]{:S(2)}, u32[]{:S(2)}) collective-permute-start(bf16[4,16,4,256]{3,2,1,0:T(4,128)(2,1)} %own_ref.2), channel_id=1, source_target_pairs={{0,1},{1,0},{2,3},{3,2},{4,5},{5,4},{6,7},{7,6},{8,9},{9,8},{10,11... | collective-permute-start | bytes 393224 | tf_op jit(solution)/shard_map/ppermute | solution.py:333
  0.7 0.1 collective-permute-start.1
  0.7 0.8 %reverse_bitcast_fusion.1 = bf16[3,3,8,3,8]{2,4,1,0,3:T(8,128)(2,1)S(1)} fusion(bf16[8,8,3,3,3]{1,0,4,3,2:T(8,128)(2,1)} %param.11), kind=kLoop, calls=%fused_computation.1 | loop fusion | bytes 6912 | tf_op jit(solution)/shard_map/transpose | solution.py:373
  1.6 0.3 %collective-permute-done.other_ref = bf16[4,16,4,256]{3,2,1,0:T(4,128)(2,1)S(1)} collective-permute-done((bf16[4,16,4,256]{3,2,1,0:T(4,128)(2,1)}, bf16[4,16,4,256]{3,2,1,0:T(4,128)(2,1)S(1)}, u32[]{:S(2)}, u32[]{:S(2)}) %collective-permute-start) | collective-permute-done | bytes 131104 | tf_op jit(solution)/shard_map/ppermute | solution.py:333
  1.9 0.0 copy-done.2
  1.9 0.0 copy-start
  1.9 0.9 %copy-done = bf16[4,16,4,256]{3,2,1,0:T(4,128)(2,1)S(1)} copy-done((bf16[4,16,4,256]{3,2,1,0:T(4,128)(2,1)S(1)}, bf16[4,16,4,256]{3,2,1,0:T(4,128)(2,1)}, u32[]{:S(2)}) %copy-start) | copy-done | bytes 131096
  2.8 0.0 copy-start.7
  2.8 0.5 %pack_edges.1 = bf16[592,128]{1,0:T(8,128)(2,1)S(1)} custom-call(bf16[4,16,4,256]{3,2,1,0:T(4,128)(2,1)S(1)} %copy-done, bf16[4,16,4,256]{3,2,1,0:T(4,128)(2,1)S(1)} %collective-permute-done.other_ref, bf16[32,4,256]{2,1,0:T(4,128)(2,1)S(1)} %copy-done.2), custom_call_target="tpu_custom_call" | custom-call | tf_op jit(solution)/shard_map/pack_edges/pallas_call | solution.py:353
  3.3 4.0 %collective-permute-start.2 = (bf16[592,128]{1,0:T(8,128)(2,1)S(1)}, bf16[592,128]{1,0:T(8,128)(2,1)S(1)}, u32[]{:S(2)}, u32[]{:S(2)}) collective-permute-start(bf16[592,128]{1,0:T(8,128)(2,1)S(1)} %pack_edges.1), channel_id=1, source_target_pairs={{0,2},{2,4},{4,6},{6,8},{8,10},{10,12},{12,14},{14,16},{16,18},{18... | collective-permute-start | bytes 454664 | tf_op jit(solution)/shard_map/ppermute | solution.py:364
  7.3 0.0 copy-done.7
  7.4 0.1 stack_reshape.6
  7.5 0.0 copy-start.1
  7.5 0.1 stack_reshape.7
  7.6 0.0 copy-start.3
  7.6 0.0 copy-start.4
  7.7 0.0 copy-start.5
  7.7 0.0 copy-start.6
  7.7 0.0 collective-permute-done.1.before.after
  7.7 0.1 copy.17.taps_ref
  7.8 1.7 %collective-permute-done.2.got_ref = bf16[592,128]{1,0:T(8,128)(2,1)S(1)} collective-permute-done((bf16[592,128]{1,0:T(8,128)(2,1)S(1)}, bf16[592,128]{1,0:T(8,128)(2,1)S(1)}, u32[]{:S(2)}, u32[]{:S(2)}) %collective-permute-start.2) | collective-permute-done | bytes 151584 | tf_op jit(solution)/shard_map/ppermute | solution.py:364
  9.4 3.1 %collective-permute-start.3 = (bf16[592,128]{1,0:T(8,128)(2,1)S(1)}, bf16[592,128]{1,0:T(8,128)(2,1)S(1)}, u32[]{:S(2)}, u32[]{:S(2)}) collective-permute-start(bf16[592,128]{1,0:T(8,128)(2,1)S(1)} %collective-permute-done.2.got_ref), channel_id=1, source_target_pairs={{0,1},{1,0},{2,3},{3,2},{4,5},{5,4},{6,7},{7,6},{8,9},{9,8},{10,11... | collective-permute-start | bytes 454664 | tf_op jit(solution)/shard_map/ppermute | solution.py:333
  12.6 0.0 copy-done.1
  12.6 0.0 copy-done.3
  12.6 0.0 copy-done.4
  12.6 0.0 copy-done.5
  12.6 0.0 copy-done.6
  12.6 5.0 %inner_columns.1 = (bf16[4,256,128]{2,1,0:T(8,128)(2,1)S(1)}, bf16[256,128]{1,0:T(8,128)(2,1)S(1)}, bf16[128,256]{1,0:T(8,128)(2,1)S(1)}) custom-call(s32[4,8]{1,0:T(4,128)S(1)} %copy-done.3, s32[4,8]{1,0:T(4,128)S(1)} %collective-permute-done.1.before.after, s32[4,8]{1,0:T(4,128)S(1)} %collective-permute-done.1.before.after, f32[8]{0:T(128)S(1)} %copy-done.4, ...), custom_call_target="tpu_custom_call" | custom-call | flops 5000000000 | bytes 1000000 | tf_op jit(solution)/shard_map/inner_columns/pallas_call | solution.py:386
  17.5 0.0 collective-permute-done.3.swapped_ref
  17.6 5.2 %outer_columns.1 = bf16[8,8,4,256]{3,2,1,0:T(4,128)(2,1)} custom-call(s32[4,8]{1,0:T(4,128)S(1)} %copy-done.3, s32[4,8]{1,0:T(4,128)S(1)} %collective-permute-done.1.before.after, s32[4,8]{1,0:T(4,128)S(1)} %collective-permute-done.1.before.after, f32[8]{0:T(128)S(1)} %copy-done.4, f32[8]{0:T(128)S(1)} %copy-done.5, f32[8]{0:T(128)S(1)} %copy-done.6, ...), custom_call_target="tpu_custom_call" | custom-call | tf_op jit(solution)/shard_map/outer_columns/pallas_call | solution.py:408
  (4 shorter events, 0.1 us)
Async XLA Ops:
  0.0 1.9 %copy-start.2 = (bf16[32,4,256]{2,1,0:T(4,128)(2,1)S(1)}, bf16[32,4,256]{2,1,0:T(4,128)(2,1)}, u32[]{:S(2)}) copy-start(bf16[32,4,256]{2,1,0:T(4,128)(2,1)} %ref_ref.3) | copy-start | bytes 196612
  0.0 1.9 %collective-permute-start = (bf16[4,16,4,256]{3,2,1,0:T(4,128)(2,1)}, bf16[4,16,4,256]{3,2,1,0:T(4,128)(2,1)S(1)}, u32[]{:S(2)}, u32[]{:S(2)}) collective-permute-start(bf16[4,16,4,256]{3,2,1,0:T(4,128)(2,1)} %own_ref.2), channel_id=1, source_target_pairs={{0,1},{1,0},{2,3},{3,2},{4,5},{5,4},{6,7},{7,6},{8,9},{9,8},{10,11... | collective-permute-start | bytes 393224 | tf_op jit(solution)/shard_map/ppermute | solution.py:333
  0.7 7.0 %collective-permute-start.1 = (s32[4,8]{1,0:T(4,128)}, s32[4,8]{1,0:T(4,128)S(1)}, u32[]{:S(2)}, u32[]{:S(2)}) collective-permute-start(s32[4,8]{1,0:T(4,128)} %shifts.3), channel_id=1, source_target_pairs={{0,1},{1,0},{2,3},{3,2},{4,5},{5,4},{6,7},{7,6},{8,9},{9,8},{10,11... | collective-permute-start | bytes 392 | tf_op jit(solution)/shard_map/ppermute | solution.py:333
  1.9 0.9 %copy-start = (bf16[4,16,4,256]{3,2,1,0:T(4,128)(2,1)S(1)}, bf16[4,16,4,256]{3,2,1,0:T(4,128)(2,1)}, u32[]{:S(2)}) copy-start(bf16[4,16,4,256]{3,2,1,0:T(4,128)(2,1)} %own_ref.2) | copy-start | bytes 393220
  2.8 4.5 %copy-start.7 = (bf16[8,8,3,3,3]{1,0,4,3,2:T(8,128)(2,1)S(1)}, bf16[8,8,3,3,3]{1,0,4,3,2:T(8,128)(2,1)}, u32[]{:S(2)}) copy-start(bf16[8,8,3,3,3]{1,0,4,3,2:T(8,128)(2,1)} %param.13) | copy-start | bytes 10372
  3.3 6.1 %collective-permute-start.2 = (bf16[592,128]{1,0:T(8,128)(2,1)S(1)}, bf16[592,128]{1,0:T(8,128)(2,1)S(1)}, u32[]{:S(2)}, u32[]{:S(2)}) collective-permute-start(bf16[592,128]{1,0:T(8,128)(2,1)S(1)} %pack_edges.1), channel_id=1, source_target_pairs={{0,2},{2,4},{4,6},{6,8},{8,10},{10,12},{12,14},{14,16},{16,18},{18... | collective-permute-start | bytes 454664 | tf_op jit(solution)/shard_map/ppermute | solution.py:364
  7.5 5.1 %copy-start.1 = (bf16[4,16,4,256]{3,2,1,0:T(4,128)(2,1)S(1)}, bf16[4,16,4,256]{3,2,1,0:T(4,128)(2,1)}, u32[]{:S(2)}) copy-start(bf16[4,16,4,256]{3,2,1,0:T(4,128)(2,1)} %own_ref.2) | copy-start | bytes 393220
  7.6 4.9 %copy-start.3 = (s32[4,8]{1,0:T(4,128)S(1)}, s32[4,8]{1,0:T(4,128)}, u32[]{:S(2)}) copy-start(s32[4,8]{1,0:T(4,128)} %shifts.3) | copy-start | bytes 388
  7.6 4.9 %copy-start.4 = (f32[8]{0:T(128)S(1)}, f32[8]{0:T(128)}, u32[]{:S(2)}) copy-start(f32[8]{0:T(128)} %bias_one.3) | copy-start | bytes 100
  7.7 4.9 %copy-start.5 = (f32[8]{0:T(128)S(1)}, f32[8]{0:T(128)}, u32[]{:S(2)}) copy-start(f32[8]{0:T(128)} %bias_two.3) | copy-start | bytes 100
  7.7 4.9 %copy-start.6 = (f32[8]{0:T(128)S(1)}, f32[8]{0:T(128)}, u32[]{:S(2)}) copy-start(f32[8]{0:T(128)} %view_head.3) | copy-start | bytes 100
  9.4 8.1 %collective-permute-start.3 = (bf16[592,128]{1,0:T(8,128)(2,1)S(1)}, bf16[592,128]{1,0:T(8,128)(2,1)S(1)}, u32[]{:S(2)}, u32[]{:S(2)}) collective-permute-start(bf16[592,128]{1,0:T(8,128)(2,1)S(1)} %collective-permute-done.2.got_ref), channel_id=1, source_target_pairs={{0,1},{1,0},{2,3},{3,2},{4,5},{5,4},{6,7},{7,6},{8,9},{9,8},{10,11... | collective-permute-start | bytes 454664 | tf_op jit(solution)/shard_map/ppermute | solution.py:333

commit v3 on v2

v3 whole, which is shorter than its diff:
```python
import jax
import jax.numpy as jnp
from jax import lax
from jax.experimental import pallas as pl
from jax.experimental.pallas import tpu as pltpu
from jax.sharding import PartitionSpec as P

GROUPS = 8
MAX_SHIFT = 128
LEAD = MAX_SHIFT + 16
EDGE = 16
FAR = -3.0e38


def iota(shape, dim):
    return lax.broadcasted_iota(jnp.int32, shape, dim)


def dot(left, right):
    return jnp.dot(left, right, preferred_element_type=jnp.float32)


def dot_nt(left, right):
    return lax.dot_general(
        left, right, (((1,), (1,)), ((), ())), preferred_element_type=jnp.float32
    )


def position():
    tile, plane = lax.axis_index("tile"), lax.axis_index("plane")
    tiles, sides = lax.axis_size("tile"), lax.axis_size("plane")
    order = plane if sides == 2 else 0 * plane
    role = jnp.minimum(plane, 1)
    return role, order, tile == 0, tile == tiles - 1, plane == 0, plane == sides - 1


def columns_of(count, width, start):
    picked = iota((count, width), 0) + start == iota((count, width), 1)
    return picked.astype(jnp.bfloat16)


def lane_order(half, rows, side):
    lanes = 2 * half * rows
    inner = 2 * half // GROUPS
    at, to = iota((lanes, 2 * lanes), 0), iota((lanes, 2 * lanes), 1)
    k, g = (to // (GROUPS * rows)) % inner, (to // rows) % GROUPS
    channel = g * inner + k - half * side
    row = (to // lanes) * (half * rows) + channel * rows + to % rows
    held = (channel >= 0) & (channel < half) & (row == at)
    return held.astype(jnp.bfloat16)


def ref_order(lanes, rows):
    at, to = iota((lanes, lanes), 0), iota((lanes, lanes), 1)
    k, g, h = to // (GROUPS * rows), (to // rows) % GROUPS, to % rows
    return ((g * (lanes // (GROUPS * rows)) + k) * rows + h == at).astype(jnp.bfloat16)


def turned_half(half_ref, pick, side):
    views, half, rows, width = half_ref.shape
    lanes = 2 * half * rows
    block = half_ref[...].reshape(views * half * rows, width)
    columns = dot_nt(pick, block).astype(jnp.bfloat16)
    order = lane_order(half, rows, side)
    return [dot(columns[:, i : i + lanes], order) for i in range(0, columns.shape[1], lanes)]


def turned_ref(ref_ref, pick):
    channels, rows, width = ref_ref.shape
    lanes = channels * rows
    columns = dot_nt(pick, ref_ref[...].reshape(lanes, width)).astype(jnp.bfloat16)
    return dot(columns, ref_order(lanes, rows))


def edge_start(role, width, count):
    return jnp.where(role == 0, width - count, 0)


def store_pairs(target_ref, pairs):
    lanes = target_ref.shape[1]
    for i, pair in enumerate(pairs):
        for k in range(2):
            at = (2 * i + k) * LEAD
            part = pair[:, k * lanes : (k + 1) * lanes]
            target_ref[at : at + LEAD] = part.astype(jnp.bfloat16)


def pack_own_body(own_ref, ref_ref, part_ref):
    width = own_ref.shape[3]
    role, order, *_ = position()
    pick = columns_of(LEAD, width, edge_start(role, width, LEAD))
    store_pairs(part_ref, turned_half(own_ref, pick, order))
    pick = columns_of(EDGE, width, edge_start(role, width, EDGE))
    part_ref[own_ref.shape[0] * LEAD :] = turned_ref(ref_ref, pick).astype(jnp.bfloat16)


def pack_other_body(part_ref, other_ref, packet_ref):
    width = other_ref.shape[3]
    lanes = packet_ref.shape[1]
    role, order, *_ = position()
    pick = columns_of(LEAD, width, edge_start(role, width, LEAD))
    pairs = turned_half(other_ref, pick, 1 - order)
    for i, pair in enumerate(pairs):
        for k in range(2):
            at = (2 * i + k) * LEAD
            part = pair[:, k * lanes : (k + 1) * lanes]
            both = part_ref[at : at + LEAD].astype(jnp.float32) + part
            packet_ref[at : at + LEAD] = both.astype(jnp.bfloat16)
    at = other_ref.shape[0] * LEAD
    packet_ref[at:] = part_ref[at:]


def lane_table(values_ref, rows, lane):
    which = (lane // rows) % GROUPS
    table = jnp.zeros(lane.shape, jnp.float32)
    for o in range(GROUPS):
        table = jnp.where(which == o, values_ref[o], table)
    return table


def build_band(taps_ref, which, band_ref, rows):
    block = GROUPS * rows
    spread = iota((3 * GROUPS, 128), 1) // rows == iota((3 * GROUPS, 128), 0)
    wide = dot(taps_ref[which], spread.astype(jnp.bfloat16)).astype(jnp.bfloat16)
    stretch = (iota((block, GROUPS), 0) // rows == iota((block, GROUPS), 1)).astype(jnp.bfloat16)
    lane = iota((block, 128), 1)
    gap = iota((block, 128), 0) % rows - lane % rows + 1
    depth, out_lanes = band_ref.shape[0] // 3, band_ref.shape[1]
    per_tile = 128 // block
    zero = jnp.zeros((block, 128), jnp.bfloat16)
    for e in range(3):
        base = jnp.zeros((block, 128), jnp.float32)
        for b in range(3):
            at = (b * 3 + e) * GROUPS
            base = jnp.where(gap == b, dot(stretch, wide[at : at + GROUPS]), base)
        for j in range(depth // block):
            offset = j - 2
            first, turn = offset // per_tile, offset % per_tile
            moved = pltpu.roll(base, turn * block, 1) if turn else base
            for t in range(out_lanes // 128):
                if t == first:
                    part = jnp.where(lane >= turn * block, moved, 0.0).astype(jnp.bfloat16)
                elif t == first + 1 and turn > per_tile - 3:
                    part = jnp.where(lane < turn * block, moved, 0.0).astype(jnp.bfloat16)
                else:
                    part = zero
                at = e * depth + j * block
                band_ref[at : at + block, t * 128 : (t + 1) * 128] = part


def build_tables(planes, rows, inner, bias_one, bias_two, view_head, ends, table_ref, spread_ref):
    block = GROUPS * rows
    out_lanes = planes * block
    span = table_ref.shape[1]
    is_first_plane, is_last_plane = ends
    at = iota((1, span), 1)
    plane = at // block
    outside = ((plane < 2) & is_first_plane) | ((plane >= planes + 2) & is_last_plane)
    table_ref[0:1] = jnp.where(outside, 0.0, 1.0 / inner)
    outside = ((plane == 0) & is_first_plane) | ((plane == planes + 1) & is_last_plane)
    table_ref[1:2] = jnp.where(outside, FAR, lane_table(bias_one, rows, at))
    table_ref[2:3] = lane_table(bias_two, rows, at)
    table_ref[3:4] = lane_table(view_head, rows, at)
    row, lane = iota((out_lanes, out_lanes), 0), iota((out_lanes, out_lanes), 1)
    same = ((row // block == lane // block) & (row % rows == lane % rows)).astype(jnp.bfloat16)
    spread_ref[0:out_lanes] = same
    spread_ref[out_lanes:] = same


def fill(v, pieces, shift_of, src, wide, match, table_ref, block):
    for at, src_at, wide_at, count in pieces:
        quarter = iota((count, 128), 1) // block
        lower, middle, even = quarter < 2, (quarter == 1) | (quarter == 2), quarter % 2 == 0
        here = wide[wide_at : wide_at + count]
        for q in range(match.shape[1] // 128):

            def product(j):
                return src[v, pl.ds(src_at - shift_of(v, q * 4 + j - 2), count)] * here

            a, c, b, d = (product(j) for j in range(4))
            x = jnp.where(lower, a, b) + pltpu.roll(jnp.where(lower, b, a), 64, 1)
            z = jnp.where(middle, c, d) + pltpu.roll(jnp.where(middle, d, c), 64, 1)
            y = jnp.where(even, x, z) + pltpu.roll(jnp.where(even, z, x), 96, 1)
            y = y * table_ref[0:1, q * 128 : (q + 1) * 128]
            y = y.astype(jnp.bfloat16).astype(jnp.float32)
            match[at : at + count, q * 128 : (q + 1) * 128] = y


def weigh(views, tall, planes, block, match, first, table_ref, band_one, band_two, spread_ref, mend):
    out_lanes = planes * block
    span = match.shape[1]
    rest = span - out_lanes
    high = views * tall
    moved = [match[e : e + high].astype(jnp.bfloat16) for e in range(3)]
    raw = dot(jnp.concatenate(moved, axis=1), band_one[...])
    raw = jnp.maximum(raw + table_ref[1:2, 0:out_lanes], 0.0)
    first[0:high, 0:out_lanes] = raw.astype(jnp.bfloat16).astype(jnp.float32)
    raw = sum(
        dot(moved[e][:, out_lanes:], band_one[e * span : e * span + rest, 0:rest])
        for e in range(3)
    )
    raw = jnp.maximum(raw + table_ref[1:2, out_lanes:], 0.0)
    first[0:high, out_lanes:] = raw.astype(jnp.bfloat16).astype(jnp.float32)
    mend()
    moved = [first[e : e + high].astype(jnp.bfloat16) for e in range(3)]
    second = dot(jnp.concatenate(moved, axis=1), band_two[...])
    second = jnp.maximum(second + table_ref[2:3, 0:out_lanes], 0.0) * table_ref[3:4, 0:out_lanes]
    upper = second.astype(jnp.bfloat16)
    under = (second - upper.astype(jnp.float32)).astype(jnp.bfloat16)
    score = dot(jnp.concatenate([upper, under], axis=1), spread_ref[...])
    weight = 1.0 / (1.0 + jnp.exp(-score))
    total = weighted = 0.0
    for v in range(views):
        part = weight[v * tall : (v + 1) * tall]
        at = v * tall + 2
        total = total + part
        weighted = weighted + part * match[at : at + tall, 2 * block : 2 * block + out_lanes]
    return weighted / total


def shift_reader(shifts, before, after):
    planes = shifts.shape[1]

    def shift_of(v, d):
        if d < 0:
            return before[v, planes + d]
        return shifts[v, d] if d < planes else after[v, d - planes]

    return shift_of


def inner_body(
    shifts,
    before,
    after,
    bias_one,
    bias_two,
    view_head,
    own_ref,
    other_ref,
    ref_ref,
    taps_ref,
    cols_ref,
    ref_cols_ref,
    late_ref,
    table_ref,
    spread_ref,
    band_one,
    band_two,
    src,
    wide,
    match,
    first,
):
    views, half, rows, width = own_ref.shape
    planes = shifts.shape[1]
    lanes = 2 * half * rows
    inner = 2 * half // GROUPS
    block = GROUPS * rows
    _, order, _, _, *ends = position()
    pick = columns_of(width, width, 0)
    none = jnp.zeros((8, lanes), jnp.float32)
    columns = turned_ref(ref_ref, pick)
    ref_cols_ref[...] = columns.astype(jnp.bfloat16)
    wide[0:width] = columns
    wide[width:] = none
    pairs = zip(turned_half(own_ref, pick, order), turned_half(other_ref, pick, 1 - order))
    for i, (low, high) in enumerate(pairs):
        columns = low + high
        for k in range(2):
            v = 2 * i + k
            part = columns[:, k * lanes : (k + 1) * lanes]
            cols_ref[v] = part.astype(jnp.bfloat16)
            src[v, 0:8] = none
            src[v, 8 : 8 + width] = part
            src[v, 8 + width :] = none
    build_tables(
        planes, rows, inner, bias_one, bias_two, view_head, ends, table_ref, spread_ref
    )
    build_band(taps_ref, 0, band_one, rows)
    build_band(taps_ref, 1, band_two, rows)
    shift_of = shift_reader(shifts, before, after)
    out_rows = width - MAX_SHIFT
    tall = out_rows + 8
    base = MAX_SHIFT - 2
    for v in range(views):
        pieces = [
            (v * tall + r, 8 + base + r, base + r, min(48, tall - r)) for r in range(0, tall, 48)
        ]
        fill(v, pieces, shift_of, src, wide, match, table_ref, block)
    joined = weigh(
        views,
        tall,
        planes,
        block,
        match,
        first,
        table_ref,
        band_one,
        band_two,
        spread_ref,
        lambda: None,
    )
    late_ref[...] = joined[0:out_rows].astype(jnp.bfloat16)


def outer_body(
    shifts,
    before,
    after,
    cols_ref,
    ref_cols_ref,
    late_ref,
    table_ref,
    spread_ref,
    band_one,
    band_two,
    got_ref,
    swapped_ref,
    out_ref,
    src,
    wide,
    match,
    first,
    joined,
):
    views, width, lanes = cols_ref.shape
    groups, planes, rows, _ = out_ref.shape
    block = groups * rows
    _, order, is_first_tile, is_last_tile, *_ = position()

    left = jnp.where(order == 0, got_ref[...], swapped_ref[...])
    right = jnp.where(order == 0, swapped_ref[...], got_ref[...])
    for v in range(views):
        src[v, 0:LEAD] = left[v * LEAD : (v + 1) * LEAD].astype(jnp.float32)
        src[v, LEAD : LEAD + width] = cols_ref[v].astype(jnp.float32)
        src[v, LEAD + width :] = right[v * LEAD : v * LEAD + EDGE].astype(jnp.float32)
    wide[0:EDGE] = left[views * LEAD :].astype(jnp.float32)
    wide[EDGE : EDGE + width] = ref_cols_ref[...].astype(jnp.float32)
    wide[EDGE + width :] = right[views * LEAD : views * LEAD + EDGE].astype(jnp.float32)
    main = MAX_SHIFT + 8
    tall = main + 8
    shift_of = shift_reader(shifts, before, after)
    for v in range(views):
        at = v * tall
        pieces = [
            (at + r, LEAD - 2 + r, EDGE - 2 + r, min(48, main - r)) for r in range(0, main, 48)
        ]
        pieces += [(at + main, LEAD + width - 4, EDGE + width - 4, 8)]
        fill(v, pieces, shift_of, src, wide, match, table_ref, block)
    none = jnp.zeros((1, match.shape[1]), jnp.float32)

    def mend():
        for v in range(views):
            for row, at_end in ((v * tall, is_first_tile), (v * tall + main + 3, is_last_tile)):
                first[row : row + 1] = jnp.where(at_end, none, first[row : row + 1])

    part = weigh(
        views,
        tall,
        planes,
        block,
        match,
        first,
        table_ref,
        band_one,
        band_two,
        spread_ref,
        mend,
    )
    joined[0:MAX_SHIFT] = part[0:MAX_SHIFT]
    joined[MAX_SHIFT:] = late_ref[...].astype(jnp.float32)
    joined[MAX_SHIFT : MAX_SHIFT + 2] = part[MAX_SHIFT : MAX_SHIFT + 2]
    joined[width - 2 :] = part[main : main + 2]
    size = planes * block
    to = iota((size, size), 0)
    g, j, h = to // (planes * rows), (to // rows) % planes, to % rows
    perm = ((j * groups + g) * rows + h == iota((size, size), 1)).astype(jnp.bfloat16)
    turned = dot_nt(perm, joined[...].astype(jnp.bfloat16)).astype(jnp.bfloat16)
    out_ref[...] = turned.reshape(groups, planes, rows, width)


def whole(memory):
    return pl.BlockSpec(memory_space=memory)


def limit(mebibytes):
    return pltpu.CompilerParams(vmem_limit_bytes=mebibytes * 1024 * 1024)


def swap_planes(value):
    return lax.ppermute(value, "plane", [(0, 1), (1, 0)])


def per_device(ref_feat, src_feat, shifts, conv_one, bias_one, conv_two, bias_two, view_head):
    views, _, rows, width = src_feat.shape
    planes = shifts.shape[1]
    lanes = ref_feat.shape[0] * rows
    tiles, sides = lax.axis_size("tile"), lax.axis_size("plane")
    bf16, f32 = jnp.bfloat16, jnp.float32
    vmem, smem = pltpu.VMEM, pltpu.SMEM
    shape = jax.ShapeDtypeStruct
    if sides == 2:
        own, other = src_feat, swap_planes(src_feat)
    else:
        full = lax.all_gather(src_feat, "plane", axis=1, tiled=True)
        half = full.shape[1] // 2
        own, other = full[:, :half], full[:, half:]

    packet_shape = shape((views * LEAD + EDGE, lanes), bf16)
    part = pl.pallas_call(
        pack_own_body,
        out_shape=packet_shape,
        in_specs=[whole(vmem)] * 2,
        out_specs=whole(vmem),
        compiler_params=limit(8),
        name="pack_own",
    )(own, ref_feat)
    packet = pl.pallas_call(
        pack_other_body,
        out_shape=packet_shape,
        in_specs=[whole(vmem)] * 2,
        out_specs=whole(vmem),
        compiler_params=limit(8),
        name="pack_other",
    )(part, other)

    pairs = [(sides * i, sides * (i + 1)) for i in range(tiles - 1)]
    pairs += [(sides * (i + 1) + 1, sides * i + 1) for i in range(tiles - 1)]
    got = lax.ppermute(packet, ("tile", "plane"), pairs)

    own, other, shifts, conv_one, conv_two, packet = lax.optimization_barrier(
        (own, other, shifts, conv_one, conv_two, packet)
    )
    if sides == 2:
        before = after = swap_planes(shifts)
    else:
        before = lax.ppermute(shifts, "plane", [(i, i + 1) for i in range(sides - 1)])
        after = lax.ppermute(shifts, "plane", [(i + 1, i) for i in range(sides - 1)])

    def taps(kernel):
        flipped = jnp.flip(kernel, axis=2)
        return jnp.transpose(flipped, (3, 4, 1, 2, 0)).reshape(9 * GROUPS, 3 * GROUPS)

    both_taps = jnp.stack([taps(conv_one), taps(conv_two)])
    span = (planes + 4) * GROUPS * rows
    out_lanes = planes * GROUPS * rows
    late_rows = width - MAX_SHIFT
    high = views * (late_rows + 8) + 8
    inner = pl.pallas_call(
        inner_body,
        out_shape=[
            shape((views, width, lanes), bf16),
            shape((width, lanes), bf16),
            shape((late_rows, out_lanes), bf16),
            shape((8, span), f32),
            shape((2 * out_lanes, out_lanes), bf16),
            shape((3 * span, out_lanes), bf16),
            shape((3 * span, out_lanes), bf16),
        ],
        in_specs=[whole(smem)] * 6 + [whole(vmem)] * 4,
        out_specs=[whole(vmem)] * 7,
        scratch_shapes=[
            pltpu.VMEM((views, width + 16, lanes), f32),
            pltpu.VMEM((width + 8, lanes), f32),
            pltpu.VMEM((high, span), f32),
            pltpu.VMEM((high, span), f32),
        ],
        compiler_params=limit(24),
        cost_estimate=pl.CostEstimate(
            flops=5 * 10**9, bytes_accessed=10**6, transcendentals=10**5
        ),
        name="inner_columns",
    )(shifts, before, after, bias_one, bias_two, view_head, own, other, ref_feat, both_taps)
    got, *inner = lax.optimization_barrier((got, *inner))
    if sides == 2:
        swapped = swap_planes(got)
    else:
        both = lax.all_gather(got, "plane", axis=0)
        got, swapped = both[0], both[1]
    high = views * (MAX_SHIFT + 16) + 8
    return pl.pallas_call(
        outer_body,
        out_shape=shape((GROUPS, planes, rows, width), bf16),
        in_specs=[whole(smem)] * 3 + [whole(vmem)] * 9,
        out_specs=whole(vmem),
        scratch_shapes=[
            pltpu.VMEM((views, LEAD + width + EDGE, lanes), f32),
            pltpu.VMEM((EDGE + width + EDGE, lanes), f32),
            pltpu.VMEM((high, span), f32),
            pltpu.VMEM((high, span), f32),
            pltpu.VMEM((width, out_lanes), f32),
        ],
        compiler_params=limit(24),
        name="outer_columns",
    )(shifts, before, after, *inner, got, swapped)


def solution(mesh):
    placed = (
        P(None, None, "tile"),
        P(None, "plane", None, "tile"),
        P(None, "plane"),
        P(),
        P(),
        P(),
        P(),
        P(),
    )
    return jax.shard_map(
        per_device,
        mesh=mesh,
        in_specs=placed,
        out_specs=P(None, "plane", None, "tile"),
        check_vma=False,
    )
```

time: 23 us -> 19 us (0.83)
  the two profiles are of different devices: /device:TPU:25 before, /device:TPU:0 now
where the time goes in v3:
time: 19 us; the launch traced here: 18.8 us
  Pallas kernels  9.35 us (49%)
  starting transfers between devices  5.4 us (28%)
  local copies, waits for them, and re-layouts  2.16 us (11%)
  waiting for transfers between devices  1.66 us (9%)
    ppermute x1, starting transfers between devices, per_device(): got = lax.ppermute(packet, ('tile', 'plane'), pairs)  4.4 us
    pallas_call x1, Pallas kernels, per_device(): pl.pallas_call(outer_body, out_shape=shape((GROUPS, planes, rows, width),...  4.33 us
    pallas_call x1, Pallas kernels, per_device(): pl.pallas_call(inner_body, out_shape=[shape((views, width, lanes), bf16),...  4.16 us
    unnamed x20, local copies, waits for them, and re-layouts  1.79 us
    ppermute x3, waiting for transfers between devices, swap_planes(): return lax.ppermute(value, 'plane', [(0, 1), (1, 0)])  1.65 us
    ppermute x3, starting transfers between devices, swap_planes(): return lax.ppermute(value, 'plane', [(0, 1), (1, 0)])  1 us
    pallas_call x1, Pallas kernels, per_device(): pl.pallas_call(pack_own_body, out_shape=packet_shape, in_specs=[whole(vme...  0.49 us
  transfers between devices with their start and end apart: 4, of which 2 were waited for; matrix products, arithmetic and copies ran while one was open for 2% of the time, Pallas kernels for 25%

profile of v3, /device:TPU:0, one launch (start us, length us, event | category | flops | bytes accessed | tf_op | source)
XLA Modules:
  0.0 18.8 jit_solution(9311033168691182140)
XLA Ops:
  0.0 0.5 %collective-permute-start = (bf16[4,16,4,256]{3,2,1,0:T(4,128)(2,1)}, bf16[4,16,4,256]{3,2,1,0:T(4,128)(2,1)S(1)}, u32[]{:S(2)}, u32[]{:S(2)}) collective-permute-start(bf16[4,16,4,256]{3,2,1,0:T(4,128)(2,1)} %own_ref.2), channel_id=1, source_target_pairs={{0,1},{1,0},{2,3},{3,2},{4,5},{5,4},{6,7},{7,6},{8,9},{9,8},{10,11... | collective-permute-start | bytes 393224 | tf_op jit(solution)/shard_map/ppermute | solution.py:392
  0.5 0.0 copy-start
  0.5 0.9 %copy-done = bf16[4,16,4,256]{3,2,1,0:T(4,128)(2,1)S(1)} copy-done((bf16[4,16,4,256]{3,2,1,0:T(4,128)(2,1)S(1)}, bf16[4,16,4,256]{3,2,1,0:T(4,128)(2,1)}, u32[]{:S(2)}) %copy-start) | copy-done | bytes 131096
  1.4 0.0 copy-start.2
  1.4 0.8 %copy-done.2 = bf16[32,4,256]{2,1,0:T(4,128)(2,1)S(1)} copy-done((bf16[32,4,256]{2,1,0:T(4,128)(2,1)S(1)}, bf16[32,4,256]{2,1,0:T(4,128)(2,1)}, u32[]{:S(2)}) %copy-start.2) | copy-done | bytes 65560
  2.2 0.5 %pack_own.1.part_ref = bf16[592,128]{1,0:T(8,128)(2,1)S(1)} custom-call(bf16[4,16,4,256]{3,2,1,0:T(4,128)(2,1)S(1)} %copy-done, bf16[32,4,256]{2,1,0:T(4,128)(2,1)S(1)} %copy-done.2), custom_call_target="tpu_custom_call" | custom-call | tf_op jit(solution)/shard_map/pack_own/pallas_call | solution.py:411
  2.7 0.0 copy-start.4
  2.7 0.0 copy-start.8
  2.7 0.0 copy-start.9
  2.7 0.0 collective-permute-done.other_ref
  2.7 0.4 %pack_other.1 = bf16[592,128]{1,0:T(8,128)(2,1)S(1)} custom-call(bf16[592,128]{1,0:T(8,128)(2,1)S(1)} %pack_own.1.part_ref, bf16[4,16,4,256]{3,2,1,0:T(4,128)(2,1)S(1)} %collective-permute-done.other_ref), custom_call_target="tpu_custom_call" | custom-call | tf_op jit(solution)/shard_map/pack_other/pallas_call | solution.py:419
  3.1 4.4 %collective-permute-start.2 = (bf16[592,128]{1,0:T(8,128)(2,1)S(1)}, bf16[592,128]{1,0:T(8,128)(2,1)S(1)}, u32[]{:S(2)}, u32[]{:S(2)}) collective-permute-start(bf16[592,128]{1,0:T(8,128)(2,1)S(1)} %pack_other.1), channel_id=1, source_target_pairs={{0,2},{2,4},{4,6},{6,8},{8,10},{10,12},{12,14},{14,16},{16,18},{18... | collective-permute-start | bytes 454664 | tf_op jit(solution)/shard_map/ppermute | solution.py:430
  7.5 0.0 copy-done.4
  7.5 0.1 collective-permute-start.1
  7.6 0.0 copy-done.8
  7.6 0.0 copy-done.9
  7.7 0.1 stack_reshape.7
  7.8 0.0 copy-start.1
  7.8 0.0 copy-start.3
  7.8 0.1 stack_reshape.6
  8.0 0.0 copy-start.5
  8.0 0.0 copy-start.6
  8.0 0.0 copy-start.7
  8.0 0.1 copy.17.taps_ref
  8.1 0.6 %collective-permute-done.1.before.after = s32[4,8]{1,0:T(4,128)S(1)} collective-permute-done((s32[4,8]{1,0:T(4,128)S(1)}, s32[4,8]{1,0:T(4,128)S(1)}, u32[]{:S(2)}, u32[]{:S(2)}) %collective-permute-start.1) | collective-permute-done | bytes 160 | tf_op jit(solution)/shard_map/ppermute | solution.py:392
  8.7 0.0 copy-done.1
  8.7 0.0 copy-done.3
  8.7 0.0 copy-done.5
  8.7 0.0 copy-done.6
  8.8 0.0 copy-done.7
  8.8 4.2 %inner_columns.1 = (bf16[4,256,128]{2,1,0:T(8,128)(2,1)S(1)}, bf16[256,128]{1,0:T(8,128)(2,1)S(1)}, bf16[128,256]{1,0:T(8,128)(2,1)S(1)}, f32[8,384]{1,0:T(8,128...) custom-call(s32[4,8]{1,0:T(4,128)S(1)} %copy-done.4, ...), custom_call_target="tpu_custom_call" | custom-call | flops 5000000000 | bytes 1000000 | tf_op jit(solution)/shard_map/inner_columns/pallas_call | solution.py:450
  12.9 0.0 collective-permute-done.2.got_ref
  12.9 0.5 %collective-permute-start.3 = (bf16[592,128]{1,0:T(8,128)(2,1)S(1)}, bf16[592,128]{1,0:T(8,128)(2,1)S(1)}, u32[]{:S(2)}, u32[]{:S(2)}) collective-permute-start(bf16[592,128]{1,0:T(8,128)(2,1)S(1)} %collective-permute-done.2.got_ref), channel_id=1, source_target_pairs={{0,1},{1,0},{2,3},{3,2},{4,5},{5,4},{6,7},{7,6},{8,9},{9,8},{10,11... | collective-permute-start | bytes 454664 | tf_op jit(solution)/shard_map/ppermute | solution.py:392
  13.4 1.0 %collective-permute-done.3.swapped_ref = bf16[592,128]{1,0:T(8,128)(2,1)S(1)} collective-permute-done((bf16[592,128]{1,0:T(8,128)(2,1)S(1)}, bf16[592,128]{1,0:T(8,128)(2,1)S(1)}, u32[]{:S(2)}, u32[]{:S(2)}) %collective-permute-start.3) | collective-permute-done | bytes 151584 | tf_op jit(solution)/shard_map/ppermute | solution.py:392
  14.4 4.3 %outer_columns.1 = bf16[8,8,4,256]{3,2,1,0:T(4,128)(2,1)} custom-call(s32[4,8]{1,0:T(4,128)S(1)} %copy-done.4, s32[4,8]{1,0:T(4,128)S(1)} %collective-permute-done.1.before.after, s32[4,8]{1,0:T(4,128)S(1)} %collective-permute-done.1.before.after, bf16[4,256,128]{2,1,0:T(8,128)(2,1)S(1)} %get-tuple-element.37.cols_ref, ...), custom_call_target="tpu_custom_call" | custom-call | tf_op jit(solution)/shard_map/outer_columns/pallas_call | solution.py:482
  (4 shorter events, 0.1 us)
Async XLA Ops:
  0.0 2.7 %collective-permute-start = (bf16[4,16,4,256]{3,2,1,0:T(4,128)(2,1)}, bf16[4,16,4,256]{3,2,1,0:T(4,128)(2,1)S(1)}, u32[]{:S(2)}, u32[]{:S(2)}) collective-permute-start(bf16[4,16,4,256]{3,2,1,0:T(4,128)(2,1)} %own_ref.2), channel_id=1, source_target_pairs={{0,1},{1,0},{2,3},{3,2},{4,5},{5,4},{6,7},{7,6},{8,9},{9,8},{10,11... | collective-permute-start | bytes 393224 | tf_op jit(solution)/shard_map/ppermute | solution.py:392
  0.5 0.9 %copy-start = (bf16[4,16,4,256]{3,2,1,0:T(4,128)(2,1)S(1)}, bf16[4,16,4,256]{3,2,1,0:T(4,128)(2,1)}, u32[]{:S(2)}) copy-start(bf16[4,16,4,256]{3,2,1,0:T(4,128)(2,1)} %own_ref.2) | copy-start | bytes 393220
  1.4 0.8 %copy-start.2 = (bf16[32,4,256]{2,1,0:T(4,128)(2,1)S(1)}, bf16[32,4,256]{2,1,0:T(4,128)(2,1)}, u32[]{:S(2)}) copy-start(bf16[32,4,256]{2,1,0:T(4,128)(2,1)} %ref_ref.3) | copy-start | bytes 196612
  2.7 4.8 %copy-start.4 = (s32[4,8]{1,0:T(4,128)S(1)}, s32[4,8]{1,0:T(4,128)}, u32[]{:S(2)}) copy-start(s32[4,8]{1,0:T(4,128)} %shifts.1) | copy-start | bytes 388
  2.7 4.9 %copy-start.8 = (bf16[8,8,3,3,3]{1,0,4,3,2:T(8,128)(2,1)S(1)}, bf16[8,8,3,3,3]{1,0,4,3,2:T(8,128)(2,1)}, u32[]{:S(2)}) copy-start(bf16[8,8,3,3,3]{1,0,4,3,2:T(8,128)(2,1)} %param.13) | copy-start | bytes 10372
  2.7 4.9 %copy-start.9 = (bf16[8,8,3,3,3]{1,0,4,3,2:T(8,128)(2,1)S(1)}, bf16[8,8,3,3,3]{1,0,4,3,2:T(8,128)(2,1)}, u32[]{:S(2)}) copy-start(bf16[8,8,3,3,3]{1,0,4,3,2:T(8,128)(2,1)} %param.11) | copy-start | bytes 10372
  3.1 9.8 %collective-permute-start.2 = (bf16[592,128]{1,0:T(8,128)(2,1)S(1)}, bf16[592,128]{1,0:T(8,128)(2,1)S(1)}, u32[]{:S(2)}, u32[]{:S(2)}) collective-permute-start(bf16[592,128]{1,0:T(8,128)(2,1)S(1)} %pack_other.1), channel_id=1, source_target_pairs={{0,2},{2,4},{4,6},{6,8},{8,10},{10,12},{12,14},{14,16},{16,18},{18... | collective-permute-start | bytes 454664 | tf_op jit(solution)/shard_map/ppermute | solution.py:430
  7.5 1.2 %collective-permute-start.1 = (s32[4,8]{1,0:T(4,128)S(1)}, s32[4,8]{1,0:T(4,128)S(1)}, u32[]{:S(2)}, u32[]{:S(2)}) collective-permute-start(s32[4,8]{1,0:T(4,128)S(1)} %copy-done.4), channel_id=1, source_target_pairs={{0,1},{1,0},{2,3},{3,2},{4,5},{5,4},{6,7},{7,6},{8,9},{9,8},{10,11... | collective-permute-start | bytes 392 | tf_op jit(solution)/shard_map/ppermute | solution.py:392
  7.8 1.0 %copy-start.1 = (bf16[4,16,4,256]{3,2,1,0:T(4,128)(2,1)S(1)}, bf16[4,16,4,256]{3,2,1,0:T(4,128)(2,1)}, u32[]{:S(2)}) copy-start(bf16[4,16,4,256]{3,2,1,0:T(4,128)(2,1)} %own_ref.2) | copy-start | bytes 393220
  7.8 0.9 %copy-start.3 = (bf16[32,4,256]{2,1,0:T(4,128)(2,1)S(1)}, bf16[32,4,256]{2,1,0:T(4,128)(2,1)}, u32[]{:S(2)}) copy-start(bf16[32,4,256]{2,1,0:T(4,128)(2,1)} %ref_ref.3) | copy-start | bytes 196612
  8.0 0.8 %copy-start.5 = (f32[8]{0:T(128)S(1)}, f32[8]{0:T(128)}, u32[]{:S(2)}) copy-start(f32[8]{0:T(128)} %bias_one.1) | copy-start | bytes 100
  8.0 0.8 %copy-start.6 = (f32[8]{0:T(128)S(1)}, f32[8]{0:T(128)}, u32[]{:S(2)}) copy-start(f32[8]{0:T(128)} %bias_two.1) | copy-start | bytes 100
  8.0 0.8 %copy-start.7 = (f32[8]{0:T(128)S(1)}, f32[8]{0:T(128)}, u32[]{:S(2)}) copy-start(f32[8]{0:T(128)} %view_head.1) | copy-start | bytes 100
  12.9 1.5 %collective-permute-start.3 = (bf16[592,128]{1,0:T(8,128)(2,1)S(1)}, bf16[592,128]{1,0:T(8,128)(2,1)S(1)}, u32[]{:S(2)}, u32[]{:S(2)}) collective-permute-start(bf16[592,128]{1,0:T(8,128)(2,1)S(1)} %collective-permute-done.2.got_ref), channel_id=1, source_target_pairs={{0,1},{1,0},{2,3},{3,2},{4,5},{5,4},{6,7},{7,6},{8,9},{9,8},{10,11... | collective-permute-start | bytes 454664 | tf_op jit(solution)/shard_map/ppermute | solution.py:392

commit v4 on v3

--- a/solution.py
+++ b/solution.py
@@ -9,6 +9,7 @@
 MAX_SHIFT = 128
 LEAD = MAX_SHIFT + 16
 EDGE = 16
+BATCH = 2
 FAR = -3.0e38
 
 
@@ -85,13 +86,21 @@
             target_ref[at : at + LEAD] = part.astype(jnp.bfloat16)
 
 
-def pack_own_body(own_ref, ref_ref, part_ref):
+def pack_own_body(own_hbm, ref_hbm, part_ref, own_ref, ref_ref, sems):
+    copies = [
+        pltpu.make_async_copy(own_hbm, own_ref, sems.at[0]),
+        pltpu.make_async_copy(ref_hbm, ref_ref, sems.at[1]),
+    ]
+    for copy in copies:
+        copy.start()
     width = own_ref.shape[3]
     role, order, *_ = position()
     pick = columns_of(LEAD, width, edge_start(role, width, LEAD))
+    pick_ref = columns_of(EDGE, width, edge_start(role, width, EDGE))
+    copies[0].wait()
     store_pairs(part_ref, turned_half(own_ref, pick, order))
-    pick = columns_of(EDGE, width, edge_start(role, width, EDGE))
-    part_ref[own_ref.shape[0] * LEAD :] = turned_ref(ref_ref, pick).astype(jnp.bfloat16)
+    copies[1].wait()
+    part_ref[own_ref.shape[0] * LEAD :] = turned_ref(ref_ref, pick_ref).astype(jnp.bfloat16)
 
 
 def pack_other_body(part_ref, other_ref, packet_ref):
@@ -167,7 +176,7 @@
     spread_ref[out_lanes:] = same
 
 
-def fill(v, pieces, shift_of, src, wide, match, table_ref, block):
+def fill(pieces, near, src, wide, match, table_ref, block):
     for at, src_at, wide_at, count in pieces:
         quarter = iota((count, 128), 1) // block
         lower, middle, even = quarter < 2, (quarter == 1) | (quarter == 2), quarter % 2 == 0
@@ -175,7 +184,7 @@
         for q in range(match.shape[1] // 128):
 
             def product(j):
-                return src[v, pl.ds(src_at - shift_of(v, q * 4 + j - 2), count)] * here
+                return src[pl.ds(src_at - near[q * 4 + j], count)] * here
 
             a, c, b, d = (product(j) for j in range(4))
             x = jnp.where(lower, a, b) + pltpu.roll(jnp.where(lower, b, a), 64, 1)
@@ -186,47 +195,70 @@
             match[at : at + count, q * 128 : (q + 1) * 128] = y
 
 
-def weigh(views, tall, planes, block, match, first, table_ref, band_one, band_two, spread_ref, mend):
+def convolve_first(low, high, planes, block, match, first, table_ref, band_one):
     out_lanes = planes * block
     span = match.shape[1]
     rest = span - out_lanes
-    high = views * tall
-    moved = [match[e : e + high].astype(jnp.bfloat16) for e in range(3)]
+    moved = [match[low + e : high + e].astype(jnp.bfloat16) for e in range(3)]
     raw = dot(jnp.concatenate(moved, axis=1), band_one[...])
     raw = jnp.maximum(raw + table_ref[1:2, 0:out_lanes], 0.0)
-    first[0:high, 0:out_lanes] = raw.astype(jnp.bfloat16).astype(jnp.float32)
+    first[low:high, 0:out_lanes] = raw.astype(jnp.bfloat16).astype(jnp.float32)
     raw = sum(
         dot(moved[e][:, out_lanes:], band_one[e * span : e * span + rest, 0:rest])
         for e in range(3)
     )
     raw = jnp.maximum(raw + table_ref[1:2, out_lanes:], 0.0)
-    first[0:high, out_lanes:] = raw.astype(jnp.bfloat16).astype(jnp.float32)
-    mend()
-    moved = [first[e : e + high].astype(jnp.bfloat16) for e in range(3)]
+    first[low:high, out_lanes:] = raw.astype(jnp.bfloat16).astype(jnp.float32)
+
+
+def weights(low, high, planes, block, first, table_ref, band_two, spread_ref):
+    out_lanes = planes * block
+    moved = [first[low + e : high + e].astype(jnp.bfloat16) for e in range(3)]
     second = dot(jnp.concatenate(moved, axis=1), band_two[...])
     second = jnp.maximum(second + table_ref[2:3, 0:out_lanes], 0.0) * table_ref[3:4, 0:out_lanes]
     upper = second.astype(jnp.bfloat16)
     under = (second - upper.astype(jnp.float32)).astype(jnp.bfloat16)
     score = dot(jnp.concatenate([upper, under], axis=1), spread_ref[...])
-    weight = 1.0 / (1.0 + jnp.exp(-score))
+    return 1.0 / (1.0 + jnp.exp(-score))
+
+
+def blend(views, tall, batch, planes, block, filled, mend, match, first, tables):
+    table_ref, band_one, band_two, spread_ref = tables
+    out_lanes = planes * block
+    starts = range(0, views, batch)
+    for at in starts:
+        for v in range(at, at + batch):
+            filled(v)
+        convolve_first(
+            at * tall, (at + batch) * tall, planes, block, match, first, table_ref, band_one
+        )
+        for v in range(at, at + batch):
+            mend(v * tall)
     total = weighted = 0.0
-    for v in range(views):
-        part = weight[v * tall : (v + 1) * tall]
-        at = v * tall + 2
-        total = total + part
-        weighted = weighted + part * match[at : at + tall, 2 * block : 2 * block + out_lanes]
+    for at in starts:
+        weight = weights(
+            at * tall, (at + batch) * tall, planes, block, first, table_ref, band_two, spread_ref
+        )
+        for v in range(batch):
+            part = weight[v * tall : (v + 1) * tall]
+            row = (at + v) * tall + 2
+            total = total + part
+            weighted = weighted + part * match[row : row + tall, 2 * block : 2 * block + out_lanes]
     return weighted / total
 
 
-def shift_reader(shifts, before, after):
-    planes = shifts.shape[1]
-
-    def shift_of(v, d):
-        if d < 0:
-            return before[v, planes + d]
-        return shifts[v, d] if d < planes else after[v, d - planes]
-
-    return shift_of
+def pack_shifts(shifts, before, after, word_ref):
+    for row, ref in enumerate((before, shifts, after)):
+        word = ref[0:1]
+        for v in range(1, ref.shape[0]):
+            word = word | (ref[v : v + 1] << (8 * v))
+        word_ref[row : row + 1, 0 : word.shape[1]] = word
+
+
+def read_shifts(views, planes, word_ref):
+    at = [(0, planes - 2), (0, planes - 1)] + [(1, d) for d in range(planes)] + [(2, 0), (2, 1)]
+    words = [word_ref[row, d] for row, d in at]
+    return [[(word >> (8 * v)) & 255 for word in words] for v in range(views)]
 
 
 def inner_body(
@@ -243,6 +275,7 @@
     cols_ref,
     ref_cols_ref,
     late_ref,
+    word_ref,
     table_ref,
     spread_ref,
     band_one,
@@ -279,38 +312,30 @@
     )
     build_band(taps_ref, 0, band_one, rows)
     build_band(taps_ref, 1, band_two, rows)
-    shift_of = shift_reader(shifts, before, after)
+    pack_shifts(shifts, before, after, word_ref)
+    near = read_shifts(views, planes, word_ref)
     out_rows = width - MAX_SHIFT
     tall = out_rows + 8
     base = MAX_SHIFT - 2
-    for v in range(views):
+
+    def filled(v):
         pieces = [
             (v * tall + r, 8 + base + r, base + r, min(48, tall - r)) for r in range(0, tall, 48)
         ]
-        fill(v, pieces, shift_of, src, wide, match, table_ref, block)
-    joined = weigh(
-        views,
-        tall,
-        planes,
-        block,
-        match,
-        first,
-        table_ref,
-        band_one,
-        band_two,
-        spread_ref,
-        lambda: None,
+        fill(pieces, near[v], src.at[v], wide, match, table_ref, block)
+
+    tables = table_ref, band_one, band_two, spread_ref
+    joined = blend(
+        views, tall, BATCH, planes, block, filled, lambda row: None, match, first, tables
     )
     late_ref[...] = joined[0:out_rows].astype(jnp.bfloat16)
 
 
 def outer_body(
-    shifts,
-    before,
-    after,
     cols_ref,
     ref_cols_ref,
     late_ref,
+    word_ref,
     table_ref,
     spread_ref,
     band_one,
@@ -329,6 +354,7 @@
     block = groups * rows
     _, order, is_first_tile, is_last_tile, *_ = position()
 
+    near = read_shifts(views, planes, word_ref)
     left = jnp.where(order == 0, got_ref[...], swapped_ref[...])
     right = jnp.where(order == 0, swapped_ref[...], got_ref[...])
     for v in range(views):
@@ -340,34 +366,22 @@
     wide[EDGE + width :] = right[views * LEAD : views * LEAD + EDGE].astype(jnp.float32)
     main = MAX_SHIFT + 8
     tall = main + 8
-    shift_of = shift_reader(shifts, before, after)
-    for v in range(views):
+    none = jnp.zeros((1, match.shape[1]), jnp.float32)
+
+    def filled(v):
         at = v * tall
         pieces = [
             (at + r, LEAD - 2 + r, EDGE - 2 + r, min(48, main - r)) for r in range(0, main, 48)
         ]
         pieces += [(at + main, LEAD + width - 4, EDGE + width - 4, 8)]
-        fill(v, pieces, shift_of, src, wide, match, table_ref, block)
-    none = jnp.zeros((1, match.shape[1]), jnp.float32)
-
-    def mend():
-        for v in range(views):
-            for row, at_end in ((v * tall, is_first_tile), (v * tall + main + 3, is_last_tile)):
-                first[row : row + 1] = jnp.where(at_end, none, first[row : row + 1])
-
-    part = weigh(
-        views,
-        tall,
-        planes,
-        block,
-        match,
-        first,
-        table_ref,
-        band_one,
-        band_two,
-        spread_ref,
-        mend,
-    )
+        fill(pieces, near[v], src.at[v], wide, match, table_ref, block)
+
+    def mend(row):
+        for at, at_end in ((row, is_first_tile), (row + main + 3, is_last_tile)):
+            first[at : at + 1] = jnp.where(at_end, none, first[at : at + 1])
+
+    tables = table_ref, band_one, band_two, spread_ref
+    part = blend(views, tall, BATCH, planes, block, filled, mend, match, first, tables)
     joined[0:MAX_SHIFT] = part[0:MAX_SHIFT]
     joined[MAX_SHIFT:] = late_ref[...].astype(jnp.float32)
     joined[MAX_SHIFT : MAX_SHIFT + 2] = part[MAX_SHIFT : MAX_SHIFT + 2]
@@ -398,7 +412,7 @@
     lanes = ref_feat.shape[0] * rows
     tiles, sides = lax.axis_size("tile"), lax.axis_size("plane")
     bf16, f32 = jnp.bfloat16, jnp.float32
-    vmem, smem = pltpu.VMEM, pltpu.SMEM
+    vmem = pltpu.VMEM
     shape = jax.ShapeDtypeStruct
     if sides == 2:
         own, other = src_feat, swap_planes(src_feat)
@@ -411,11 +425,16 @@
     part = pl.pallas_call(
         pack_own_body,
         out_shape=packet_shape,
-        in_specs=[whole(vmem)] * 2,
+        in_specs=[whole(pltpu.HBM)] * 2,
         out_specs=whole(vmem),
+        scratch_shapes=[
+            pltpu.VMEM(own.shape, bf16),
+            pltpu.VMEM(ref_feat.shape, bf16),
+            pltpu.SemaphoreType.DMA((2,)),
+        ],
         compiler_params=limit(8),
         name="pack_own",
-    )(own, ref_feat)
+    )(*(pltpu.with_memory_space_constraint(x, pltpu.HBM) for x in (own, ref_feat)))
     packet = pl.pallas_call(
         pack_other_body,
         out_shape=packet_shape,
@@ -453,13 +472,14 @@
             shape((views, width, lanes), bf16),
             shape((width, lanes), bf16),
             shape((late_rows, out_lanes), bf16),
+            shape((8, 128), jnp.int32),
             shape((8, span), f32),
             shape((2 * out_lanes, out_lanes), bf16),
             shape((3 * span, out_lanes), bf16),
             shape((3 * span, out_lanes), bf16),
         ],
-        in_specs=[whole(smem)] * 6 + [whole(vmem)] * 4,
-        out_specs=[whole(vmem)] * 7,
+        in_specs=[whole(vmem)] * 10,
+        out_specs=[whole(vmem)] * 8,
         scratch_shapes=[
             pltpu.VMEM((views, width + 16, lanes), f32),
             pltpu.VMEM((width + 8, lanes), f32),
@@ -482,7 +502,7 @@
     return pl.pallas_call(
         outer_body,
         out_shape=shape((GROUPS, planes, rows, width), bf16),
-        in_specs=[whole(smem)] * 3 + [whole(vmem)] * 9,
+        in_specs=[whole(vmem)] * 10,
         out_specs=whole(vmem),
         scratch_shapes=[
             pltpu.VMEM((views, LEAD + width + EDGE, lanes), f32),
@@ -493,7 +513,7 @@
         ],
         compiler_params=limit(24),
         name="outer_columns",
-    )(shifts, before, after, *inner, got, swapped)
+    )(*inner, got, swapped)
 
 
 def solution(mesh):

time: 19 us -> 17.2 us (0.905)
  local copies, waits for them, and re-layouts: 2.16 us -> 0.43 us
    unnamed x20 -> x16, local copies, waits for them, and re-layouts: 1.79 us -> 0.05 us
    pallas_call x1, Pallas kernels: 0.49 us -> 1.57 us  [per_device(): pl.pallas_call(pack_own_body, out_shape=packet_shape, in_specs=[whole(plt...]
    pallas_call x1, Pallas kernels: 4.16 us -> 3.47 us  [per_device(): pl.pallas_call(inner_body, out_shape=[shape((views, width, lanes), bf16),...]
    pallas_call x1, Pallas kernels: 4.33 us -> 3.87 us  [per_device(): pl.pallas_call(outer_body, out_shape=shape((GROUPS, planes, rows, width),...]
  transfers between devices with their start and end apart: 4 -> 4, of which waited for: 2 -> 2; matrix products, arithmetic and copies ran while one was open for 2% -> 2% of each run, Pallas kernels for 25% -> 30%
where the time goes in v4:
time: 17.2 us; the launch traced here: 17 us
  Pallas kernels  9.29 us (54%)
  starting transfers between devices  5.42 us (32%)
  waiting for transfers between devices  1.65 us (10%)
  local copies, waits for them, and re-layouts  0.43 us (2%)
  between operations  0.2 us (1%)
    ppermute x1, starting transfers between devices, per_device(): got = lax.ppermute(packet, ('tile', 'plane'), pairs)  4.4 us
    pallas_call x1, Pallas kernels, per_device(): pl.pallas_call(outer_body, out_shape=shape((GROUPS, planes, rows, width),...  3.87 us
    pallas_call x1, Pallas kernels, per_device(): pl.pallas_call(inner_body, out_shape=[shape((views, width, lanes), bf16),...  3.47 us
    ppermute x3, waiting for transfers between devices, swap_planes(): return lax.ppermute(value, 'plane', [(0, 1), (1, 0)])  1.65 us
    pallas_call x1, Pallas kernels, per_device(): pl.pallas_call(pack_own_body, out_shape=packet_shape, in_specs=[whole(plt...  1.57 us
    ppermute x3, starting transfers between devices, swap_planes(): return lax.ppermute(value, 'plane', [(0, 1), (1, 0)])  1.02 us
    pallas_call x1, Pallas kernels, per_device(): pl.pallas_call(pack_other_body, out_shape=packet_shape, in_specs=[whole(v...  0.38 us
  transfers between devices with their start and end apart: 4, of which 2 were waited for; matrix products, arithmetic and copies ran while one was open for 2% of the time, Pallas kernels for 30%

profile of v4, /device:TPU:0, one launch (start us, length us, event | category | flops | bytes accessed | tf_op | source)
XLA Modules:
  0.0 17.0 jit_solution(12221074393026793103)
XLA Ops:
  0.0 0.5 %collective-permute-start = (bf16[4,16,4,256]{3,2,1,0:T(4,128)(2,1)}, bf16[4,16,4,256]{3,2,1,0:T(4,128)(2,1)S(1)}, u32[]{:S(2)}, u32[]{:S(2)}) collective-permute-start(bf16[4,16,4,256]{3,2,1,0:T(4,128)(2,1)} %own_ref), channel_id=1, source_target_pairs={{0,1},{1,0},{2,3},{3,2},{4,5},{5,4},{6,7},{7,6},{8,9},{9,8},{10,11... | collective-permute-start | bytes 393224 | tf_op jit(solution)/shard_map/ppermute | solution.py:406
  0.5 1.6 %pack_own.1.part_ref = bf16[592,128]{1,0:T(8,128)(2,1)S(1)} custom-call(bf16[4,16,4,256]{3,2,1,0:T(4,128)(2,1)} %own_ref, bf16[32,4,256]{2,1,0:T(4,128)(2,1)} %ref_ref.1), custom_call_target="tpu_custom_call" | custom-call | tf_op jit(solution)/shard_map/pack_own/pallas_call | solution.py:425
  2.0 0.0 copy-start.2
  2.0 0.0 copy-start.6
  2.1 0.0 copy-start.7
  2.1 0.0 collective-permute-done.other_ref
  2.1 0.4 %pack_other.1 = bf16[592,128]{1,0:T(8,128)(2,1)S(1)} custom-call(bf16[592,128]{1,0:T(8,128)(2,1)S(1)} %pack_own.1.part_ref, bf16[4,16,4,256]{3,2,1,0:T(4,128)(2,1)S(1)} %collective-permute-done.other_ref), custom_call_target="tpu_custom_call" | custom-call | tf_op jit(solution)/shard_map/pack_other/pallas_call | solution.py:438
  2.5 4.4 %collective-permute-start.1 = (bf16[592,128]{1,0:T(8,128)(2,1)S(1)}, bf16[592,128]{1,0:T(8,128)(2,1)S(1)}, u32[]{:S(2)}, u32[]{:S(2)}) collective-permute-start(bf16[592,128]{1,0:T(8,128)(2,1)S(1)} %pack_other.1), channel_id=1, source_target_pairs={{0,2},{2,4},{4,6},{6,8},{8,10},{10,12},{12,14},{14,16},{16,18},{18... | collective-permute-start | bytes 454664 | tf_op jit(solution)/shard_map/ppermute | solution.py:449
  6.9 0.0 copy-done.2
  6.9 0.1 collective-permute-start.2
  7.0 0.0 copy-done.6
  7.0 0.0 copy-done.7
  7.0 0.1 stack_reshape.7
  7.1 0.0 copy-start
  7.2 0.0 copy-start.1
  7.2 0.1 stack_reshape.6
  7.3 0.0 copy-start.3
  7.3 0.0 copy-start.4
  7.3 0.0 copy-start.5
  7.4 0.1 copy.17.taps_ref
  7.5 0.6 %collective-permute-done.2.before.after = s32[4,8]{1,0:T(4,128)S(1)} collective-permute-done((s32[4,8]{1,0:T(4,128)S(1)}, s32[4,8]{1,0:T(4,128)S(1)}, u32[]{:S(2)}, u32[]{:S(2)}) %collective-permute-start.2) | collective-permute-done | bytes 160 | tf_op jit(solution)/shard_map/ppermute | solution.py:406
  8.1 0.0 copy-done
  8.1 0.0 copy-done.1
  8.1 0.0 copy-done.3
  8.1 0.0 copy-done.4
  8.1 0.0 copy-done.5
  8.1 3.5 %inner_columns.1 = (bf16[4,256,128]{2,1,0:T(8,128)(2,1)S(1)}, bf16[256,128]{1,0:T(8,128)(2,1)S(1)}, bf16[128,256]{1,0:T(8,128)(2,1)S(1)}, s32[8,128]{1,0:T(8,128...) custom-call(s32[4,8]{1,0:T(4,128)S(1)} %copy-done.2, ...), custom_call_target="tpu_custom_call" | custom-call | flops 5000000000 | bytes 1000000 | tf_op jit(solution)/shard_map/inner_columns/pallas_call | solution.py:469
  11.6 0.0 collective-permute-done.1.got_ref
  11.6 0.5 %collective-permute-start.3 = (bf16[592,128]{1,0:T(8,128)(2,1)S(1)}, bf16[592,128]{1,0:T(8,128)(2,1)S(1)}, u32[]{:S(2)}, u32[]{:S(2)}) collective-permute-start(bf16[592,128]{1,0:T(8,128)(2,1)S(1)} %collective-permute-done.1.got_ref), channel_id=1, source_target_pairs={{0,1},{1,0},{2,3},{3,2},{4,5},{5,4},{6,7},{7,6},{8,9},{9,8},{10,11... | collective-permute-start | bytes 454664 | tf_op jit(solution)/shard_map/ppermute | solution.py:406
  12.1 1.0 %collective-permute-done.3.swapped_ref = bf16[592,128]{1,0:T(8,128)(2,1)S(1)} collective-permute-done((bf16[592,128]{1,0:T(8,128)(2,1)S(1)}, bf16[592,128]{1,0:T(8,128)(2,1)S(1)}, u32[]{:S(2)}, u32[]{:S(2)}) %collective-permute-start.3) | collective-permute-done | bytes 151584 | tf_op jit(solution)/shard_map/ppermute | solution.py:406
  13.1 3.9 %outer_columns.1 = bf16[8,8,4,256]{3,2,1,0:T(4,128)(2,1)} custom-call(bf16[4,256,128]{2,1,0:T(8,128)(2,1)S(1)} %get-tuple-element.40.cols_ref, bf16[256,128]{1,0:T(8,128)(2,1)S(1)} %get-tuple-element.41.ref_cols_ref, bf16[128,256]{1,0:T(8,128)(2,1)S(1)} %get-tuple-element.42.late_ref, s32[8,128]{1,0:T(8,128)S(1)} %get-tuple-element.43.word_ref, ...), custom_call_target="tpu_custom_call" | custom-call | tf_op jit(solution)/shard_map/outer_columns/pallas_call | solution.py:502
  (4 shorter events, 0.1 us)
Async XLA Ops:
  0.0 2.1 %collective-permute-start = (bf16[4,16,4,256]{3,2,1,0:T(4,128)(2,1)}, bf16[4,16,4,256]{3,2,1,0:T(4,128)(2,1)S(1)}, u32[]{:S(2)}, u32[]{:S(2)}) collective-permute-start(bf16[4,16,4,256]{3,2,1,0:T(4,128)(2,1)} %own_ref), channel_id=1, source_target_pairs={{0,1},{1,0},{2,3},{3,2},{4,5},{5,4},{6,7},{7,6},{8,9},{9,8},{10,11... | collective-permute-start | bytes 393224 | tf_op jit(solution)/shard_map/ppermute | solution.py:406
  2.0 4.8 %copy-start.2 = (s32[4,8]{1,0:T(4,128)S(1)}, s32[4,8]{1,0:T(4,128)}, u32[]{:S(2)}) copy-start(s32[4,8]{1,0:T(4,128)} %shifts) | copy-start | bytes 388
  2.0 4.9 %copy-start.6 = (bf16[8,8,3,3,3]{1,0,4,3,2:T(8,128)(2,1)S(1)}, bf16[8,8,3,3,3]{1,0,4,3,2:T(8,128)(2,1)}, u32[]{:S(2)}) copy-start(bf16[8,8,3,3,3]{1,0,4,3,2:T(8,128)(2,1)} %param.13) | copy-start | bytes 10372
  2.1 4.9 %copy-start.7 = (bf16[8,8,3,3,3]{1,0,4,3,2:T(8,128)(2,1)S(1)}, bf16[8,8,3,3,3]{1,0,4,3,2:T(8,128)(2,1)}, u32[]{:S(2)}) copy-start(bf16[8,8,3,3,3]{1,0,4,3,2:T(8,128)(2,1)} %param.11) | copy-start | bytes 10372
  2.5 9.2 %collective-permute-start.1 = (bf16[592,128]{1,0:T(8,128)(2,1)S(1)}, bf16[592,128]{1,0:T(8,128)(2,1)S(1)}, u32[]{:S(2)}, u32[]{:S(2)}) collective-permute-start(bf16[592,128]{1,0:T(8,128)(2,1)S(1)} %pack_other.1), channel_id=1, source_target_pairs={{0,2},{2,4},{4,6},{6,8},{8,10},{10,12},{12,14},{14,16},{16,18},{18... | collective-permute-start | bytes 454664 | tf_op jit(solution)/shard_map/ppermute | solution.py:449
  6.9 1.2 %collective-permute-start.2 = (s32[4,8]{1,0:T(4,128)S(1)}, s32[4,8]{1,0:T(4,128)S(1)}, u32[]{:S(2)}, u32[]{:S(2)}) collective-permute-start(s32[4,8]{1,0:T(4,128)S(1)} %copy-done.2), channel_id=1, source_target_pairs={{0,1},{1,0},{2,3},{3,2},{4,5},{5,4},{6,7},{7,6},{8,9},{9,8},{10,11... | collective-permute-start | bytes 392 | tf_op jit(solution)/shard_map/ppermute | solution.py:406
  7.1 1.0 %copy-start = (bf16[4,16,4,256]{3,2,1,0:T(4,128)(2,1)S(1)}, bf16[4,16,4,256]{3,2,1,0:T(4,128)(2,1)}, u32[]{:S(2)}) copy-start(bf16[4,16,4,256]{3,2,1,0:T(4,128)(2,1)} %own_ref) | copy-start | bytes 393220
  7.2 0.9 %copy-start.1 = (bf16[32,4,256]{2,1,0:T(4,128)(2,1)S(1)}, bf16[32,4,256]{2,1,0:T(4,128)(2,1)}, u32[]{:S(2)}) copy-start(bf16[32,4,256]{2,1,0:T(4,128)(2,1)} %ref_ref.1) | copy-start | bytes 196612
  7.3 0.8 %copy-start.3 = (f32[8]{0:T(128)S(1)}, f32[8]{0:T(128)}, u32[]{:S(2)}) copy-start(f32[8]{0:T(128)} %bias_one.1) | copy-start | bytes 100
  7.3 0.8 %copy-start.4 = (f32[8]{0:T(128)S(1)}, f32[8]{0:T(128)}, u32[]{:S(2)}) copy-start(f32[8]{0:T(128)} %bias_two.1) | copy-start | bytes 100
  7.3 0.8 %copy-start.5 = (f32[8]{0:T(128)S(1)}, f32[8]{0:T(128)}, u32[]{:S(2)}) copy-start(f32[8]{0:T(128)} %view_head.1) | copy-start | bytes 100
  11.6 1.5 %collective-permute-start.3 = (bf16[592,128]{1,0:T(8,128)(2,1)S(1)}, bf16[592,128]{1,0:T(8,128)(2,1)S(1)}, u32[]{:S(2)}, u32[]{:S(2)}) collective-permute-start(bf16[592,128]{1,0:T(8,128)(2,1)S(1)} %collective-permute-done.1.got_ref), channel_id=1, source_target_pairs={{0,1},{1,0},{2,3},{3,2},{4,5},{5,4},{6,7},{7,6},{8,9},{9,8},{10,11... | collective-permute-start | bytes 454664 | tf_op jit(solution)/shard_map/ppermute | solution.py:406

commit v5 on v4

--- a/solution.py
+++ b/solution.py
@@ -77,46 +77,30 @@
     return jnp.where(role == 0, width - count, 0)
 
 
-def store_pairs(target_ref, pairs):
-    lanes = target_ref.shape[1]
-    for i, pair in enumerate(pairs):
-        for k in range(2):
-            at = (2 * i + k) * LEAD
-            part = pair[:, k * lanes : (k + 1) * lanes]
-            target_ref[at : at + LEAD] = part.astype(jnp.bfloat16)
-
-
-def pack_own_body(own_hbm, ref_hbm, part_ref, own_ref, ref_ref, sems):
+def stage_body(own_hbm, ref_hbm, own_ref, ref_ref, sems):
     copies = [
         pltpu.make_async_copy(own_hbm, own_ref, sems.at[0]),
         pltpu.make_async_copy(ref_hbm, ref_ref, sems.at[1]),
     ]
     for copy in copies:
         copy.start()
+    for copy in copies:
+        copy.wait()
+
+
+def pack_body(own_ref, other_ref, ref_ref, packet_ref):
     width = own_ref.shape[3]
-    role, order, *_ = position()
-    pick = columns_of(LEAD, width, edge_start(role, width, LEAD))
-    pick_ref = columns_of(EDGE, width, edge_start(role, width, EDGE))
-    copies[0].wait()
-    store_pairs(part_ref, turned_half(own_ref, pick, order))
-    copies[1].wait()
-    part_ref[own_ref.shape[0] * LEAD :] = turned_ref(ref_ref, pick_ref).astype(jnp.bfloat16)
-
-
-def pack_other_body(part_ref, other_ref, packet_ref):
-    width = other_ref.shape[3]
     lanes = packet_ref.shape[1]
     role, order, *_ = position()
     pick = columns_of(LEAD, width, edge_start(role, width, LEAD))
-    pairs = turned_half(other_ref, pick, 1 - order)
-    for i, pair in enumerate(pairs):
+    halves = zip(turned_half(own_ref, pick, order), turned_half(other_ref, pick, 1 - order))
+    for i, (low, high) in enumerate(halves):
+        pair = (low + high).astype(jnp.bfloat16)
         for k in range(2):
             at = (2 * i + k) * LEAD
-            part = pair[:, k * lanes : (k + 1) * lanes]
-            both = part_ref[at : at + LEAD].astype(jnp.float32) + part
-            packet_ref[at : at + LEAD] = both.astype(jnp.bfloat16)
-    at = other_ref.shape[0] * LEAD
-    packet_ref[at:] = part_ref[at:]
+            packet_ref[at : at + LEAD] = pair[:, k * lanes : (k + 1) * lanes]
+    pick = columns_of(EDGE, width, edge_start(role, width, EDGE))
+    packet_ref[own_ref.shape[0] * LEAD :] = turned_ref(ref_ref, pick).astype(jnp.bfloat16)
 
 
 def lane_table(values_ref, rows, lane):
@@ -202,13 +186,13 @@
     moved = [match[low + e : high + e].astype(jnp.bfloat16) for e in range(3)]
     raw = dot(jnp.concatenate(moved, axis=1), band_one[...])
     raw = jnp.maximum(raw + table_ref[1:2, 0:out_lanes], 0.0)
-    first[low:high, 0:out_lanes] = raw.astype(jnp.bfloat16).astype(jnp.float32)
+    first[low:high, 0:out_lanes] = raw
     raw = sum(
         dot(moved[e][:, out_lanes:], band_one[e * span : e * span + rest, 0:rest])
         for e in range(3)
     )
     raw = jnp.maximum(raw + table_ref[1:2, out_lanes:], 0.0)
-    first[low:high, out_lanes:] = raw.astype(jnp.bfloat16).astype(jnp.float32)
+    first[low:high, out_lanes:] = raw
 
 
 def weights(low, high, planes, block, first, table_ref, band_two, spread_ref):
@@ -222,24 +206,25 @@
     return 1.0 / (1.0 + jnp.exp(-score))
 
 
-def blend(views, tall, batch, planes, block, filled, mend, match, first, tables):
-    table_ref, band_one, band_two, spread_ref = tables
-    out_lanes = planes * block
-    starts = range(0, views, batch)
-    for at in starts:
-        for v in range(at, at + batch):
+def first_stage(views, tall, planes, block, filled, mend, match, first, table_ref, band_one):
+    for at in range(0, views, BATCH):
+        for v in range(at, at + BATCH):
             filled(v)
         convolve_first(
-            at * tall, (at + batch) * tall, planes, block, match, first, table_ref, band_one
+            at * tall, (at + BATCH) * tall, planes, block, match, first, table_ref, band_one
         )
-        for v in range(at, at + batch):
+        for v in range(at, at + BATCH):
             mend(v * tall)
+
+
+def second_stage(views, tall, planes, block, match, first, table_ref, band_two, spread_ref):
+    out_lanes = planes * block
     total = weighted = 0.0
-    for at in starts:
+    for at in range(0, views, BATCH):
         weight = weights(
-            at * tall, (at + batch) * tall, planes, block, first, table_ref, band_two, spread_ref
+            at * tall, (at + BATCH) * tall, planes, block, first, table_ref, band_two, spread_ref
         )
-        for v in range(batch):
+        for v in range(BATCH):
             part = weight[v * tall : (v + 1) * tall]
             row = (at + v) * tall + 2
             total = total + part
@@ -274,16 +259,15 @@
     taps_ref,
     cols_ref,
     ref_cols_ref,
-    late_ref,
     word_ref,
     table_ref,
     spread_ref,
     band_one,
     band_two,
+    match,
+    first,
     src,
     wide,
-    match,
-    first,
 ):
     views, half, rows, width = own_ref.shape
     planes = shifts.shape[1]
@@ -324,9 +308,19 @@
         ]
         fill(pieces, near[v], src.at[v], wide, match, table_ref, block)
 
-    tables = table_ref, band_one, band_two, spread_ref
-    joined = blend(
-        views, tall, BATCH, planes, block, filled, lambda row: None, match, first, tables
+    first_stage(
+        views, tall, planes, block, filled, lambda row: None, match, first, table_ref, band_one
+    )
+    for ref in (match, first):
+        ref[views * tall :] = jnp.zeros((8, match.shape[1]), jnp.float32)
+
+
+def late_body(match, first, table_ref, spread_ref, band_two, late_ref):
+    out_rows, out_lanes = late_ref.shape
+    block = (match.shape[1] - out_lanes) // 4
+    views = match.shape[0] // (out_rows + 8)
+    joined = second_stage(
+        views, out_rows + 8, out_lanes // block, block, match, first, table_ref, band_two, spread_ref
     )
     late_ref[...] = joined[0:out_rows].astype(jnp.bfloat16)
 
@@ -334,12 +328,12 @@
 def outer_body(
     cols_ref,
     ref_cols_ref,
-    late_ref,
     word_ref,
     table_ref,
     spread_ref,
     band_one,
     band_two,
+    late_ref,
     got_ref,
     swapped_ref,
     out_ref,
@@ -380,8 +374,10 @@
         for at, at_end in ((row, is_first_tile), (row + main + 3, is_last_tile)):
             first[at : at + 1] = jnp.where(at_end, none, first[at : at + 1])
 
-    tables = table_ref, band_one, band_two, spread_ref
-    part = blend(views, tall, BATCH, planes, block, filled, mend, match, first, tables)
+    first_stage(views, tall, planes, block, filled, mend, match, first, table_ref, band_one)
+    part = second_stage(
+        views, tall, planes, block, match, first, table_ref, band_two, spread_ref
+    )
     joined[0:MAX_SHIFT] = part[0:MAX_SHIFT]
     joined[MAX_SHIFT:] = late_ref[...].astype(jnp.float32)
     joined[MAX_SHIFT : MAX_SHIFT + 2] = part[MAX_SHIFT : MAX_SHIFT + 2]
@@ -422,27 +418,23 @@
         own, other = full[:, :half], full[:, half:]
 
     packet_shape = shape((views * LEAD + EDGE, lanes), bf16)
-    part = pl.pallas_call(
-        pack_own_body,
-        out_shape=packet_shape,
+    own, ref_feat = pl.pallas_call(
+        stage_body,
+        out_shape=[shape(own.shape, bf16), shape(ref_feat.shape, bf16)],
         in_specs=[whole(pltpu.HBM)] * 2,
-        out_specs=whole(vmem),
-        scratch_shapes=[
-            pltpu.VMEM(own.shape, bf16),
-            pltpu.VMEM(ref_feat.shape, bf16),
-            pltpu.SemaphoreType.DMA((2,)),
-        ],
+        out_specs=[whole(vmem)] * 2,
+        scratch_shapes=[pltpu.SemaphoreType.DMA((2,))],
         compiler_params=limit(8),
-        name="pack_own",
+        name="stage",
     )(*(pltpu.with_memory_space_constraint(x, pltpu.HBM) for x in (own, ref_feat)))
     packet = pl.pallas_call(
-        pack_other_body,
+        pack_body,
         out_shape=packet_shape,
-        in_specs=[whole(vmem)] * 2,
+        in_specs=[whole(vmem)] * 3,
         out_specs=whole(vmem),
         compiler_params=limit(8),
-        name="pack_other",
-    )(part, other)
+        name="pack_edges",
+    )(own, other, ref_feat)
 
     pairs = [(sides * i, sides * (i + 1)) for i in range(tiles - 1)]
     pairs += [(sides * (i + 1) + 1, sides * i + 1) for i in range(tiles - 1)]
@@ -466,38 +458,48 @@
     out_lanes = planes * GROUPS * rows
     late_rows = width - MAX_SHIFT
     high = views * (late_rows + 8) + 8
-    inner = pl.pallas_call(
+    *inner, match, first = pl.pallas_call(
         inner_body,
         out_shape=[
             shape((views, width, lanes), bf16),
             shape((width, lanes), bf16),
-            shape((late_rows, out_lanes), bf16),
             shape((8, 128), jnp.int32),
             shape((8, span), f32),
             shape((2 * out_lanes, out_lanes), bf16),
             shape((3 * span, out_lanes), bf16),
             shape((3 * span, out_lanes), bf16),
+            shape((high, span), f32),
+            shape((high, span), f32),
         ],
         in_specs=[whole(vmem)] * 10,
-        out_specs=[whole(vmem)] * 8,
+        out_specs=[whole(vmem)] * 9,
         scratch_shapes=[
             pltpu.VMEM((views, width + 16, lanes), f32),
             pltpu.VMEM((width + 8, lanes), f32),
-            pltpu.VMEM((high, span), f32),
-            pltpu.VMEM((high, span), f32),
         ],
         compiler_params=limit(24),
         cost_estimate=pl.CostEstimate(
-            flops=5 * 10**9, bytes_accessed=10**6, transcendentals=10**5
+            flops=3 * 10**9, bytes_accessed=10**6, transcendentals=10**5
         ),
         name="inner_columns",
     )(shifts, before, after, bias_one, bias_two, view_head, own, other, ref_feat, both_taps)
-    got, *inner = lax.optimization_barrier((got, *inner))
+    got, match, first, *inner = lax.optimization_barrier((got, match, first, *inner))
     if sides == 2:
         swapped = swap_planes(got)
     else:
         both = lax.all_gather(got, "plane", axis=0)
         got, swapped = both[0], both[1]
+    late = pl.pallas_call(
+        late_body,
+        out_shape=shape((late_rows, out_lanes), bf16),
+        in_specs=[whole(vmem)] * 5,
+        out_specs=whole(vmem),
+        compiler_params=limit(24),
+        cost_estimate=pl.CostEstimate(
+            flops=2 * 10**9, bytes_accessed=10**6, transcendentals=10**5
+        ),
+        name="late_columns",
+    )(match, first, inner[3], inner[4], inner[6])
     high = views * (MAX_SHIFT + 16) + 8
     return pl.pallas_call(
         outer_body,
@@ -513,7 +515,7 @@
         ],
         compiler_params=limit(24),
         name="outer_columns",
-    )(*inner, got, swapped)
+    )(*inner, late, got, swapped)
 
 
 def solution(mesh):

time: 17.2 us -> 16.9 us (0.983)
  the two profiles are of different devices: /device:TPU:0 before, /device:TPU:25 now
where the time goes in v5:
time: 16.9 us; the launch traced here: 16.7 us
  Pallas kernels  8.68 us (51%)
  starting transfers between devices  6.53 us (39%)
  waiting for transfers between devices  0.93 us (6%)
  local copies, waits for them, and re-layouts  0.41 us (2%)
    ppermute x1, starting transfers between devices, per_device(): got = lax.ppermute(packet, ('tile', 'plane'), pairs)  3.96 us
    pallas_call x1, Pallas kernels, per_device(): pl.pallas_call(outer_body, out_shape=shape((GROUPS, planes, rows, width),...  3.76 us
    ppermute x3, starting transfers between devices, swap_planes(): return lax.ppermute(value, 'plane', [(0, 1), (1, 0)])  2.57 us
    pallas_call x1, Pallas kernels, per_device(): pl.pallas_call(inner_body, out_shape=[shape((views, width, lanes), bf16),...  2.18 us
    pallas_call x1, Pallas kernels, per_device(): pl.pallas_call(late_body, out_shape=shape((late_rows, out_lanes), bf16),...  1.3 us
    ppermute x3, waiting for transfers between devices, swap_planes(): return lax.ppermute(value, 'plane', [(0, 1), (1, 0)])  0.93 us
    pallas_call x1, Pallas kernels, per_device(): pl.pallas_call(stage_body, out_shape=[shape(own.shape, bf16), shape(ref_f...  0.92 us
    pallas_call x1, Pallas kernels, per_device(): pl.pallas_call(pack_body, out_shape=packet_shape, in_specs=[whole(vmem)]...  0.51 us
  transfers between devices with their start and end apart: 4, of which 2 were waited for; matrix products, arithmetic and copies ran while one was open for 2% of the time, Pallas kernels for 26%

profile of v5, /device:TPU:25, one launch (start us, length us, event | category | flops | bytes accessed | tf_op | source)
XLA Modules:
  0.0 16.7 jit_solution(14186111059198741613)
XLA Ops:
  0.0 0.7 %collective-permute-start = (bf16[4,16,4,256]{3,2,1,0:T(4,128)(2,1)}, bf16[4,16,4,256]{3,2,1,0:T(4,128)(2,1)S(1)}, u32[]{:S(2)}, u32[]{:S(2)}) collective-permute-start(bf16[4,16,4,256]{3,2,1,0:T(4,128)(2,1)} %own_hbm.1), channel_id=1, source_target_pairs={{0,1},{1,0},{2,3},{3,2},{4,5},{5,4},{6,7},{7,6},{8,9},{9,8},{10,11... | collective-permute-start | bytes 393224 | tf_op jit(solution)/shard_map/ppermute | solution.py:402
  0.7 0.9 %stage.1 = (bf16[4,16,4,256]{3,2,1,0:T(4,128)(2,1)S(1)}, bf16[32,4,256]{2,1,0:T(4,128)(2,1)S(1)}) custom-call(bf16[4,16,4,256]{3,2,1,0:T(4,128)(2,1)} %own_hbm.1, bf16[32,4,256]{2,1,0:T(4,128)(2,1)} %ref_hbm.1), custom_call_target="tpu_custom_call" | custom-call | tf_op jit(solution)/shard_map/stage/pallas_call | solution.py:421
  1.6 0.3 %collective-permute-done.other_ref = bf16[4,16,4,256]{3,2,1,0:T(4,128)(2,1)S(1)} collective-permute-done((bf16[4,16,4,256]{3,2,1,0:T(4,128)(2,1)}, bf16[4,16,4,256]{3,2,1,0:T(4,128)(2,1)S(1)}, u32[]{:S(2)}, u32[]{:S(2)}) %collective-permute-start) | collective-permute-done | bytes 131104 | tf_op jit(solution)/shard_map/ppermute | solution.py:402
  1.9 0.0 copy-start
  1.9 0.0 copy-start.4
  1.9 0.0 copy-start.5
  1.9 0.5 %pack_edges.1 = bf16[592,128]{1,0:T(8,128)(2,1)S(1)} custom-call(bf16[4,16,4,256]{3,2,1,0:T(4,128)(2,1)S(1)} %get-tuple-element.34.own_ref, bf16[4,16,4,256]{3,2,1,0:T(4,128)(2,1)S(1)} %collective-permute-done.other_ref, bf16[32,4,256]{2,1,0:T(4,128)(2,1)S(1)} %get-tuple-element.32.ref_ref), custom_call_target="tpu_custom_call" | custom-call | tf_op jit(solution)/shard_map/pack_edges/pallas_call | solution.py:430
  2.4 4.0 %collective-permute-start.1 = (bf16[592,128]{1,0:T(8,128)(2,1)S(1)}, bf16[592,128]{1,0:T(8,128)(2,1)S(1)}, u32[]{:S(2)}, u32[]{:S(2)}) collective-permute-start(bf16[592,128]{1,0:T(8,128)(2,1)S(1)} %pack_edges.1), channel_id=1, source_target_pairs={{0,2},{2,4},{4,6},{6,8},{8,10},{10,12},{12,14},{14,16},{16,18},{18... | collective-permute-start | bytes 454664 | tf_op jit(solution)/shard_map/ppermute | solution.py:441
  6.4 0.0 copy-done
  6.4 0.1 collective-permute-start.2
  6.4 0.0 copy-done.4
  6.5 0.0 copy-done.5
  6.5 0.1 stack_reshape.7
  6.7 0.1 stack_reshape.6
  6.8 0.0 copy-start.1
  6.8 0.0 copy-start.2
  6.8 0.0 copy-start.3
  6.8 0.1 copy.17.taps_ref
  6.9 0.7 %collective-permute-done.2.before.after = s32[4,8]{1,0:T(4,128)S(1)} collective-permute-done((s32[4,8]{1,0:T(4,128)S(1)}, s32[4,8]{1,0:T(4,128)S(1)}, u32[]{:S(2)}, u32[]{:S(2)}) %collective-permute-start.2) | collective-permute-done | bytes 160 | tf_op jit(solution)/shard_map/ppermute | solution.py:402
  7.6 0.0 copy-done.1
  7.6 0.0 copy-done.2
  7.6 0.0 copy-done.3
  7.6 2.2 %inner_columns.1 = (bf16[4,256,128]{2,1,0:T(8,128)(2,1)S(1)}, bf16[256,128]{1,0:T(8,128)(2,1)S(1)}, s32[8,128]{1,0:T(8,128)S(1)}, f32[8,384]{1,0:T(8,128)S(1)}, ...) custom-call(s32[4,8]{1,0:T(4,128)S(1)} %copy-done, ...), custom_call_target="tpu_custom_call" | custom-call | flops 3000000000 | bytes 1000000 | tf_op jit(solution)/shard_map/inner_columns/pallas_call | solution.py:461
  9.8 0.0 collective-permute-done.1.got_ref
  9.8 1.8 %collective-permute-start.3 = (bf16[592,128]{1,0:T(8,128)(2,1)S(1)}, bf16[592,128]{1,0:T(8,128)(2,1)S(1)}, u32[]{:S(2)}, u32[]{:S(2)}) collective-permute-start(bf16[592,128]{1,0:T(8,128)(2,1)S(1)} %collective-permute-done.1.got_ref), channel_id=1, source_target_pairs={{0,1},{1,0},{2,3},{3,2},{4,5},{5,4},{6,7},{7,6},{8,9},{9,8},{10,11... | collective-permute-start | bytes 454664 | tf_op jit(solution)/shard_map/ppermute | solution.py:402
  11.6 1.3 %late_columns.1.late_ref = bf16[128,256]{1,0:T(8,128)(2,1)S(1)} custom-call(f32[552,384]{1,0:T(8,128)S(1)} %get-tuple-element.54.match, f32[552,384]{1,0:T(8,128)S(1)} %get-tuple-element.55.first, f32[8,384]{1,0:T(8,128)S(1)} %get-tuple-element.50.table_ref, bf16[512,256]{1,0:T(8,128)(2,1)S(1)} %get-tuple-element.51.spread_ref, ...), custom_call_target="tpu_custom_call" | custom-call | flops 2000000000 | bytes 1000000 | tf_op jit(solution)/shard_map/late_columns/pallas_call | solution.py:492
  12.9 0.0 collective-permute-done.3.swapped_ref
  12.9 3.8 %outer_columns.1 = bf16[8,8,4,256]{3,2,1,0:T(4,128)(2,1)} custom-call(bf16[4,256,128]{2,1,0:T(8,128)(2,1)S(1)} %get-tuple-element.47.cols_ref, bf16[256,128]{1,0:T(8,128)(2,1)S(1)} %get-tuple-element.48.ref_cols_ref, s32[8,128]{1,0:T(8,128)S(1)} %get-tuple-element.49.word_ref, f32[8,384]{1,0:T(8,128)S(1)} %get-tuple-element.50.table_ref, ...), custom_call_target="tpu_custom_call" | custom-call | tf_op jit(solution)/shard_map/outer_columns/pallas_call | solution.py:504
  (4 shorter events, 0.1 us)
Async XLA Ops:
  0.0 1.9 %collective-permute-start = (bf16[4,16,4,256]{3,2,1,0:T(4,128)(2,1)}, bf16[4,16,4,256]{3,2,1,0:T(4,128)(2,1)S(1)}, u32[]{:S(2)}, u32[]{:S(2)}) collective-permute-start(bf16[4,16,4,256]{3,2,1,0:T(4,128)(2,1)} %own_hbm.1), channel_id=1, source_target_pairs={{0,1},{1,0},{2,3},{3,2},{4,5},{5,4},{6,7},{7,6},{8,9},{9,8},{10,11... | collective-permute-start | bytes 393224 | tf_op jit(solution)/shard_map/ppermute | solution.py:402
  1.9 4.5 %copy-start = (s32[4,8]{1,0:T(4,128)S(1)}, s32[4,8]{1,0:T(4,128)}, u32[]{:S(2)}) copy-start(s32[4,8]{1,0:T(4,128)} %shifts) | copy-start | bytes 388
  1.9 4.6 %copy-start.4 = (bf16[8,8,3,3,3]{1,0,4,3,2:T(8,128)(2,1)S(1)}, bf16[8,8,3,3,3]{1,0,4,3,2:T(8,128)(2,1)}, u32[]{:S(2)}) copy-start(bf16[8,8,3,3,3]{1,0,4,3,2:T(8,128)(2,1)} %param.13) | copy-start | bytes 10372
  1.9 4.6 %copy-start.5 = (bf16[8,8,3,3,3]{1,0,4,3,2:T(8,128)(2,1)S(1)}, bf16[8,8,3,3,3]{1,0,4,3,2:T(8,128)(2,1)}, u32[]{:S(2)}) copy-start(bf16[8,8,3,3,3]{1,0,4,3,2:T(8,128)(2,1)} %param.11) | copy-start | bytes 10372
  2.4 7.4 %collective-permute-start.1 = (bf16[592,128]{1,0:T(8,128)(2,1)S(1)}, bf16[592,128]{1,0:T(8,128)(2,1)S(1)}, u32[]{:S(2)}, u32[]{:S(2)}) collective-permute-start(bf16[592,128]{1,0:T(8,128)(2,1)S(1)} %pack_edges.1), channel_id=1, source_target_pairs={{0,2},{2,4},{4,6},{6,8},{8,10},{10,12},{12,14},{14,16},{16,18},{18... | collective-permute-start | bytes 454664 | tf_op jit(solution)/shard_map/ppermute | solution.py:441
  6.4 1.2 %collective-permute-start.2 = (s32[4,8]{1,0:T(4,128)S(1)}, s32[4,8]{1,0:T(4,128)S(1)}, u32[]{:S(2)}, u32[]{:S(2)}) collective-permute-start(s32[4,8]{1,0:T(4,128)S(1)} %copy-done), channel_id=1, source_target_pairs={{0,1},{1,0},{2,3},{3,2},{4,5},{5,4},{6,7},{7,6},{8,9},{9,8},{10,11... | collective-permute-start | bytes 392 | tf_op jit(solution)/shard_map/ppermute | solution.py:402
  6.8 0.8 %copy-start.1 = (f32[8]{0:T(128)S(1)}, f32[8]{0:T(128)}, u32[]{:S(2)}) copy-start(f32[8]{0:T(128)} %bias_one.1) | copy-start | bytes 100
  6.8 0.8 %copy-start.2 = (f32[8]{0:T(128)S(1)}, f32[8]{0:T(128)}, u32[]{:S(2)}) copy-start(f32[8]{0:T(128)} %bias_two.1) | copy-start | bytes 100
  6.8 0.8 %copy-start.3 = (f32[8]{0:T(128)S(1)}, f32[8]{0:T(128)}, u32[]{:S(2)}) copy-start(f32[8]{0:T(128)} %view_head.1) | copy-start | bytes 100
  9.8 3.1 %collective-permute-start.3 = (bf16[592,128]{1,0:T(8,128)(2,1)S(1)}, bf16[592,128]{1,0:T(8,128)(2,1)S(1)}, u32[]{:S(2)}, u32[]{:S(2)}) collective-permute-start(bf16[592,128]{1,0:T(8,128)(2,1)S(1)} %collective-permute-done.1.got_ref), channel_id=1, source_target_pairs={{0,1},{1,0},{2,3},{3,2},{4,5},{5,4},{6,7},{7,6},{8,9},{9,8},{10,11... | collective-permute-start | bytes 454664 | tf_op jit(solution)/shard_map/ppermute | solution.py:402

commit v6 on v5

--- a/solution.py
+++ b/solution.py
@@ -7,7 +7,7 @@
 
 GROUPS = 8
 MAX_SHIFT = 128
-LEAD = MAX_SHIFT + 16
+LEAD = MAX_SHIFT + 8
 EDGE = 16
 BATCH = 2
 FAR = -3.0e38
@@ -77,71 +77,134 @@
     return jnp.where(role == 0, width - count, 0)
 
 
-def stage_body(own_hbm, ref_hbm, own_ref, ref_ref, sems):
+def stacked(pair, lanes):
+    return jnp.concatenate([pair[:, 0:lanes], pair[:, lanes:]], axis=0)
+
+
+def pack_own_body(own_hbm, ref_hbm, own_ref, ref_ref, part_ref, sems):
     copies = [
         pltpu.make_async_copy(own_hbm, own_ref, sems.at[0]),
         pltpu.make_async_copy(ref_hbm, ref_ref, sems.at[1]),
     ]
     for copy in copies:
         copy.start()
-    for copy in copies:
-        copy.wait()
-
-
-def pack_body(own_ref, other_ref, ref_ref, packet_ref):
-    width = own_ref.shape[3]
+    views, _, _, width = own_ref.shape
+    lanes = part_ref.shape[1]
+    role, order, *_ = position()
+    pick = columns_of(LEAD, width, edge_start(role, width, LEAD))
+    pick_ref = columns_of(EDGE, width, edge_start(role, width, EDGE))
+    copies[0].wait()
+    for i, pair in enumerate(turned_half(own_ref, pick, order)):
+        at = 2 * i * LEAD
+        part_ref[at : at + 2 * LEAD] = stacked(pair, lanes).astype(jnp.bfloat16)
+    copies[1].wait()
+    part_ref[views * LEAD :] = turned_ref(ref_ref, pick_ref).astype(jnp.bfloat16)
+
+
+def pack_other_body(part_ref, other_ref, packet_ref):
+    views, _, _, width = other_ref.shape
     lanes = packet_ref.shape[1]
     role, order, *_ = position()
     pick = columns_of(LEAD, width, edge_start(role, width, LEAD))
-    halves = zip(turned_half(own_ref, pick, order), turned_half(other_ref, pick, 1 - order))
-    for i, (low, high) in enumerate(halves):
-        pair = (low + high).astype(jnp.bfloat16)
-        for k in range(2):
-            at = (2 * i + k) * LEAD
-            packet_ref[at : at + LEAD] = pair[:, k * lanes : (k + 1) * lanes]
-    pick = columns_of(EDGE, width, edge_start(role, width, EDGE))
-    packet_ref[own_ref.shape[0] * LEAD :] = turned_ref(ref_ref, pick).astype(jnp.bfloat16)
+    for i, pair in enumerate(turned_half(other_ref, pick, 1 - order)):
+        at = 2 * i * LEAD
+        both = part_ref[at : at + 2 * LEAD].astype(jnp.float32) + stacked(pair, lanes)
+        packet_ref[at : at + 2 * LEAD] = both.astype(jnp.bfloat16)
+    packet_ref[views * LEAD :] = part_ref[views * LEAD :]
 
 
 def lane_table(values_ref, rows, lane):
-    which = (lane // rows) % GROUPS
+    which = lane // rows % GROUPS
     table = jnp.zeros(lane.shape, jnp.float32)
     for o in range(GROUPS):
         table = jnp.where(which == o, values_ref[o], table)
     return table
 
 
-def build_band(taps_ref, which, band_ref, rows):
+def base_blocks(taps_ref, which, rows, apart):
     block = GROUPS * rows
-    spread = iota((3 * GROUPS, 128), 1) // rows == iota((3 * GROUPS, 128), 0)
-    wide = dot(taps_ref[which], spread.astype(jnp.bfloat16)).astype(jnp.bfloat16)
+    slots = 128 // (4 * rows)
+    at, lane = iota((3 * GROUPS, 128), 0), iota((3 * GROUPS, 128), 1)
+    if apart:
+        spreads = [
+            (lane // (slots * rows) + t * 4 == at % GROUPS)
+            & ((lane // rows) % slots == at // GROUPS)
+            for t in range(2)
+        ]
+    else:
+        spreads = [lane // rows == at]
     stretch = (iota((block, GROUPS), 0) // rows == iota((block, GROUPS), 1)).astype(jnp.bfloat16)
+    gap = iota((block, 128), 0) % rows - iota((block, 128), 1) % rows + 1
+    found = []
+    for spread in spreads:
+        wide = dot(taps_ref[which], spread.astype(jnp.bfloat16)).astype(jnp.bfloat16)
+        for e in range(3):
+            base = jnp.zeros((block, 128), jnp.float32)
+            for b in range(3):
+                at = (b * 3 + e) * GROUPS
+                base = jnp.where(gap == b, dot(stretch, wide[at : at + GROUPS]), base)
+            found.append(base)
+    return [found[i : i + 3] for i in range(0, len(found), 3)]
+
+
+def band_rows(e, j, block):
+    per_tile = 128 // block
+    whole = 2 * per_tile
+    if j < whole:
+        return (e * whole + j) * block
+    return (3 * whole + 2 * e + j - whole) * block
+
+
+def build_band_one(taps_ref, band_ref, rest_ref, rows):
+    block = GROUPS * rows
     lane = iota((block, 128), 1)
-    gap = iota((block, 128), 0) % rows - lane % rows + 1
-    depth, out_lanes = band_ref.shape[0] // 3, band_ref.shape[1]
     per_tile = 128 // block
     zero = jnp.zeros((block, 128), jnp.bfloat16)
-    for e in range(3):
-        base = jnp.zeros((block, 128), jnp.float32)
-        for b in range(3):
-            at = (b * 3 + e) * GROUPS
-            base = jnp.where(gap == b, dot(stretch, wide[at : at + GROUPS]), base)
-        for j in range(depth // block):
-            offset = j - 2
-            first, turn = offset // per_tile, offset % per_tile
+    (bases,) = base_blocks(taps_ref, 0, rows, False)
+    for e, base in enumerate(bases):
+        low_parts, high_parts = [], []
+        for turn in range(per_tile):
             moved = pltpu.roll(base, turn * block, 1) if turn else base
-            for t in range(out_lanes // 128):
+            high_parts.append(jnp.where(lane >= turn * block, moved, 0.0).astype(jnp.bfloat16))
+            low_parts.append(jnp.where(lane < turn * block, moved, 0.0).astype(jnp.bfloat16))
+        for j in range(2 * per_tile + 2):
+            first, turn = (j - 2) // per_tile, (j - 2) % per_tile
+            at = band_rows(e, j, block)
+            for t in range(2):
+                part = zero
                 if t == first:
-                    part = jnp.where(lane >= turn * block, moved, 0.0).astype(jnp.bfloat16)
+                    part = high_parts[turn]
                 elif t == first + 1 and turn > per_tile - 3:
-                    part = jnp.where(lane < turn * block, moved, 0.0).astype(jnp.bfloat16)
-                else:
-                    part = zero
-                at = e * depth + j * block
+                    part = low_parts[turn]
                 band_ref[at : at + block, t * 128 : (t + 1) * 128] = part
-
-
-def build_tables(planes, rows, inner, bias_one, bias_two, view_head, ends, table_ref, spread_ref):
+                if t == 0 and j < per_tile:
+                    rest_ref[(e * per_tile + j) * block : (e * per_tile + j + 1) * block] = part
+    for j in range(2):
+        at = (3 * (2 * per_tile + 2) + j) * block
+        band_ref[at : at + block] = jnp.zeros((block, 256), jnp.bfloat16)
+
+
+def build_band_two(taps_ref, band_ref, rows):
+    block = GROUPS * rows
+    per_tile = 128 // block
+    slots = 2 * per_tile
+    plane = (iota((block, 128), 1) // rows) % slots
+    for t, bases in enumerate(base_blocks(taps_ref, 1, rows, True)):
+        for e, base in enumerate(bases):
+            for j in range(slots + 2):
+                turn = (j - 2) * rows % 128
+                moved = pltpu.roll(base, turn, 1) if turn else base
+                held = (plane >= j - 2) & (plane <= j)
+                at = band_rows(e, j, block)
+                band_ref[at : at + block, t * 128 : (t + 1) * 128] = jnp.where(
+                    held, moved, 0.0
+                ).astype(jnp.bfloat16)
+    for j in range(2):
+        at = (3 * (slots + 2) + j) * block
+        band_ref[at : at + block] = jnp.zeros((block, 256), jnp.bfloat16)
+
+
+def build_tables(planes, rows, inner, bias_one, bias_two, view_head, ends, table_ref, spread_ref, perm_ref):
     block = GROUPS * rows
     out_lanes = planes * block
     span = table_ref.shape[1]
@@ -152,12 +215,15 @@
     table_ref[0:1] = jnp.where(outside, 0.0, 1.0 / inner)
     outside = ((plane == 0) & is_first_plane) | ((plane == planes + 1) & is_last_plane)
     table_ref[1:2] = jnp.where(outside, FAR, lane_table(bias_one, rows, at))
-    table_ref[2:3] = lane_table(bias_two, rows, at)
-    table_ref[3:4] = lane_table(view_head, rows, at)
-    row, lane = iota((out_lanes, out_lanes), 0), iota((out_lanes, out_lanes), 1)
-    same = ((row // block == lane // block) & (row % rows == lane % rows)).astype(jnp.bfloat16)
-    spread_ref[0:out_lanes] = same
-    spread_ref[out_lanes:] = same
+    table_ref[2:3] = lane_table(bias_two, planes * rows, at)
+    table_ref[3:4] = lane_table(view_head, planes * rows, at)
+    row, lane = iota(spread_ref.shape, 0), iota(spread_ref.shape, 1)
+    same = (row // rows % planes == lane // block) & (row % rows == lane % rows)
+    spread_ref[...] = same.astype(jnp.bfloat16)
+    to = iota(perm_ref.shape, 0)
+    g, j, h = to // (planes * rows), (to // rows) % planes, to % rows
+    perm = (j * GROUPS + g) * rows + h == iota(perm_ref.shape, 1)
+    perm_ref[...] = perm.astype(jnp.bfloat16)
 
 
 def fill(pieces, near, src, wide, match, table_ref, block):
@@ -179,40 +245,47 @@
             match[at : at + count, q * 128 : (q + 1) * 128] = y
 
 
-def convolve_first(low, high, planes, block, match, first, table_ref, band_one):
+def three_taps(volume, low, high, out_lanes):
+    tile = volume.shape[1] - out_lanes
+    parts = [volume[low + e : high + e] for e in range(3)]
+    tails = [part[:, out_lanes:] for part in parts]
+    near = iota((high - low, tile), 1) < tile // 2
+    paired = jnp.where(near, tails[0], pltpu.roll(tails[1], tile // 2, 1))
+    sides = [part[:, 0:out_lanes] for part in parts] + [paired, tails[2]]
+    wide = jnp.concatenate([side.astype(jnp.bfloat16) for side in sides], axis=1)
+    return wide, jnp.concatenate([tail.astype(jnp.bfloat16) for tail in tails], axis=1)
+
+
+def convolve_first(low, high, planes, block, match, first, table_ref, band_one, rest_ref):
     out_lanes = planes * block
-    span = match.shape[1]
-    rest = span - out_lanes
-    moved = [match[low + e : high + e].astype(jnp.bfloat16) for e in range(3)]
-    raw = dot(jnp.concatenate(moved, axis=1), band_one[...])
-    raw = jnp.maximum(raw + table_ref[1:2, 0:out_lanes], 0.0)
-    first[low:high, 0:out_lanes] = raw
-    raw = sum(
-        dot(moved[e][:, out_lanes:], band_one[e * span : e * span + rest, 0:rest])
-        for e in range(3)
-    )
-    raw = jnp.maximum(raw + table_ref[1:2, out_lanes:], 0.0)
-    first[low:high, out_lanes:] = raw
+    wide, tails = three_taps(match, low, high, out_lanes)
+    raw = dot(wide, band_one[...])
+    first[low:high, 0:out_lanes] = jnp.maximum(raw + table_ref[1:2, 0:out_lanes], 0.0)
+    raw = dot(tails, rest_ref[...])
+    first[low:high, out_lanes:] = jnp.maximum(raw + table_ref[1:2, out_lanes:], 0.0)
 
 
 def weights(low, high, planes, block, first, table_ref, band_two, spread_ref):
     out_lanes = planes * block
-    moved = [first[low + e : high + e].astype(jnp.bfloat16) for e in range(3)]
-    second = dot(jnp.concatenate(moved, axis=1), band_two[...])
+    wide, _ = three_taps(first, low, high, out_lanes)
+    second = dot(wide, band_two[...])
     second = jnp.maximum(second + table_ref[2:3, 0:out_lanes], 0.0) * table_ref[3:4, 0:out_lanes]
+    half = out_lanes // 2
+    second = second[:, 0:half] + second[:, half:]
     upper = second.astype(jnp.bfloat16)
     under = (second - upper.astype(jnp.float32)).astype(jnp.bfloat16)
     score = dot(jnp.concatenate([upper, under], axis=1), spread_ref[...])
     return 1.0 / (1.0 + jnp.exp(-score))
 
 
-def first_stage(views, tall, planes, block, filled, mend, match, first, table_ref, band_one):
+def first_stage(
+    views, tall, planes, block, filled, mend, match, first, table_ref, band_one, rest_ref
+):
     for at in range(0, views, BATCH):
         for v in range(at, at + BATCH):
             filled(v)
-        convolve_first(
-            at * tall, (at + BATCH) * tall, planes, block, match, first, table_ref, band_one
-        )
+        low, high = at * tall, (at + BATCH) * tall
+        convolve_first(low, high, planes, block, match, first, table_ref, band_one, rest_ref)
         for v in range(at, at + BATCH):
             mend(v * tall)
 
@@ -262,7 +335,9 @@
     word_ref,
     table_ref,
     spread_ref,
+    perm_ref,
     band_one,
+    rest_ref,
     band_two,
     match,
     first,
@@ -292,10 +367,10 @@
             src[v, 8 : 8 + width] = part
             src[v, 8 + width :] = none
     build_tables(
-        planes, rows, inner, bias_one, bias_two, view_head, ends, table_ref, spread_ref
-    )
-    build_band(taps_ref, 0, band_one, rows)
-    build_band(taps_ref, 1, band_two, rows)
+        planes, rows, inner, bias_one, bias_two, view_head, ends, table_ref, spread_ref, perm_ref
+    )
+    build_band_one(taps_ref, band_one, rest_ref, rows)
+    build_band_two(taps_ref, band_two, rows)
     pack_shifts(shifts, before, after, word_ref)
     near = read_shifts(views, planes, word_ref)
     out_rows = width - MAX_SHIFT
@@ -309,7 +384,17 @@
         fill(pieces, near[v], src.at[v], wide, match, table_ref, block)
 
     first_stage(
-        views, tall, planes, block, filled, lambda row: None, match, first, table_ref, band_one
+        views,
+        tall,
+        planes,
+        block,
+        filled,
+        lambda row: None,
+        match,
+        first,
+        table_ref,
+        band_one,
+        rest_ref,
     )
     for ref in (match, first):
         ref[views * tall :] = jnp.zeros((8, match.shape[1]), jnp.float32)
@@ -331,7 +416,9 @@
     word_ref,
     table_ref,
     spread_ref,
+    perm_ref,
     band_one,
+    rest_ref,
     band_two,
     late_ref,
     got_ref,
@@ -351,10 +438,14 @@
     near = read_shifts(views, planes, word_ref)
     left = jnp.where(order == 0, got_ref[...], swapped_ref[...])
     right = jnp.where(order == 0, swapped_ref[...], got_ref[...])
-    for v in range(views):
-        src[v, 0:LEAD] = left[v * LEAD : (v + 1) * LEAD].astype(jnp.float32)
-        src[v, LEAD : LEAD + width] = cols_ref[v].astype(jnp.float32)
-        src[v, LEAD + width :] = right[v * LEAD : v * LEAD + EDGE].astype(jnp.float32)
+    for v in range(0, views, 2):
+        at = v * LEAD
+        pair = left[at : at + 2 * LEAD].astype(jnp.float32)
+        ends = right[at : at + LEAD + 24].astype(jnp.float32)
+        for k in range(2):
+            src[v + k, 0:LEAD] = pair[k * LEAD : (k + 1) * LEAD]
+            src[v + k, LEAD : LEAD + width] = cols_ref[v + k].astype(jnp.float32)
+            src[v + k, LEAD + width :] = ends[k * LEAD : k * LEAD + EDGE]
     wide[0:EDGE] = left[views * LEAD :].astype(jnp.float32)
     wide[EDGE : EDGE + width] = ref_cols_ref[...].astype(jnp.float32)
     wide[EDGE + width :] = right[views * LEAD : views * LEAD + EDGE].astype(jnp.float32)
@@ -374,7 +465,9 @@
         for at, at_end in ((row, is_first_tile), (row + main + 3, is_last_tile)):
             first[at : at + 1] = jnp.where(at_end, none, first[at : at + 1])
 
-    first_stage(views, tall, planes, block, filled, mend, match, first, table_ref, band_one)
+    first_stage(
+        views, tall, planes, block, filled, mend, match, first, table_ref, band_one, rest_ref
+    )
     part = second_stage(
         views, tall, planes, block, match, first, table_ref, band_two, spread_ref
     )
@@ -382,11 +475,7 @@
     joined[MAX_SHIFT:] = late_ref[...].astype(jnp.float32)
     joined[MAX_SHIFT : MAX_SHIFT + 2] = part[MAX_SHIFT : MAX_SHIFT + 2]
     joined[width - 2 :] = part[main : main + 2]
-    size = planes * block
-    to = iota((size, size), 0)
-    g, j, h = to // (planes * rows), (to // rows) % planes, to % rows
-    perm = ((j * groups + g) * rows + h == iota((size, size), 1)).astype(jnp.bfloat16)
-    turned = dot_nt(perm, joined[...].astype(jnp.bfloat16)).astype(jnp.bfloat16)
+    turned = dot_nt(perm_ref[...], joined[...].astype(jnp.bfloat16)).astype(jnp.bfloat16)
     out_ref[...] = turned.reshape(groups, planes, rows, width)
 
 
@@ -418,23 +507,23 @@
         own, other = full[:, :half], full[:, half:]
 
     packet_shape = shape((views * LEAD + EDGE, lanes), bf16)
-    own, ref_feat = pl.pallas_call(
-        stage_body,
-        out_shape=[shape(own.shape, bf16), shape(ref_feat.shape, bf16)],
+    own, ref_feat, part = pl.pallas_call(
+        pack_own_body,
+        out_shape=[shape(own.shape, bf16), shape(ref_feat.shape, bf16), packet_shape],
         in_specs=[whole(pltpu.HBM)] * 2,
-        out_specs=[whole(vmem)] * 2,
+        out_specs=[whole(vmem)] * 3,
         scratch_shapes=[pltpu.SemaphoreType.DMA((2,))],
         compiler_params=limit(8),
-        name="stage",
+        name="pack_own",
     )(*(pltpu.with_memory_space_constraint(x, pltpu.HBM) for x in (own, ref_feat)))
     packet = pl.pallas_call(
-        pack_body,
+        pack_other_body,
         out_shape=packet_shape,
-        in_specs=[whole(vmem)] * 3,
+        in_specs=[whole(vmem)] * 2,
         out_specs=whole(vmem),
         compiler_params=limit(8),
-        name="pack_edges",
-    )(own, other, ref_feat)
+        name="pack_other",
+    )(part, other)
 
     pairs = [(sides * i, sides * (i + 1)) for i in range(tiles - 1)]
     pairs += [(sides * (i + 1) + 1, sides * i + 1) for i in range(tiles - 1)]
@@ -465,14 +554,16 @@
             shape((width, lanes), bf16),
             shape((8, 128), jnp.int32),
             shape((8, span), f32),
-            shape((2 * out_lanes, out_lanes), bf16),
-            shape((3 * span, out_lanes), bf16),
-            shape((3 * span, out_lanes), bf16),
+            shape((256, out_lanes), bf16),
+            shape((out_lanes, out_lanes), bf16),
+            shape((4 * out_lanes, out_lanes), bf16),
+            shape((3 * (span - out_lanes), span - out_lanes), bf16),
+            shape((4 * out_lanes, out_lanes), bf16),
             shape((high, span), f32),
             shape((high, span), f32),
         ],
         in_specs=[whole(vmem)] * 10,
-        out_specs=[whole(vmem)] * 9,
+        out_specs=[whole(vmem)] * 11,
         scratch_shapes=[
             pltpu.VMEM((views, width + 16, lanes), f32),
             pltpu.VMEM((width + 8, lanes), f32),
@@ -499,12 +590,12 @@
             flops=2 * 10**9, bytes_accessed=10**6, transcendentals=10**5
         ),
         name="late_columns",
-    )(match, first, inner[3], inner[4], inner[6])
+    )(match, first, inner[3], inner[4], inner[8])
     high = views * (MAX_SHIFT + 16) + 8
     return pl.pallas_call(
         outer_body,
         out_shape=shape((GROUPS, planes, rows, width), bf16),
-        in_specs=[whole(vmem)] * 10,
+        in_specs=[whole(vmem)] * 12,
         out_specs=whole(vmem),
         scratch_shapes=[
             pltpu.VMEM((views, LEAD + width + EDGE, lanes), f32),

time: 16.9 us -> 16.2 us (0.959)
  starting transfers between devices: 6.53 us -> 6.08 us
  waiting for transfers between devices: 0.93 us -> 0.67 us
    pallas_call x2, Pallas kernels: 1.43 us -> 1.94 us  [the longest x1 1.57 us: per_device(): pl.pallas_call(pack_own_body, out_shape=[shape(own.shape, bf16), shape(re...]
    ppermute x3, starting transfers between devices: 2.57 us -> 2.12 us  [swap_planes(): return lax.ppermute(value, 'plane', [(0, 1), (1, 0)])]
    pallas_call x1, Pallas kernels: 3.76 us -> 3.37 us  [per_device(): pl.pallas_call(outer_body, out_shape=shape((GROUPS, planes, rows, width),...]
    pallas_call x1, Pallas kernels: 1.3 us -> 1.03 us  [per_device(): pl.pallas_call(late_body, out_shape=shape((late_rows, out_lanes), bf16),...]
    ppermute x3, waiting for transfers between devices: 0.93 us -> 0.66 us  [swap_planes(): return lax.ppermute(value, 'plane', [(0, 1), (1, 0)])]
  transfers between devices with their start and end apart: 4 -> 4, of which waited for: 2 -> 1; matrix products, arithmetic and copies ran while one was open for 2% -> 2% of each run, Pallas kernels for 26% -> 31%
where the time goes in v6:
time: 16.2 us; the launch traced here: 16 us
  Pallas kernels  8.65 us (53%)
  starting transfers between devices  6.08 us (38%)
  waiting for transfers between devices  0.67 us (4%)
  local copies, waits for them, and re-layouts  0.42 us (3%)
  between operations  0.17 us (1%)
    ppermute x1, starting transfers between devices, per_device(): got = lax.ppermute(packet, ('tile', 'plane'), pairs)  3.96 us
    pallas_call x1, Pallas kernels, per_device(): pl.pallas_call(outer_body, out_shape=shape((GROUPS, planes, rows, width),...  3.37 us
    pallas_call x1, Pallas kernels, per_device(): pl.pallas_call(inner_body, out_shape=[shape((views, width, lanes), bf16),...  2.3 us
    ppermute x3, starting transfers between devices, swap_planes(): return lax.ppermute(value, 'plane', [(0, 1), (1, 0)])  2.12 us
    pallas_call x1, Pallas kernels, per_device(): pl.pallas_call(pack_own_body, out_shape=[shape(own.shape, bf16), shape(re...  1.57 us
    pallas_call x1, Pallas kernels, per_device(): pl.pallas_call(late_body, out_shape=shape((late_rows, out_lanes), bf16),...  1.03 us
    ppermute x3, waiting for transfers between devices, swap_planes(): return lax.ppermute(value, 'plane', [(0, 1), (1, 0)])  0.66 us
    pallas_call x1, Pallas kernels, per_device(): pl.pallas_call(pack_other_body, out_shape=packet_shape, in_specs=[whole(v...  0.37 us
  transfers between devices with their start and end apart: 4, of which 1 were waited for; matrix products, arithmetic and copies ran while one was open for 2% of the time, Pallas kernels for 31%

profile of v6, /device:TPU:25, one launch (start us, length us, event | category | flops | bytes accessed | tf_op | source)
XLA Modules:
  0.0 16.0 jit_solution(12352580077042154257)
XLA Ops:
  0.0 0.7 %collective-permute-start = (bf16[4,16,4,256]{3,2,1,0:T(4,128)(2,1)}, bf16[4,16,4,256]{3,2,1,0:T(4,128)(2,1)S(1)}, u32[]{:S(2)}, u32[]{:S(2)}) collective-permute-start(bf16[4,16,4,256]{3,2,1,0:T(4,128)(2,1)} %own_hbm.1), channel_id=1, source_target_pairs={{0,1},{1,0},{2,3},{3,2},{4,5},{5,4},{6,7},{7,6},{8,9},{9,8},{10,11... | collective-permute-start | bytes 393224 | tf_op jit(solution)/shard_map/ppermute | solution.py:491
  0.7 1.6 %pack_own.1 = (bf16[4,16,4,256]{3,2,1,0:T(4,128)(2,1)S(1)}, bf16[32,4,256]{2,1,0:T(4,128)(2,1)S(1)}, bf16[560,128]{1,0:T(8,128)(2,1)S(1)}) custom-call(bf16[4,16,4,256]{3,2,1,0:T(4,128)(2,1)} %own_hbm.1, bf16[32,4,256]{2,1,0:T(4,128)(2,1)} %ref_hbm.1), custom_call_target="tpu_custom_call" | custom-call | tf_op jit(solution)/shard_map/pack_own/pallas_call | solution.py:510
  2.3 0.0 collective-permute-done.other_ref
  2.3 0.0 copy-start
  2.3 0.0 copy-start.4
  2.3 0.0 copy-start.5
  2.3 0.4 %pack_other.1 = bf16[560,128]{1,0:T(8,128)(2,1)S(1)} custom-call(bf16[560,128]{1,0:T(8,128)(2,1)S(1)} %get-tuple-element.36.part_ref, bf16[4,16,4,256]{3,2,1,0:T(4,128)(2,1)S(1)} %collective-permute-done.other_ref), custom_call_target="tpu_custom_call" | custom-call | tf_op jit(solution)/shard_map/pack_other/pallas_call | solution.py:519
  2.7 4.0 %collective-permute-start.1 = (bf16[560,128]{1,0:T(8,128)(2,1)S(1)}, bf16[560,128]{1,0:T(8,128)(2,1)S(1)}, u32[]{:S(2)}, u32[]{:S(2)}) collective-permute-start(bf16[560,128]{1,0:T(8,128)(2,1)S(1)} %pack_other.1), channel_id=1, source_target_pairs={{0,2},{2,4},{4,6},{6,8},{8,10},{10,12},{12,14},{14,16},{16,18},{18... | collective-permute-start | bytes 430088 | tf_op jit(solution)/shard_map/ppermute | solution.py:530
  6.6 0.0 copy-done
  6.7 0.1 collective-permute-start.2
  6.7 0.0 copy-done.4
  6.7 0.0 copy-done.5
  6.8 0.1 stack_reshape.7
  7.0 0.1 stack_reshape.6
  7.1 0.1 copy.17.taps_ref
  7.2 0.0 copy-start.1
  7.2 0.0 copy-start.2
  7.2 0.0 copy-start.3
  7.2 0.7 %collective-permute-done.2.before.after = s32[4,8]{1,0:T(4,128)S(1)} collective-permute-done((s32[4,8]{1,0:T(4,128)S(1)}, s32[4,8]{1,0:T(4,128)S(1)}, u32[]{:S(2)}, u32[]{:S(2)}) %collective-permute-start.2) | collective-permute-done | bytes 160 | tf_op jit(solution)/shard_map/ppermute | solution.py:491
  7.9 0.0 copy-done.1
  7.9 0.0 copy-done.2
  7.9 0.0 copy-done.3
  7.9 2.3 %inner_columns.1 = (bf16[4,256,128]{2,1,0:T(8,128)(2,1)S(1)}, bf16[256,128]{1,0:T(8,128)(2,1)S(1)}, s32[8,128]{1,0:T(8,128)S(1)}, f32[8,384]{1,0:T(8,128)S(1)}, ...) custom-call(s32[4,8]{1,0:T(4,128)S(1)} %copy-done, ...), custom_call_target="tpu_custom_call" | custom-call | flops 3000000000 | bytes 1000000 | tf_op jit(solution)/shard_map/inner_columns/pallas_call | solution.py:550
  10.2 0.0 collective-permute-done.1.got_ref
  10.2 1.4 %collective-permute-start.3 = (bf16[560,128]{1,0:T(8,128)(2,1)S(1)}, bf16[560,128]{1,0:T(8,128)(2,1)S(1)}, u32[]{:S(2)}, u32[]{:S(2)}) collective-permute-start(bf16[560,128]{1,0:T(8,128)(2,1)S(1)} %collective-permute-done.1.got_ref), channel_id=1, source_target_pairs={{0,1},{1,0},{2,3},{3,2},{4,5},{5,4},{6,7},{7,6},{8,9},{9,8},{10,11... | collective-permute-start | bytes 430088 | tf_op jit(solution)/shard_map/ppermute | solution.py:491
  11.6 1.0 %late_columns.1.late_ref = bf16[128,256]{1,0:T(8,128)(2,1)S(1)} custom-call(f32[552,384]{1,0:T(8,128)S(1)} %get-tuple-element.64.match, f32[552,384]{1,0:T(8,128)S(1)} %get-tuple-element.65.first, f32[8,384]{1,0:T(8,128)S(1)} %get-tuple-element.58.table_ref, bf16[256,256]{1,0:T(8,128)(2,1)S(1)} %get-tuple-element.59.spread_ref, ...), custom_call_target="tpu_custom_call" | custom-call | flops 2000000000 | bytes 1000000 | tf_op jit(solution)/shard_map/late_columns/pallas_call | solution.py:583
  12.6 0.0 collective-permute-done.3.swapped_ref
  12.6 3.4 %outer_columns.1 = bf16[8,8,4,256]{3,2,1,0:T(4,128)(2,1)} custom-call(bf16[4,256,128]{2,1,0:T(8,128)(2,1)S(1)} %get-tuple-element.55.cols_ref, bf16[256,128]{1,0:T(8,128)(2,1)S(1)} %get-tuple-element.56.ref_cols_ref, s32[8,128]{1,0:T(8,128)S(1)} %get-tuple-element.57.word_ref, f32[8,384]{1,0:T(8,128)S(1)} %get-tuple-element.58.table_ref, ...), custom_call_target="tpu_custom_call" | custom-call | tf_op jit(solution)/shard_map/outer_columns/pallas_call | solution.py:595
  (4 shorter events, 0.1 us)
Async XLA Ops:
  0.0 2.3 %collective-permute-start = (bf16[4,16,4,256]{3,2,1,0:T(4,128)(2,1)}, bf16[4,16,4,256]{3,2,1,0:T(4,128)(2,1)S(1)}, u32[]{:S(2)}, u32[]{:S(2)}) collective-permute-start(bf16[4,16,4,256]{3,2,1,0:T(4,128)(2,1)} %own_hbm.1), channel_id=1, source_target_pairs={{0,1},{1,0},{2,3},{3,2},{4,5},{5,4},{6,7},{7,6},{8,9},{9,8},{10,11... | collective-permute-start | bytes 393224 | tf_op jit(solution)/shard_map/ppermute | solution.py:491
  2.3 4.4 %copy-start = (s32[4,8]{1,0:T(4,128)S(1)}, s32[4,8]{1,0:T(4,128)}, u32[]{:S(2)}) copy-start(s32[4,8]{1,0:T(4,128)} %shifts) | copy-start | bytes 388
  2.3 4.5 %copy-start.4 = (bf16[8,8,3,3,3]{1,0,4,3,2:T(8,128)(2,1)S(1)}, bf16[8,8,3,3,3]{1,0,4,3,2:T(8,128)(2,1)}, u32[]{:S(2)}) copy-start(bf16[8,8,3,3,3]{1,0,4,3,2:T(8,128)(2,1)} %param.13) | copy-start | bytes 10372
  2.3 4.5 %copy-start.5 = (bf16[8,8,3,3,3]{1,0,4,3,2:T(8,128)(2,1)S(1)}, bf16[8,8,3,3,3]{1,0,4,3,2:T(8,128)(2,1)}, u32[]{:S(2)}) copy-start(bf16[8,8,3,3,3]{1,0,4,3,2:T(8,128)(2,1)} %param.11) | copy-start | bytes 10372
  2.7 7.5 %collective-permute-start.1 = (bf16[560,128]{1,0:T(8,128)(2,1)S(1)}, bf16[560,128]{1,0:T(8,128)(2,1)S(1)}, u32[]{:S(2)}, u32[]{:S(2)}) collective-permute-start(bf16[560,128]{1,0:T(8,128)(2,1)S(1)} %pack_other.1), channel_id=1, source_target_pairs={{0,2},{2,4},{4,6},{6,8},{8,10},{10,12},{12,14},{14,16},{16,18},{18... | collective-permute-start | bytes 430088 | tf_op jit(solution)/shard_map/ppermute | solution.py:530
  6.7 1.2 %collective-permute-start.2 = (s32[4,8]{1,0:T(4,128)S(1)}, s32[4,8]{1,0:T(4,128)S(1)}, u32[]{:S(2)}, u32[]{:S(2)}) collective-permute-start(s32[4,8]{1,0:T(4,128)S(1)} %copy-done), channel_id=1, source_target_pairs={{0,1},{1,0},{2,3},{3,2},{4,5},{5,4},{6,7},{7,6},{8,9},{9,8},{10,11... | collective-permute-start | bytes 392 | tf_op jit(solution)/shard_map/ppermute | solution.py:491
  7.2 0.7 %copy-start.1 = (f32[8]{0:T(128)S(1)}, f32[8]{0:T(128)}, u32[]{:S(2)}) copy-start(f32[8]{0:T(128)} %bias_one.1) | copy-start | bytes 100
  7.2 0.7 %copy-start.2 = (f32[8]{0:T(128)S(1)}, f32[8]{0:T(128)}, u32[]{:S(2)}) copy-start(f32[8]{0:T(128)} %bias_two.1) | copy-start | bytes 100
  7.2 0.7 %copy-start.3 = (f32[8]{0:T(128)S(1)}, f32[8]{0:T(128)}, u32[]{:S(2)}) copy-start(f32[8]{0:T(128)} %view_head.1) | copy-start | bytes 100
  10.2 2.4 %collective-permute-start.3 = (bf16[560,128]{1,0:T(8,128)(2,1)S(1)}, bf16[560,128]{1,0:T(8,128)(2,1)S(1)}, u32[]{:S(2)}, u32[]{:S(2)}) collective-permute-start(bf16[560,128]{1,0:T(8,128)(2,1)S(1)} %collective-permute-done.1.got_ref), channel_id=1, source_target_pairs={{0,1},{1,0},{2,3},{3,2},{4,5},{5,4},{6,7},{7,6},{8,9},{9,8},{10,11... | collective-permute-start | bytes 430088 | tf_op jit(solution)/shard_map/ppermute | solution.py:491

commit v7 on v6

--- a/solution.py
+++ b/solution.py
@@ -438,6 +438,8 @@
     near = read_shifts(views, planes, word_ref)
     left = jnp.where(order == 0, got_ref[...], swapped_ref[...])
     right = jnp.where(order == 0, swapped_ref[...], got_ref[...])
+    left = jnp.where(is_first_tile, jnp.zeros_like(left), left)
+    right = jnp.where(is_last_tile, jnp.zeros_like(right), right)
     for v in range(0, views, 2):
         at = v * LEAD
         pair = left[at : at + 2 * LEAD].astype(jnp.float32)
@@ -527,6 +529,7 @@
 
     pairs = [(sides * i, sides * (i + 1)) for i in range(tiles - 1)]
     pairs += [(sides * (i + 1) + 1, sides * i + 1) for i in range(tiles - 1)]
+    pairs += [(sides * (tiles - 1), sides * (tiles - 1) + 1), (1, 0)]
     got = lax.ppermute(packet, ("tile", "plane"), pairs)
 
     own, other, shifts, conv_one, conv_two, packet = lax.optimization_barrier(

time: 16.2 us -> 14.3 us (0.88)
  starting transfers between devices: 6.08 us -> 4.26 us
    ppermute x1, starting transfers between devices: 3.96 us -> 2.11 us  [per_device(): got = lax.ppermute(packet, ('tile', 'plane'), pairs)]
  transfers between devices with their start and end apart: 4 -> 4, of which waited for: 1 -> 1; matrix products, arithmetic and copies ran while one was open for 2% -> 3% of each run, Pallas kernels for 31% -> 35%
where the time goes in v7:
time: 14.3 us; the launch traced here: 14.2 us
  Pallas kernels  8.67 us (61%)
  starting transfers between devices  4.26 us (30%)
  waiting for transfers between devices  0.68 us (5%)
  local copies, waits for them, and re-layouts  0.42 us (3%)
  between operations  0.15 us (1%)
    pallas_call x1, Pallas kernels, per_device(): pl.pallas_call(outer_body, out_shape=shape((GROUPS, planes, rows, width),...  3.39 us
    pallas_call x1, Pallas kernels, per_device(): pl.pallas_call(inner_body, out_shape=[shape((views, width, lanes), bf16),...  2.3 us
    ppermute x3, starting transfers between devices, swap_planes(): return lax.ppermute(value, 'plane', [(0, 1), (1, 0)])  2.15 us
    ppermute x1, starting transfers between devices, per_device(): got = lax.ppermute(packet, ('tile', 'plane'), pairs)  2.11 us
    pallas_call x1, Pallas kernels, per_device(): pl.pallas_call(pack_own_body, out_shape=[shape(own.shape, bf16), shape(re...  1.57 us
    pallas_call x1, Pallas kernels, per_device(): pl.pallas_call(late_body, out_shape=shape((late_rows, out_lanes), bf16),...  1.03 us
    ppermute x3, waiting for transfers between devices, swap_planes(): return lax.ppermute(value, 'plane', [(0, 1), (1, 0)])  0.68 us
    pallas_call x1, Pallas kernels, per_device(): pl.pallas_call(pack_other_body, out_shape=packet_shape, in_specs=[whole(v...  0.37 us
  transfers between devices with their start and end apart: 4, of which 1 were waited for; matrix products, arithmetic and copies ran while one was open for 3% of the time, Pallas kernels for 35%

profile of v7, /device:TPU:25, one launch (start us, length us, event | category | flops | bytes accessed | tf_op | source)
XLA Modules:
  0.0 14.2 jit_solution(2629196976022976375)
XLA Ops:
  0.0 0.7 %collective-permute-start = (bf16[4,16,4,256]{3,2,1,0:T(4,128)(2,1)}, bf16[4,16,4,256]{3,2,1,0:T(4,128)(2,1)S(1)}, u32[]{:S(2)}, u32[]{:S(2)}) collective-permute-start(bf16[4,16,4,256]{3,2,1,0:T(4,128)(2,1)} %own_hbm.1), channel_id=1, source_target_pairs={{0,1},{1,0},{2,3},{3,2},{4,5},{5,4},{6,7},{7,6},{8,9},{9,8},{10,11... | collective-permute-start | bytes 393224 | tf_op jit(solution)/shard_map/ppermute | solution.py:493
  0.7 1.6 %pack_own.1 = (bf16[4,16,4,256]{3,2,1,0:T(4,128)(2,1)S(1)}, bf16[32,4,256]{2,1,0:T(4,128)(2,1)S(1)}, bf16[560,128]{1,0:T(8,128)(2,1)S(1)}) custom-call(bf16[4,16,4,256]{3,2,1,0:T(4,128)(2,1)} %own_hbm.1, bf16[32,4,256]{2,1,0:T(4,128)(2,1)} %ref_hbm.1), custom_call_target="tpu_custom_call" | custom-call | tf_op jit(solution)/shard_map/pack_own/pallas_call | solution.py:512
  2.3 0.0 collective-permute-done.other_ref
  2.3 0.0 copy-start
  2.3 0.0 copy-start.4
  2.3 0.0 copy-start.5
  2.3 0.4 %pack_other.1 = bf16[560,128]{1,0:T(8,128)(2,1)S(1)} custom-call(bf16[560,128]{1,0:T(8,128)(2,1)S(1)} %get-tuple-element.36.part_ref, bf16[4,16,4,256]{3,2,1,0:T(4,128)(2,1)S(1)} %collective-permute-done.other_ref), custom_call_target="tpu_custom_call" | custom-call | tf_op jit(solution)/shard_map/pack_other/pallas_call | solution.py:521
  2.7 2.1 %collective-permute-start.1 = (bf16[560,128]{1,0:T(8,128)(2,1)S(1)}, bf16[560,128]{1,0:T(8,128)(2,1)S(1)}, u32[]{:S(2)}, u32[]{:S(2)}) collective-permute-start(bf16[560,128]{1,0:T(8,128)(2,1)S(1)} %pack_other.1), channel_id=1, source_target_pairs={{0,2},{2,4},{4,6},{6,8},{8,10},{10,12},{12,14},{14,16},{16,18},{18... | collective-permute-start | bytes 430088 | tf_op jit(solution)/shard_map/ppermute | solution.py:533
  4.8 0.0 copy-done
  4.8 0.0 collective-permute-start.2
  4.8 0.0 copy-done.4
  4.8 0.0 copy-done.5
  4.9 0.1 stack_reshape.7
  5.0 0.1 stack_reshape.6
  5.1 0.1 copy.17.taps_ref
  5.2 0.0 copy-start.1
  5.2 0.0 copy-start.2
  5.3 0.0 copy-start.3
  5.3 0.7 %collective-permute-done.2.before.after = s32[4,8]{1,0:T(4,128)S(1)} collective-permute-done((s32[4,8]{1,0:T(4,128)S(1)}, s32[4,8]{1,0:T(4,128)S(1)}, u32[]{:S(2)}, u32[]{:S(2)}) %collective-permute-start.2) | collective-permute-done | bytes 160 | tf_op jit(solution)/shard_map/ppermute | solution.py:493
  5.9 0.0 copy-done.1
  5.9 0.0 copy-done.2
  6.0 0.0 copy-done.3
  6.0 2.3 %inner_columns.1 = (bf16[4,256,128]{2,1,0:T(8,128)(2,1)S(1)}, bf16[256,128]{1,0:T(8,128)(2,1)S(1)}, s32[8,128]{1,0:T(8,128)S(1)}, f32[8,384]{1,0:T(8,128)S(1)}, ...) custom-call(s32[4,8]{1,0:T(4,128)S(1)} %copy-done, ...), custom_call_target="tpu_custom_call" | custom-call | flops 3000000000 | bytes 1000000 | tf_op jit(solution)/shard_map/inner_columns/pallas_call | solution.py:553
  8.3 0.0 collective-permute-done.1.got_ref
  8.3 1.5 %collective-permute-start.3 = (bf16[560,128]{1,0:T(8,128)(2,1)S(1)}, bf16[560,128]{1,0:T(8,128)(2,1)S(1)}, u32[]{:S(2)}, u32[]{:S(2)}) collective-permute-start(bf16[560,128]{1,0:T(8,128)(2,1)S(1)} %collective-permute-done.1.got_ref), channel_id=1, source_target_pairs={{0,1},{1,0},{2,3},{3,2},{4,5},{5,4},{6,7},{7,6},{8,9},{9,8},{10,11... | collective-permute-start | bytes 430088 | tf_op jit(solution)/shard_map/ppermute | solution.py:493
  9.7 1.0 %late_columns.1.late_ref = bf16[128,256]{1,0:T(8,128)(2,1)S(1)} custom-call(f32[552,384]{1,0:T(8,128)S(1)} %get-tuple-element.64.match, f32[552,384]{1,0:T(8,128)S(1)} %get-tuple-element.65.first, f32[8,384]{1,0:T(8,128)S(1)} %get-tuple-element.58.table_ref, bf16[256,256]{1,0:T(8,128)(2,1)S(1)} %get-tuple-element.59.spread_ref, ...), custom_call_target="tpu_custom_call" | custom-call | flops 2000000000 | bytes 1000000 | tf_op jit(solution)/shard_map/late_columns/pallas_call | solution.py:586
  10.8 0.0 collective-permute-done.3.swapped_ref
  10.8 3.4 %outer_columns.1 = bf16[8,8,4,256]{3,2,1,0:T(4,128)(2,1)} custom-call(bf16[4,256,128]{2,1,0:T(8,128)(2,1)S(1)} %get-tuple-element.55.cols_ref, bf16[256,128]{1,0:T(8,128)(2,1)S(1)} %get-tuple-element.56.ref_cols_ref, s32[8,128]{1,0:T(8,128)S(1)} %get-tuple-element.57.word_ref, f32[8,384]{1,0:T(8,128)S(1)} %get-tuple-element.58.table_ref, ...), custom_call_target="tpu_custom_call" | custom-call | tf_op jit(solution)/shard_map/outer_columns/pallas_call | solution.py:598
  (4 shorter events, 0.1 us)
Async XLA Ops:
  0.0 2.3 %collective-permute-start = (bf16[4,16,4,256]{3,2,1,0:T(4,128)(2,1)}, bf16[4,16,4,256]{3,2,1,0:T(4,128)(2,1)S(1)}, u32[]{:S(2)}, u32[]{:S(2)}) collective-permute-start(bf16[4,16,4,256]{3,2,1,0:T(4,128)(2,1)} %own_hbm.1), channel_id=1, source_target_pairs={{0,1},{1,0},{2,3},{3,2},{4,5},{5,4},{6,7},{7,6},{8,9},{9,8},{10,11... | collective-permute-start | bytes 393224 | tf_op jit(solution)/shard_map/ppermute | solution.py:493
  2.3 2.5 %copy-start = (s32[4,8]{1,0:T(4,128)S(1)}, s32[4,8]{1,0:T(4,128)}, u32[]{:S(2)}) copy-start(s32[4,8]{1,0:T(4,128)} %shifts) | copy-start | bytes 388
  2.3 2.5 %copy-start.4 = (bf16[8,8,3,3,3]{1,0,4,3,2:T(8,128)(2,1)S(1)}, bf16[8,8,3,3,3]{1,0,4,3,2:T(8,128)(2,1)}, u32[]{:S(2)}) copy-start(bf16[8,8,3,3,3]{1,0,4,3,2:T(8,128)(2,1)} %param.13) | copy-start | bytes 10372
  2.3 2.5 %copy-start.5 = (bf16[8,8,3,3,3]{1,0,4,3,2:T(8,128)(2,1)S(1)}, bf16[8,8,3,3,3]{1,0,4,3,2:T(8,128)(2,1)}, u32[]{:S(2)}) copy-start(bf16[8,8,3,3,3]{1,0,4,3,2:T(8,128)(2,1)} %param.11) | copy-start | bytes 10372
  2.7 5.6 %collective-permute-start.1 = (bf16[560,128]{1,0:T(8,128)(2,1)S(1)}, bf16[560,128]{1,0:T(8,128)(2,1)S(1)}, u32[]{:S(2)}, u32[]{:S(2)}) collective-permute-start(bf16[560,128]{1,0:T(8,128)(2,1)S(1)} %pack_other.1), channel_id=1, source_target_pairs={{0,2},{2,4},{4,6},{6,8},{8,10},{10,12},{12,14},{14,16},{16,18},{18... | collective-permute-start | bytes 430088 | tf_op jit(solution)/shard_map/ppermute | solution.py:533
  4.8 1.2 %collective-permute-start.2 = (s32[4,8]{1,0:T(4,128)S(1)}, s32[4,8]{1,0:T(4,128)S(1)}, u32[]{:S(2)}, u32[]{:S(2)}) collective-permute-start(s32[4,8]{1,0:T(4,128)S(1)} %copy-done), channel_id=1, source_target_pairs={{0,1},{1,0},{2,3},{3,2},{4,5},{5,4},{6,7},{7,6},{8,9},{9,8},{10,11... | collective-permute-start | bytes 392 | tf_op jit(solution)/shard_map/ppermute | solution.py:493
  5.2 0.7 %copy-start.1 = (f32[8]{0:T(128)S(1)}, f32[8]{0:T(128)}, u32[]{:S(2)}) copy-start(f32[8]{0:T(128)} %bias_one.1) | copy-start | bytes 100
  5.2 0.7 %copy-start.2 = (f32[8]{0:T(128)S(1)}, f32[8]{0:T(128)}, u32[]{:S(2)}) copy-start(f32[8]{0:T(128)} %bias_two.1) | copy-start | bytes 100
  5.3 0.7 %copy-start.3 = (f32[8]{0:T(128)S(1)}, f32[8]{0:T(128)}, u32[]{:S(2)}) copy-start(f32[8]{0:T(128)} %view_head.1) | copy-start | bytes 100
  8.3 2.5 %collective-permute-start.3 = (bf16[560,128]{1,0:T(8,128)(2,1)S(1)}, bf16[560,128]{1,0:T(8,128)(2,1)S(1)}, u32[]{:S(2)}, u32[]{:S(2)}) collective-permute-start(bf16[560,128]{1,0:T(8,128)(2,1)S(1)} %collective-permute-done.1.got_ref), channel_id=1, source_target_pairs={{0,1},{1,0},{2,3},{3,2},{4,5},{5,4},{6,7},{7,6},{8,9},{9,8},{10,11... | collective-permute-start | bytes 430088 | tf_op jit(solution)/shard_map/ppermute | solution.py:493

commit v8 on v7

--- a/solution.py
+++ b/solution.py
@@ -57,12 +57,11 @@
     return ((g * (lanes // (GROUPS * rows)) + k) * rows + h == at).astype(jnp.bfloat16)
 
 
-def turned_half(half_ref, pick, side):
+def turned_half(half_ref, pick, order):
     views, half, rows, width = half_ref.shape
     lanes = 2 * half * rows
     block = half_ref[...].reshape(views * half * rows, width)
     columns = dot_nt(pick, block).astype(jnp.bfloat16)
-    order = lane_order(half, rows, side)
     return [dot(columns[:, i : i + lanes], order) for i in range(0, columns.shape[1], lanes)]
 
 
@@ -81,32 +80,34 @@
     return jnp.concatenate([pair[:, 0:lanes], pair[:, lanes:]], axis=0)
 
 
-def pack_own_body(own_hbm, ref_hbm, own_ref, ref_ref, part_ref, sems):
+def pack_own_body(
+    own_hbm, ref_hbm, own_ref, ref_ref, part_ref, pick_ref, own_order_ref, other_order_ref, sems
+):
     copies = [
         pltpu.make_async_copy(own_hbm, own_ref, sems.at[0]),
         pltpu.make_async_copy(ref_hbm, ref_ref, sems.at[1]),
     ]
     for copy in copies:
         copy.start()
-    views, _, _, width = own_ref.shape
+    views, half, rows, width = own_ref.shape
     lanes = part_ref.shape[1]
     role, order, *_ = position()
-    pick = columns_of(LEAD, width, edge_start(role, width, LEAD))
-    pick_ref = columns_of(EDGE, width, edge_start(role, width, EDGE))
+    pick_ref[...] = columns_of(LEAD, width, edge_start(role, width, LEAD))
+    own_order_ref[...] = lane_order(half, rows, order)
+    other_order_ref[...] = lane_order(half, rows, 1 - order)
+    few = columns_of(EDGE, width, edge_start(role, width, EDGE))
     copies[0].wait()
-    for i, pair in enumerate(turned_half(own_ref, pick, order)):
+    for i, pair in enumerate(turned_half(own_ref, pick_ref[...], own_order_ref[...])):
         at = 2 * i * LEAD
         part_ref[at : at + 2 * LEAD] = stacked(pair, lanes).astype(jnp.bfloat16)
     copies[1].wait()
-    part_ref[views * LEAD :] = turned_ref(ref_ref, pick_ref).astype(jnp.bfloat16)
-
-
-def pack_other_body(part_ref, other_ref, packet_ref):
-    views, _, _, width = other_ref.shape
+    part_ref[views * LEAD :] = turned_ref(ref_ref, few).astype(jnp.bfloat16)
+
+
+def pack_other_body(part_ref, pick_ref, other_order_ref, other_ref, packet_ref):
+    views = other_ref.shape[0]
     lanes = packet_ref.shape[1]
-    role, order, *_ = position()
-    pick = columns_of(LEAD, width, edge_start(role, width, LEAD))
-    for i, pair in enumerate(turned_half(other_ref, pick, 1 - order)):
+    for i, pair in enumerate(turned_half(other_ref, pick_ref[...], other_order_ref[...])):
         at = 2 * i * LEAD
         both = part_ref[at : at + 2 * LEAD].astype(jnp.float32) + stacked(pair, lanes)
         packet_ref[at : at + 2 * LEAD] = both.astype(jnp.bfloat16)
@@ -265,13 +266,16 @@
     first[low:high, out_lanes:] = jnp.maximum(raw + table_ref[1:2, out_lanes:], 0.0)
 
 
-def weights(low, high, planes, block, first, table_ref, band_two, spread_ref):
+def convolve_second(low, high, planes, block, first, table_ref, band_two):
     out_lanes = planes * block
     wide, _ = three_taps(first, low, high, out_lanes)
     second = dot(wide, band_two[...])
     second = jnp.maximum(second + table_ref[2:3, 0:out_lanes], 0.0) * table_ref[3:4, 0:out_lanes]
     half = out_lanes // 2
-    second = second[:, 0:half] + second[:, half:]
+    return second[:, 0:half] + second[:, half:]
+
+
+def weights(second, spread_ref):
     upper = second.astype(jnp.bfloat16)
     under = (second - upper.astype(jnp.float32)).astype(jnp.bfloat16)
     score = dot(jnp.concatenate([upper, under], axis=1), spread_ref[...])
@@ -293,10 +297,13 @@
 def second_stage(views, tall, planes, block, match, first, table_ref, band_two, spread_ref):
     out_lanes = planes * block
     total = weighted = 0.0
-    for at in range(0, views, BATCH):
-        weight = weights(
-            at * tall, (at + BATCH) * tall, planes, block, first, table_ref, band_two, spread_ref
-        )
+    steps = range(0, views, BATCH)
+    seconds = [
+        convolve_second(at * tall, (at + BATCH) * tall, planes, block, first, table_ref, band_two)
+        for at in steps
+    ]
+    for at, second in zip(steps, seconds):
+        weight = weights(second, spread_ref)
         for v in range(BATCH):
             part = weight[v * tall : (v + 1) * tall]
             row = (at + v) * tall + 2
@@ -329,6 +336,8 @@
     own_ref,
     other_ref,
     ref_ref,
+    own_order_ref,
+    other_order_ref,
     taps_ref,
     cols_ref,
     ref_cols_ref,
@@ -349,14 +358,17 @@
     lanes = 2 * half * rows
     inner = 2 * half // GROUPS
     block = GROUPS * rows
-    _, order, _, _, *ends = position()
+    _, _, _, _, *ends = position()
     pick = columns_of(width, width, 0)
     none = jnp.zeros((8, lanes), jnp.float32)
     columns = turned_ref(ref_ref, pick)
     ref_cols_ref[...] = columns.astype(jnp.bfloat16)
     wide[0:width] = columns
     wide[width:] = none
-    pairs = zip(turned_half(own_ref, pick, order), turned_half(other_ref, pick, 1 - order))
+    pairs = zip(
+        turned_half(own_ref, pick, own_order_ref[...]),
+        turned_half(other_ref, pick, other_order_ref[...]),
+    )
     for i, (low, high) in enumerate(pairs):
         columns = low + high
         for k in range(2):
@@ -509,11 +521,19 @@
         own, other = full[:, :half], full[:, half:]
 
     packet_shape = shape((views * LEAD + EDGE, lanes), bf16)
-    own, ref_feat, part = pl.pallas_call(
+    order_shape = shape((lanes, 2 * lanes), bf16)
+    own, ref_feat, part, pick, own_order, other_order = pl.pallas_call(
         pack_own_body,
-        out_shape=[shape(own.shape, bf16), shape(ref_feat.shape, bf16), packet_shape],
+        out_shape=[
+            shape(own.shape, bf16),
+            shape(ref_feat.shape, bf16),
+            packet_shape,
+            shape((LEAD, width), bf16),
+            order_shape,
+            order_shape,
+        ],
         in_specs=[whole(pltpu.HBM)] * 2,
-        out_specs=[whole(vmem)] * 3,
+        out_specs=[whole(vmem)] * 6,
         scratch_shapes=[pltpu.SemaphoreType.DMA((2,))],
         compiler_params=limit(8),
         name="pack_own",
@@ -521,11 +541,11 @@
     packet = pl.pallas_call(
         pack_other_body,
         out_shape=packet_shape,
-        in_specs=[whole(vmem)] * 2,
+        in_specs=[whole(vmem)] * 4,
         out_specs=whole(vmem),
         compiler_params=limit(8),
         name="pack_other",
-    )(part, other)
+    )(part, pick, other_order, other)
 
     pairs = [(sides * i, sides * (i + 1)) for i in range(tiles - 1)]
     pairs += [(sides * (i + 1) + 1, sides * i + 1) for i in range(tiles - 1)]
@@ -565,7 +585,7 @@
             shape((high, span), f32),
             shape((high, span), f32),
         ],
-        in_specs=[whole(vmem)] * 10,
+        in_specs=[whole(vmem)] * 12,
         out_specs=[whole(vmem)] * 11,
         scratch_shapes=[
             pltpu.VMEM((views, width + 16, lanes), f32),
@@ -576,7 +596,20 @@
             flops=3 * 10**9, bytes_accessed=10**6, transcendentals=10**5
         ),
         name="inner_columns",
-    )(shifts, before, after, bias_one, bias_two, view_head, own, other, ref_feat, both_taps)
+    )(
+        shifts,
+        before,
+        after,
+        bias_one,
+        bias_two,
+        view_head,
+        own,
+        other,
+        ref_feat,
+        own_order,
+        other_order,
+        both_taps,
+    )
     got, match, first, *inner = lax.optimization_barrier((got, match, first, *inner))
     if sides == 2:
         swapped = swap_planes(got)

time: 14.3 us -> 14.1 us (0.986)
  local copies, waits for them, and re-layouts: 0.42 us -> 1.09 us
  starting transfers between devices: 4.26 us -> 3.59 us
  Pallas kernels: 8.67 us -> 8.15 us
  waiting for transfers between devices: 0.68 us -> 0.98 us
    ppermute x3, starting transfers between devices: 2.15 us -> 1.48 us  [swap_planes(): return lax.ppermute(value, 'plane', [(0, 1), (1, 0)])]
    unnamed x12, local copies, waits for them, and re-layouts: 0.04 us -> 0.7 us
    pallas_call x1, Pallas kernels: 1.03 us -> 0.73 us  [per_device(): pl.pallas_call(late_body, out_shape=shape((late_rows, out_lanes), bf16),...]
    ppermute x3, waiting for transfers between devices: 0.68 us -> 0.98 us  [swap_planes(): return lax.ppermute(value, 'plane', [(0, 1), (1, 0)])]
    pallas_call x1, Pallas kernels: 3.39 us -> 3.19 us  [per_device(): pl.pallas_call(outer_body, out_shape=shape((GROUPS, planes, rows, width),...]
  transfers between devices with their start and end apart: 4 -> 4, of which waited for: 1 -> 2; matrix products, arithmetic and copies ran while one was open for 3% -> 3% of each run, Pallas kernels for 35% -> 33%
where the time goes in v8:
time: 14.1 us; the launch traced here: 13.9 us
  Pallas kernels  8.15 us (58%)
  starting transfers between devices  3.59 us (25%)
  local copies, waits for them, and re-layouts  1.09 us (8%)
  waiting for transfers between devices  0.98 us (7%)
    pallas_call x1, Pallas kernels, per_device(): pl.pallas_call(outer_body, out_shape=shape((GROUPS, planes, rows, width),...  3.19 us
    pallas_call x1, Pallas kernels, per_device(): pl.pallas_call(inner_body, out_shape=[shape((views, width, lanes), bf16),...  2.29 us
    ppermute x1, starting transfers between devices, per_device(): got = lax.ppermute(packet, ('tile', 'plane'), pairs)  2.11 us
    pallas_call x1, Pallas kernels, per_device(): pl.pallas_call(pack_own_body, out_shape=[shape(own.shape, bf16), shape(re...  1.57 us
    ppermute x3, starting transfers between devices, swap_planes(): return lax.ppermute(value, 'plane', [(0, 1), (1, 0)])  1.48 us
    ppermute x3, waiting for transfers between devices, swap_planes(): return lax.ppermute(value, 'plane', [(0, 1), (1, 0)])  0.98 us
    pallas_call x1, Pallas kernels, per_device(): pl.pallas_call(late_body, out_shape=shape((late_rows, out_lanes), bf16),...  0.73 us
    unnamed x12, local copies, waits for them, and re-layouts  0.7 us
  transfers between devices with their start and end apart: 4, of which 2 were waited for; matrix products, arithmetic and copies ran while one was open for 3% of the time, Pallas kernels for 33%

profile of v8, /device:TPU:25, one launch (start us, length us, event | category | flops | bytes accessed | tf_op | source)
XLA Modules:
  0.0 13.9 jit_solution(17840917852143101974)
XLA Ops:
  0.0 0.7 %collective-permute-start = (bf16[4,16,4,256]{3,2,1,0:T(4,128)(2,1)}, bf16[4,16,4,256]{3,2,1,0:T(4,128)(2,1)S(1)}, u32[]{:S(2)}, u32[]{:S(2)}) collective-permute-start(bf16[4,16,4,256]{3,2,1,0:T(4,128)(2,1)} %own_hbm.1), channel_id=1, source_target_pairs={{0,1},{1,0},{2,3},{3,2},{4,5},{5,4},{6,7},{7,6},{8,9},{9,8},{10,11... | collective-permute-start | bytes 393224 | tf_op jit(solution)/shard_map/ppermute | solution.py:505
  0.7 1.6 %pack_own.1 = (bf16[4,16,4,256]{3,2,1,0:T(4,128)(2,1)S(1)}, bf16[32,4,256]{2,1,0:T(4,128)(2,1)S(1)}, bf16[560,128]{1,0:T(8,128)(2,1)S(1)}, bf16[136,256]{1,0:T(8...) custom-call(bf16[4,16,4,256]{3,2,1,0:T(4,128)(2,1)} %own_hbm.1, bf16[32,4,256]{2,1,0:T(4,128)(2,1)} %ref_hbm.1), custom_call_target="tpu_custom_call" | custom-call | tf_op jit(solution)/shard_map/pack_own/pallas_call | solution.py:525
  2.2 0.0 collective-permute-done.other_ref
  2.3 0.0 copy-start
  2.3 0.0 copy-start.4
  2.3 0.0 copy-start.5
  2.3 0.4 %pack_other.1 = bf16[560,128]{1,0:T(8,128)(2,1)S(1)} custom-call(bf16[560,128]{1,0:T(8,128)(2,1)S(1)} %get-tuple-element.39.part_ref, bf16[136,256]{1,0:T(8,128)(2,1)S(1)} %get-tuple-element.40.pick_ref, bf16[128,256]{1,0:T(8,128)(2,1)S(1)} %get-tuple-element.41.other_order_ref, bf16[4,16,4,256]{3,2,1,0:T(4,128)(2,1)S(1)} %collective-permute-done.other_ref), custom_call_target="tpu_custom_call" | custom-call | tf_op jit(solution)/shard_map/pack_other/pallas_call | solution.py:541
  2.7 2.1 %collective-permute-start.1 = (bf16[560,128]{1,0:T(8,128)(2,1)S(1)}, bf16[560,128]{1,0:T(8,128)(2,1)S(1)}, u32[]{:S(2)}, u32[]{:S(2)}) collective-permute-start(bf16[560,128]{1,0:T(8,128)(2,1)S(1)} %pack_other.1), channel_id=1, source_target_pairs={{0,2},{2,4},{4,6},{6,8},{8,10},{10,12},{12,14},{14,16},{16,18},{18... | collective-permute-start | bytes 430088 | tf_op jit(solution)/shard_map/ppermute | solution.py:553
  4.8 0.0 copy-done
  4.8 0.0 collective-permute-start.2
  4.8 0.0 copy-done.4
  4.8 0.0 copy-done.5
  4.9 0.1 stack_reshape.7
  5.0 0.1 stack_reshape.6
  5.1 0.1 copy.17.taps_ref
  5.2 0.7 %collective-permute-done.2.before.after = s32[4,8]{1,0:T(4,128)S(1)} collective-permute-done((s32[4,8]{1,0:T(4,128)S(1)}, s32[4,8]{1,0:T(4,128)S(1)}, u32[]{:S(2)}, u32[]{:S(2)}) %collective-permute-start.2) | collective-permute-done | bytes 160 | tf_op jit(solution)/shard_map/ppermute | solution.py:505
  5.9 0.0 copy-start.1
  6.0 0.0 copy-start.2
  6.0 0.0 copy-start.3
  6.0 0.6 %copy-done.1 = f32[8]{0:T(128)S(1)} copy-done((f32[8]{0:T(128)S(1)}, f32[8]{0:T(128)}, u32[]{:S(2)}) %copy-start.1) | copy-done | bytes 56
  6.6 0.0 copy-done.2
  6.6 0.0 copy-done.3
  6.6 2.3 %inner_columns.1 = (bf16[4,256,128]{2,1,0:T(8,128)(2,1)S(1)}, bf16[256,128]{1,0:T(8,128)(2,1)S(1)}, s32[8,128]{1,0:T(8,128)S(1)}, f32[8,384]{1,0:T(8,128)S(1)}, ...) custom-call(s32[4,8]{1,0:T(4,128)S(1)} %copy-done, ...), custom_call_target="tpu_custom_call" | custom-call | flops 3000000000 | bytes 1000000 | tf_op jit(solution)/shard_map/inner_columns/pallas_call | solution.py:573
  8.9 0.0 collective-permute-done.1.got_ref
  8.9 0.8 %collective-permute-start.3 = (bf16[560,128]{1,0:T(8,128)(2,1)S(1)}, bf16[560,128]{1,0:T(8,128)(2,1)S(1)}, u32[]{:S(2)}, u32[]{:S(2)}) collective-permute-start(bf16[560,128]{1,0:T(8,128)(2,1)S(1)} %collective-permute-done.1.got_ref), channel_id=1, source_target_pairs={{0,1},{1,0},{2,3},{3,2},{4,5},{5,4},{6,7},{7,6},{8,9},{9,8},{10,11... | collective-permute-start | bytes 430088 | tf_op jit(solution)/shard_map/ppermute | solution.py:505
  9.7 0.7 %late_columns.1.late_ref = bf16[128,256]{1,0:T(8,128)(2,1)S(1)} custom-call(f32[552,384]{1,0:T(8,128)S(1)} %get-tuple-element.70.match, f32[552,384]{1,0:T(8,128)S(1)} %get-tuple-element.71.first, f32[8,384]{1,0:T(8,128)S(1)} %get-tuple-element.64.table_ref, bf16[256,256]{1,0:T(8,128)(2,1)S(1)} %get-tuple-element.65.spread_ref, ...), custom_call_target="tpu_custom_call" | custom-call | flops 2000000000 | bytes 1000000 | tf_op jit(solution)/shard_map/late_columns/pallas_call | solution.py:619
  10.5 0.3 %collective-permute-done.3.swapped_ref = bf16[560,128]{1,0:T(8,128)(2,1)S(1)} collective-permute-done((bf16[560,128]{1,0:T(8,128)(2,1)S(1)}, bf16[560,128]{1,0:T(8,128)(2,1)S(1)}, u32[]{:S(2)}, u32[]{:S(2)}) %collective-permute-start.3) | collective-permute-done | bytes 143392 | tf_op jit(solution)/shard_map/ppermute | solution.py:505
  10.7 3.2 %outer_columns.1 = bf16[8,8,4,256]{3,2,1,0:T(4,128)(2,1)} custom-call(bf16[4,256,128]{2,1,0:T(8,128)(2,1)S(1)} %get-tuple-element.61.cols_ref, bf16[256,128]{1,0:T(8,128)(2,1)S(1)} %get-tuple-element.62.ref_cols_ref, s32[8,128]{1,0:T(8,128)S(1)} %get-tuple-element.63.word_ref, f32[8,384]{1,0:T(8,128)S(1)} %get-tuple-element.64.table_ref, ...), custom_call_target="tpu_custom_call" | custom-call | tf_op jit(solution)/shard_map/outer_columns/pallas_call | solution.py:631
  (4 shorter events, 0.1 us)
Async XLA Ops:
  0.0 2.3 %collective-permute-start = (bf16[4,16,4,256]{3,2,1,0:T(4,128)(2,1)}, bf16[4,16,4,256]{3,2,1,0:T(4,128)(2,1)S(1)}, u32[]{:S(2)}, u32[]{:S(2)}) collective-permute-start(bf16[4,16,4,256]{3,2,1,0:T(4,128)(2,1)} %own_hbm.1), channel_id=1, source_target_pairs={{0,1},{1,0},{2,3},{3,2},{4,5},{5,4},{6,7},{7,6},{8,9},{9,8},{10,11... | collective-permute-start | bytes 393224 | tf_op jit(solution)/shard_map/ppermute | solution.py:505
  2.3 2.5 %copy-start = (s32[4,8]{1,0:T(4,128)S(1)}, s32[4,8]{1,0:T(4,128)}, u32[]{:S(2)}) copy-start(s32[4,8]{1,0:T(4,128)} %shifts) | copy-start | bytes 388
  2.3 2.5 %copy-start.4 = (bf16[8,8,3,3,3]{1,0,4,3,2:T(8,128)(2,1)S(1)}, bf16[8,8,3,3,3]{1,0,4,3,2:T(8,128)(2,1)}, u32[]{:S(2)}) copy-start(bf16[8,8,3,3,3]{1,0,4,3,2:T(8,128)(2,1)} %param.13) | copy-start | bytes 10372
  2.3 2.5 %copy-start.5 = (bf16[8,8,3,3,3]{1,0,4,3,2:T(8,128)(2,1)S(1)}, bf16[8,8,3,3,3]{1,0,4,3,2:T(8,128)(2,1)}, u32[]{:S(2)}) copy-start(bf16[8,8,3,3,3]{1,0,4,3,2:T(8,128)(2,1)} %param.11) | copy-start | bytes 10372
  2.7 6.2 %collective-permute-start.1 = (bf16[560,128]{1,0:T(8,128)(2,1)S(1)}, bf16[560,128]{1,0:T(8,128)(2,1)S(1)}, u32[]{:S(2)}, u32[]{:S(2)}) collective-permute-start(bf16[560,128]{1,0:T(8,128)(2,1)S(1)} %pack_other.1), channel_id=1, source_target_pairs={{0,2},{2,4},{4,6},{6,8},{8,10},{10,12},{12,14},{14,16},{16,18},{18... | collective-permute-start | bytes 430088 | tf_op jit(solution)/shard_map/ppermute | solution.py:553
  4.8 1.2 %collective-permute-start.2 = (s32[4,8]{1,0:T(4,128)S(1)}, s32[4,8]{1,0:T(4,128)S(1)}, u32[]{:S(2)}, u32[]{:S(2)}) collective-permute-start(s32[4,8]{1,0:T(4,128)S(1)} %copy-done), channel_id=1, source_target_pairs={{0,1},{1,0},{2,3},{3,2},{4,5},{5,4},{6,7},{7,6},{8,9},{9,8},{10,11... | collective-permute-start | bytes 392 | tf_op jit(solution)/shard_map/ppermute | solution.py:505
  5.9 0.7 %copy-start.1 = (f32[8]{0:T(128)S(1)}, f32[8]{0:T(128)}, u32[]{:S(2)}) copy-start(f32[8]{0:T(128)} %bias_one.1) | copy-start | bytes 100
  6.0 0.7 %copy-start.2 = (f32[8]{0:T(128)S(1)}, f32[8]{0:T(128)}, u32[]{:S(2)}) copy-start(f32[8]{0:T(128)} %bias_two.1) | copy-start | bytes 100
  6.0 0.7 %copy-start.3 = (f32[8]{0:T(128)S(1)}, f32[8]{0:T(128)}, u32[]{:S(2)}) copy-start(f32[8]{0:T(128)} %view_head.1) | copy-start | bytes 100
  8.9 1.8 %collective-permute-start.3 = (bf16[560,128]{1,0:T(8,128)(2,1)S(1)}, bf16[560,128]{1,0:T(8,128)(2,1)S(1)}, u32[]{:S(2)}, u32[]{:S(2)}) collective-permute-start(bf16[560,128]{1,0:T(8,128)(2,1)S(1)} %collective-permute-done.1.got_ref), channel_id=1, source_target_pairs={{0,1},{1,0},{2,3},{3,2},{4,5},{5,4},{6,7},{7,6},{8,9},{9,8},{10,11... | collective-permute-start | bytes 430088 | tf_op jit(solution)/shard_map/ppermute | solution.py:505

commit v9 on v8

--- a/solution.py
+++ b/solution.py
@@ -80,15 +80,17 @@
     return jnp.concatenate([pair[:, 0:lanes], pair[:, lanes:]], axis=0)
 
 
-def pack_own_body(
-    own_hbm, ref_hbm, own_ref, ref_ref, part_ref, pick_ref, own_order_ref, other_order_ref, sems
-):
+def pack_own_body(*refs):
+    count = (len(refs) - 5) // 2
+    sources, targets = refs[:count], refs[count : 2 * count]
+    part_ref, pick_ref, own_order_ref, other_order_ref, sems = refs[2 * count :]
     copies = [
-        pltpu.make_async_copy(own_hbm, own_ref, sems.at[0]),
-        pltpu.make_async_copy(ref_hbm, ref_ref, sems.at[1]),
+        pltpu.make_async_copy(source, target, sems.at[i])
+        for i, (source, target) in enumerate(zip(sources, targets))
     ]
     for copy in copies:
         copy.start()
+    own_ref, ref_ref = targets[:2]
     views, half, rows, width = own_ref.shape
     lanes = part_ref.shape[1]
     role, order, *_ = position()
@@ -100,7 +102,8 @@
     for i, pair in enumerate(turned_half(own_ref, pick_ref[...], own_order_ref[...])):
         at = 2 * i * LEAD
         part_ref[at : at + 2 * LEAD] = stacked(pair, lanes).astype(jnp.bfloat16)
-    copies[1].wait()
+    for copy in copies[1:]:
+        copy.wait()
     part_ref[views * LEAD :] = turned_ref(ref_ref, few).astype(jnp.bfloat16)
 
 
@@ -261,9 +264,15 @@
     out_lanes = planes * block
     wide, tails = three_taps(match, low, high, out_lanes)
     raw = dot(wide, band_one[...])
-    first[low:high, 0:out_lanes] = jnp.maximum(raw + table_ref[1:2, 0:out_lanes], 0.0)
+    main = jnp.maximum(raw + table_ref[1:2, 0:out_lanes], 0.0)
     raw = dot(tails, rest_ref[...])
-    first[low:high, out_lanes:] = jnp.maximum(raw + table_ref[1:2, out_lanes:], 0.0)
+    rest = jnp.maximum(raw + table_ref[1:2, out_lanes:], 0.0)
+
+    def store():
+        first[low:high, 0:out_lanes] = main
+        first[low:high, out_lanes:] = rest
+
+    return store
 
 
 def convolve_second(low, high, planes, block, first, table_ref, band_two):
@@ -285,13 +294,18 @@
 def first_stage(
     views, tall, planes, block, filled, mend, match, first, table_ref, band_one, rest_ref
 ):
-    for at in range(0, views, BATCH):
-        for v in range(at, at + BATCH):
+    store = None
+    for v in range(views + 1):
+        if v < views:
             filled(v)
-        low, high = at * tall, (at + BATCH) * tall
-        convolve_first(low, high, planes, block, match, first, table_ref, band_one, rest_ref)
-        for v in range(at, at + BATCH):
-            mend(v * tall)
+        if store is not None:
+            store()
+            mend((v - 1) * tall)
+        if v < views:
+            low, high = v * tall, (v + 1) * tall
+            store = convolve_first(
+                low, high, planes, block, match, first, table_ref, band_one, rest_ref
+            )
 
 
 def second_stage(views, tall, planes, block, match, first, table_ref, band_two, spread_ref):
@@ -441,6 +455,8 @@
     match,
     first,
     joined,
+    buffer,
+    sems,
 ):
     views, width, lanes = cols_ref.shape
     groups, planes, rows, _ = out_ref.shape
@@ -449,9 +465,8 @@
 
     near = read_shifts(views, planes, word_ref)
     left = jnp.where(order == 0, got_ref[...], swapped_ref[...])
+    left = jnp.where(is_first_tile, jnp.zeros_like(left), left)
     right = jnp.where(order == 0, swapped_ref[...], got_ref[...])
-    left = jnp.where(is_first_tile, jnp.zeros_like(left), left)
-    right = jnp.where(is_last_tile, jnp.zeros_like(right), right)
     for v in range(0, views, 2):
         at = v * LEAD
         pair = left[at : at + 2 * LEAD].astype(jnp.float32)
@@ -462,7 +477,7 @@
             src[v + k, LEAD + width :] = ends[k * LEAD : k * LEAD + EDGE]
     wide[0:EDGE] = left[views * LEAD :].astype(jnp.float32)
     wide[EDGE : EDGE + width] = ref_cols_ref[...].astype(jnp.float32)
-    wide[EDGE + width :] = right[views * LEAD : views * LEAD + EDGE].astype(jnp.float32)
+    wide[EDGE + width :] = jnp.where(is_last_tile, 0.0, right[views * LEAD :].astype(jnp.float32))
     main = MAX_SHIFT + 8
     tall = main + 8
     none = jnp.zeros((1, match.shape[1]), jnp.float32)
@@ -489,8 +504,18 @@
     joined[MAX_SHIFT:] = late_ref[...].astype(jnp.float32)
     joined[MAX_SHIFT : MAX_SHIFT + 2] = part[MAX_SHIFT : MAX_SHIFT + 2]
     joined[width - 2 :] = part[main : main + 2]
-    turned = dot_nt(perm_ref[...], joined[...].astype(jnp.bfloat16)).astype(jnp.bfloat16)
-    out_ref[...] = turned.reshape(groups, planes, rows, width)
+    copies = []
+    for half in range(2):
+        at = half * (groups // 2)
+        span = pl.ds(at, groups // 2)
+        chosen = perm_ref[at * planes * rows : (at + groups // 2) * planes * rows]
+        turned = dot_nt(chosen, joined[...].astype(jnp.bfloat16)).astype(jnp.bfloat16)
+        buffer[at : at + groups // 2] = turned.reshape(groups // 2, planes, rows, width)
+        copy = pltpu.make_async_copy(buffer.at[span], out_ref.at[span], sems.at[half])
+        copy.start()
+        copies.append(copy)
+    for copy in copies:
+        copy.wait()
 
 
 def whole(memory):
@@ -522,22 +547,18 @@
 
     packet_shape = shape((views * LEAD + EDGE, lanes), bf16)
     order_shape = shape((lanes, 2 * lanes), bf16)
-    own, ref_feat, part, pick, own_order, other_order = pl.pallas_call(
+    staged = (own, ref_feat, shifts, bias_one, bias_two, view_head)
+    *staged, part, pick, own_order, other_order = pl.pallas_call(
         pack_own_body,
-        out_shape=[
-            shape(own.shape, bf16),
-            shape(ref_feat.shape, bf16),
-            packet_shape,
-            shape((LEAD, width), bf16),
-            order_shape,
-            order_shape,
-        ],
-        in_specs=[whole(pltpu.HBM)] * 2,
-        out_specs=[whole(vmem)] * 6,
-        scratch_shapes=[pltpu.SemaphoreType.DMA((2,))],
+        out_shape=[shape(x.shape, x.dtype) for x in staged]
+        + [packet_shape, shape((LEAD, width), bf16), order_shape, order_shape],
+        in_specs=[whole(pltpu.HBM)] * len(staged),
+        out_specs=[whole(vmem)] * (len(staged) + 4),
+        scratch_shapes=[pltpu.SemaphoreType.DMA((len(staged),))],
         compiler_params=limit(8),
         name="pack_own",
-    )(*(pltpu.with_memory_space_constraint(x, pltpu.HBM) for x in (own, ref_feat)))
+    )(*(pltpu.with_memory_space_constraint(x, pltpu.HBM) for x in staged))
+    own, ref_feat, shifts, bias_one, bias_two, view_head = staged
     packet = pl.pallas_call(
         pack_other_body,
         out_shape=packet_shape,
@@ -632,13 +653,15 @@
         outer_body,
         out_shape=shape((GROUPS, planes, rows, width), bf16),
         in_specs=[whole(vmem)] * 12,
-        out_specs=whole(vmem),
+        out_specs=whole(pltpu.HBM),
         scratch_shapes=[
             pltpu.VMEM((views, LEAD + width + EDGE, lanes), f32),
             pltpu.VMEM((EDGE + width + EDGE, lanes), f32),
             pltpu.VMEM((high, span), f32),
             pltpu.VMEM((high, span), f32),
             pltpu.VMEM((width, out_lanes), f32),
+            pltpu.VMEM((GROUPS, planes, rows, width), bf16),
+            pltpu.SemaphoreType.DMA((2,)),
         ],
         compiler_params=limit(24),
         name="outer_columns",

time: 14.1 us -> 14.1 us (level)
  starting transfers between devices: 3.59 us -> 4.29 us
  local copies, waits for them, and re-layouts: 1.09 us -> 0.39 us
    ppermute x3, starting transfers between devices: 1.48 us -> 2.18 us  [swap_planes(): return lax.ppermute(value, 'plane', [(0, 1), (1, 0)])]
    unnamed x12 -> x4, local copies, waits for them, and re-layouts: 0.7 us -> 0.01 us
where the time goes in v9:
time: 14.1 us; the launch traced here: 13.9 us
  Pallas kernels  8.14 us (58%)
  starting transfers between devices  4.29 us (30%)
  waiting for transfers between devices  0.98 us (7%)
  local copies, waits for them, and re-layouts  0.39 us (3%)
    pallas_call x1, Pallas kernels, per_device(): pl.pallas_call(outer_body, out_shape=shape((GROUPS, planes, rows, width),...  3.14 us
    pallas_call x1, Pallas kernels, per_device(): pl.pallas_call(inner_body, out_shape=[shape((views, width, lanes), bf16),...  2.28 us
    ppermute x3, starting transfers between devices, swap_planes(): return lax.ppermute(value, 'plane', [(0, 1), (1, 0)])  2.18 us
    ppermute x1, starting transfers between devices, per_device(): got = lax.ppermute(packet, ('tile', 'plane'), pairs)  2.11 us
    pallas_call x1, Pallas kernels, per_device(): pl.pallas_call(pack_own_body, out_shape=[shape(x.shape, x.dtype) for x in...  1.61 us
    ppermute x3, waiting for transfers between devices, swap_planes(): return lax.ppermute(value, 'plane', [(0, 1), (1, 0)])  0.98 us
    pallas_call x1, Pallas kernels, per_device(): pl.pallas_call(late_body, out_shape=shape((late_rows, out_lanes), bf16),...  0.74 us
    pallas_call x1, Pallas kernels, per_device(): pl.pallas_call(pack_other_body, out_shape=packet_shape, in_specs=[whole(v...  0.38 us
  transfers between devices with their start and end apart: 4, of which 2 were waited for; matrix products, arithmetic and copies ran while one was open for 3% of the time, Pallas kernels for 33%

profile of v9, /device:TPU:25, one launch (start us, length us, event | category | flops | bytes accessed | tf_op | source)
XLA Modules:
  0.0 13.9 jit_solution(13243567507533952847)
XLA Ops:
  0.0 0.7 %collective-permute-start = (bf16[4,16,4,256]{3,2,1,0:T(4,128)(2,1)}, bf16[4,16,4,256]{3,2,1,0:T(4,128)(2,1)S(1)}, u32[]{:S(2)}, u32[]{:S(2)}) collective-permute-start(bf16[4,16,4,256]{3,2,1,0:T(4,128)(2,1)} %refs_0_.1), channel_id=1, source_target_pairs={{0,1},{1,0},{2,3},{3,2},{4,5},{5,4},{6,7},{7,6},{8,9},{9,8},{10,11... | collective-permute-start | bytes 393224 | tf_op jit(solution)/shard_map/ppermute | solution.py:530
  0.7 1.6 %pack_own.1 = (bf16[4,16,4,256]{3,2,1,0:T(4,128)(2,1)S(1)}, bf16[32,4,256]{2,1,0:T(4,128)(2,1)S(1)}, s32[4,8]{1,0:T(4,128)S(1)}, f32[8]{0:T(128)S(1)}, f32[8]{0:...) custom-call(bf16[4,16,4,256]{3,2,1,0:T(4,128)(2,1)} %refs_0_.1, ...), custom_call_target="tpu_custom_call" | custom-call | tf_op jit(solution)/shard_map/pack_own/pallas_call | solution.py:551
  2.3 0.0 collective-permute-done.other_ref
  2.3 0.0 copy-start
  2.3 0.0 copy-start.1
  2.3 0.4 %pack_other.1 = bf16[560,128]{1,0:T(8,128)(2,1)S(1)} custom-call(bf16[560,128]{1,0:T(8,128)(2,1)S(1)} %get-tuple-element.43.part_ref, bf16[136,256]{1,0:T(8,128)(2,1)S(1)} %get-tuple-element.44.pick_ref, bf16[128,256]{1,0:T(8,128)(2,1)S(1)} %get-tuple-element.45.other_order_ref, bf16[4,16,4,256]{3,2,1,0:T(4,128)(2,1)S(1)} %collective-permute-done.other_ref), custom_call_target="tpu_custom_call" | custom-call | tf_op jit(solution)/shard_map/pack_other/pallas_call | solution.py:562
  2.7 2.1 %collective-permute-start.1 = (bf16[560,128]{1,0:T(8,128)(2,1)S(1)}, bf16[560,128]{1,0:T(8,128)(2,1)S(1)}, u32[]{:S(2)}, u32[]{:S(2)}) collective-permute-start(bf16[560,128]{1,0:T(8,128)(2,1)S(1)} %pack_other.1), channel_id=1, source_target_pairs={{0,2},{2,4},{4,6},{6,8},{8,10},{10,12},{12,14},{14,16},{16,18},{18... | collective-permute-start | bytes 430088 | tf_op jit(solution)/shard_map/ppermute | solution.py:574
  4.8 0.0 collective-permute-start.2
  4.8 0.0 copy-done
  4.8 0.0 copy-done.1
  4.9 0.1 stack_reshape.7
  5.0 0.1 stack_reshape.6
  5.2 0.1 copy.17.taps_ref
  5.3 0.7 %collective-permute-done.2.before.after = s32[4,8]{1,0:T(4,128)S(1)} collective-permute-done((s32[4,8]{1,0:T(4,128)S(1)}, s32[4,8]{1,0:T(4,128)S(1)}, u32[]{:S(2)}, u32[]{:S(2)}) %collective-permute-start.2) | collective-permute-done | bytes 160 | tf_op jit(solution)/shard_map/ppermute | solution.py:530
  6.0 2.3 %inner_columns.1 = (bf16[4,256,128]{2,1,0:T(8,128)(2,1)S(1)}, bf16[256,128]{1,0:T(8,128)(2,1)S(1)}, s32[8,128]{1,0:T(8,128)S(1)}, f32[8,384]{1,0:T(8,128)S(1)}, ...) custom-call(s32[4,8]{1,0:T(4,128)S(1)} %get-tuple-element.48.shifts,, ...), custom_call_target="tpu_custom_call" | custom-call | flops 3000000000 | bytes 1000000 | tf_op jit(solution)/shard_map/inner_columns/pallas_call | solution.py:594
  8.3 0.0 collective-permute-done.1.got_ref
  8.3 1.5 %collective-permute-start.3 = (bf16[560,128]{1,0:T(8,128)(2,1)S(1)}, bf16[560,128]{1,0:T(8,128)(2,1)S(1)}, u32[]{:S(2)}, u32[]{:S(2)}) collective-permute-start(bf16[560,128]{1,0:T(8,128)(2,1)S(1)} %collective-permute-done.1.got_ref), channel_id=1, source_target_pairs={{0,1},{1,0},{2,3},{3,2},{4,5},{5,4},{6,7},{7,6},{8,9},{9,8},{10,11... | collective-permute-start | bytes 430088 | tf_op jit(solution)/shard_map/ppermute | solution.py:530
  9.8 0.7 %late_columns.1.late_ref = bf16[128,256]{1,0:T(8,128)(2,1)S(1)} custom-call(f32[552,384]{1,0:T(8,128)S(1)} %get-tuple-element.78.match, f32[552,384]{1,0:T(8,128)S(1)} %get-tuple-element.79.first, f32[8,384]{1,0:T(8,128)S(1)} %get-tuple-element.72.table_ref, bf16[256,256]{1,0:T(8,128)(2,1)S(1)} %get-tuple-element.73.spread_ref, ...), custom_call_target="tpu_custom_call" | custom-call | flops 2000000000 | bytes 1000000 | tf_op jit(solution)/shard_map/late_columns/pallas_call | solution.py:640
  10.5 0.3 %collective-permute-done.3.swapped_ref = bf16[560,128]{1,0:T(8,128)(2,1)S(1)} collective-permute-done((bf16[560,128]{1,0:T(8,128)(2,1)S(1)}, bf16[560,128]{1,0:T(8,128)(2,1)S(1)}, u32[]{:S(2)}, u32[]{:S(2)}) %collective-permute-start.3) | collective-permute-done | bytes 143392 | tf_op jit(solution)/shard_map/ppermute | solution.py:530
  10.8 3.1 %outer_columns.1 = bf16[8,8,4,256]{3,2,1,0:T(4,128)(2,1)} custom-call(bf16[4,256,128]{2,1,0:T(8,128)(2,1)S(1)} %get-tuple-element.69.cols_ref, bf16[256,128]{1,0:T(8,128)(2,1)S(1)} %get-tuple-element.70.ref_cols_ref, s32[8,128]{1,0:T(8,128)S(1)} %get-tuple-element.71.word_ref, f32[8,384]{1,0:T(8,128)S(1)} %get-tuple-element.72.table_ref, ...), custom_call_target="tpu_custom_call" | custom-call | tf_op jit(solution)/shard_map/outer_columns/pallas_call | solution.py:652
  (4 shorter events, 0.1 us)
Async XLA Ops:
  0.0 2.3 %collective-permute-start = (bf16[4,16,4,256]{3,2,1,0:T(4,128)(2,1)}, bf16[4,16,4,256]{3,2,1,0:T(4,128)(2,1)S(1)}, u32[]{:S(2)}, u32[]{:S(2)}) collective-permute-start(bf16[4,16,4,256]{3,2,1,0:T(4,128)(2,1)} %refs_0_.1), channel_id=1, source_target_pairs={{0,1},{1,0},{2,3},{3,2},{4,5},{5,4},{6,7},{7,6},{8,9},{9,8},{10,11... | collective-permute-start | bytes 393224 | tf_op jit(solution)/shard_map/ppermute | solution.py:530
  2.3 2.5 %copy-start = (bf16[8,8,3,3,3]{1,0,4,3,2:T(8,128)(2,1)S(1)}, bf16[8,8,3,3,3]{1,0,4,3,2:T(8,128)(2,1)}, u32[]{:S(2)}) copy-start(bf16[8,8,3,3,3]{1,0,4,3,2:T(8,128)(2,1)} %param.13) | copy-start | bytes 10372
  2.3 2.5 %copy-start.1 = (bf16[8,8,3,3,3]{1,0,4,3,2:T(8,128)(2,1)S(1)}, bf16[8,8,3,3,3]{1,0,4,3,2:T(8,128)(2,1)}, u32[]{:S(2)}) copy-start(bf16[8,8,3,3,3]{1,0,4,3,2:T(8,128)(2,1)} %param.11) | copy-start | bytes 10372
  2.7 5.5 %collective-permute-start.1 = (bf16[560,128]{1,0:T(8,128)(2,1)S(1)}, bf16[560,128]{1,0:T(8,128)(2,1)S(1)}, u32[]{:S(2)}, u32[]{:S(2)}) collective-permute-start(bf16[560,128]{1,0:T(8,128)(2,1)S(1)} %pack_other.1), channel_id=1, source_target_pairs={{0,2},{2,4},{4,6},{6,8},{8,10},{10,12},{12,14},{14,16},{16,18},{18... | collective-permute-start | bytes 430088 | tf_op jit(solution)/shard_map/ppermute | solution.py:574
  4.8 1.2 %collective-permute-start.2 = (s32[4,8]{1,0:T(4,128)S(1)}, s32[4,8]{1,0:T(4,128)S(1)}, u32[]{:S(2)}, u32[]{:S(2)}) collective-permute-start(s32[4,8]{1,0:T(4,128)S(1)} %get-tuple-element.48.shifts), channel_id=1, source_target_pairs={{0,1},{1,0},{2,3},{3,2},{4,5},{5,4},{6,7},{7,6},{8,9},{9,8},{10,11... | collective-permute-start | bytes 392 | tf_op jit(solution)/shard_map/ppermute | solution.py:530
  8.3 2.5 %collective-permute-start.3 = (bf16[560,128]{1,0:T(8,128)(2,1)S(1)}, bf16[560,128]{1,0:T(8,128)(2,1)S(1)}, u32[]{:S(2)}, u32[]{:S(2)}) collective-permute-start(bf16[560,128]{1,0:T(8,128)(2,1)S(1)} %collective-permute-done.1.got_ref), channel_id=1, source_target_pairs={{0,1},{1,0},{2,3},{3,2},{4,5},{5,4},{6,7},{7,6},{8,9},{9,8},{10,11... | collective-permute-start | bytes 430088 | tf_op jit(solution)/shard_map/ppermute | solution.py:530

commit v10 on v9

--- a/solution.py
+++ b/solution.py
@@ -231,16 +231,24 @@
 
 
 def fill(pieces, near, src, wide, match, table_ref, block):
+    shared = lax.axis_size("plane") == 2
+    last = len(near) - 2
     for at, src_at, wide_at, count in pieces:
         quarter = iota((count, 128), 1) // block
         lower, middle, even = quarter < 2, (quarter == 1) | (quarter == 2), quarter % 2 == 0
         here = wide[wide_at : wide_at + count]
-        for q in range(match.shape[1] // 128):
-
-            def product(j):
-                return src[pl.ds(src_at - near[q * 4 + j], count)] * here
-
-            a, c, b, d = (product(j) for j in range(4))
+        ready = {}
+
+        def product(j):
+            if shared and j >= last:
+                j -= last
+            if j not in ready:
+                ready[j] = src[pl.ds(src_at - near[j], count)] * here
+            return ready[j]
+
+        tiles = match.shape[1] // 128
+        for q in (0, *reversed(range(1, tiles))):
+            a, c, b, d = (product(q * 4 + k) for k in range(4))
             x = jnp.where(lower, a, b) + pltpu.roll(jnp.where(lower, b, a), 64, 1)
             z = jnp.where(middle, c, d) + pltpu.roll(jnp.where(middle, d, c), 64, 1)
             y = jnp.where(even, x, z) + pltpu.roll(jnp.where(even, z, x), 96, 1)
@@ -288,7 +296,7 @@
     upper = second.astype(jnp.bfloat16)
     under = (second - upper.astype(jnp.float32)).astype(jnp.bfloat16)
     score = dot(jnp.concatenate([upper, under], axis=1), spread_ref[...])
-    return 1.0 / (1.0 + jnp.exp(-score))
+    return jax.nn.sigmoid(score)
 
 
 def first_stage(
@@ -337,6 +345,11 @@
 def read_shifts(views, planes, word_ref):
     at = [(0, planes - 2), (0, planes - 1)] + [(1, d) for d in range(planes)] + [(2, 0), (2, 1)]
     words = [word_ref[row, d] for row, d in at]
+    if lax.axis_size("plane") == 2:
+        _, _, _, _, is_first_plane, _ = position()
+        for k in range(2):
+            inside = jnp.where(is_first_plane, words[planes + 2 + k], words[k])
+            words[k] = words[planes + 2 + k] = inside
     return [[(word >> (8 * v)) & 255 for word in words] for v in range(views)]
 
 

time: 14.1 us -> 13.9 us (0.986)
  Pallas kernels: 8.14 us -> 7.91 us
where the time goes in v10:
time: 13.9 us; the launch traced here: 13.8 us
  Pallas kernels  7.91 us (57%)
  starting transfers between devices  4.36 us (31%)
  waiting for transfers between devices  1.02 us (7%)
  local copies, waits for them, and re-layouts  0.39 us (3%)
    pallas_call x1, Pallas kernels, per_device(): pl.pallas_call(outer_body, out_shape=shape((GROUPS, planes, rows, width),...  3.01 us
    ppermute x3, starting transfers between devices, swap_planes(): return lax.ppermute(value, 'plane', [(0, 1), (1, 0)])  2.25 us
    pallas_call x1, Pallas kernels, per_device(): pl.pallas_call(inner_body, out_shape=[shape((views, width, lanes), bf16),...  2.21 us
    ppermute x1, starting transfers between devices, per_device(): got = lax.ppermute(packet, ('tile', 'plane'), pairs)  2.11 us
    pallas_call x1, Pallas kernels, per_device(): pl.pallas_call(pack_own_body, out_shape=[shape(x.shape, x.dtype) for x in...  1.61 us
    ppermute x3, waiting for transfers between devices, swap_planes(): return lax.ppermute(value, 'plane', [(0, 1), (1, 0)])  1.01 us
    pallas_call x1, Pallas kernels, per_device(): pl.pallas_call(late_body, out_shape=shape((late_rows, out_lanes), bf16),...  0.7 us
    pallas_call x1, Pallas kernels, per_device(): pl.pallas_call(pack_other_body, out_shape=packet_shape, in_specs=[whole(v...  0.38 us
  transfers between devices with their start and end apart: 4, of which 2 were waited for; matrix products, arithmetic and copies ran while one was open for 3% of the time, Pallas kernels for 33%

profile of v10, /device:TPU:25, one launch (start us, length us, event | category | flops | bytes accessed | tf_op | source)
XLA Modules:
  0.0 13.8 jit_solution(11972401734061692927)
XLA Ops:
  0.0 0.7 %collective-permute-start = (bf16[4,16,4,256]{3,2,1,0:T(4,128)(2,1)}, bf16[4,16,4,256]{3,2,1,0:T(4,128)(2,1)S(1)}, u32[]{:S(2)}, u32[]{:S(2)}) collective-permute-start(bf16[4,16,4,256]{3,2,1,0:T(4,128)(2,1)} %refs_0_.1), channel_id=1, source_target_pairs={{0,1},{1,0},{2,3},{3,2},{4,5},{5,4},{6,7},{7,6},{8,9},{9,8},{10,11... | collective-permute-start | bytes 393224 | tf_op jit(solution)/shard_map/ppermute | solution.py:543
  0.7 1.6 %pack_own.1 = (bf16[4,16,4,256]{3,2,1,0:T(4,128)(2,1)S(1)}, bf16[32,4,256]{2,1,0:T(4,128)(2,1)S(1)}, s32[4,8]{1,0:T(4,128)S(1)}, f32[8]{0:T(128)S(1)}, f32[8]{0:...) custom-call(bf16[4,16,4,256]{3,2,1,0:T(4,128)(2,1)} %refs_0_.1, ...), custom_call_target="tpu_custom_call" | custom-call | tf_op jit(solution)/shard_map/pack_own/pallas_call | solution.py:564
  2.3 0.0 collective-permute-done.other_ref
  2.3 0.0 copy-start
  2.3 0.0 copy-start.1
  2.3 0.4 %pack_other.1 = bf16[560,128]{1,0:T(8,128)(2,1)S(1)} custom-call(bf16[560,128]{1,0:T(8,128)(2,1)S(1)} %get-tuple-element.43.part_ref, bf16[136,256]{1,0:T(8,128)(2,1)S(1)} %get-tuple-element.44.pick_ref, bf16[128,256]{1,0:T(8,128)(2,1)S(1)} %get-tuple-element.45.other_order_ref, bf16[4,16,4,256]{3,2,1,0:T(4,128)(2,1)S(1)} %collective-permute-done.other_ref), custom_call_target="tpu_custom_call" | custom-call | tf_op jit(solution)/shard_map/pack_other/pallas_call | solution.py:575
  2.7 2.1 %collective-permute-start.1 = (bf16[560,128]{1,0:T(8,128)(2,1)S(1)}, bf16[560,128]{1,0:T(8,128)(2,1)S(1)}, u32[]{:S(2)}, u32[]{:S(2)}) collective-permute-start(bf16[560,128]{1,0:T(8,128)(2,1)S(1)} %pack_other.1), channel_id=1, source_target_pairs={{0,2},{2,4},{4,6},{6,8},{8,10},{10,12},{12,14},{14,16},{16,18},{18... | collective-permute-start | bytes 430088 | tf_op jit(solution)/shard_map/ppermute | solution.py:587
  4.8 0.0 collective-permute-start.2
  4.8 0.0 copy-done
  4.8 0.0 copy-done.1
  4.9 0.1 stack_reshape.7
  5.0 0.1 stack_reshape.6
  5.2 0.1 copy.17.taps_ref
  5.3 0.7 %collective-permute-done.2.before.after = s32[4,8]{1,0:T(4,128)S(1)} collective-permute-done((s32[4,8]{1,0:T(4,128)S(1)}, s32[4,8]{1,0:T(4,128)S(1)}, u32[]{:S(2)}, u32[]{:S(2)}) %collective-permute-start.2) | collective-permute-done | bytes 160 | tf_op jit(solution)/shard_map/ppermute | solution.py:543
  6.0 2.2 %inner_columns.1 = (bf16[4,256,128]{2,1,0:T(8,128)(2,1)S(1)}, bf16[256,128]{1,0:T(8,128)(2,1)S(1)}, s32[8,128]{1,0:T(8,128)S(1)}, f32[8,384]{1,0:T(8,128)S(1)}, ...) custom-call(s32[4,8]{1,0:T(4,128)S(1)} %get-tuple-element.48.shifts,, ...), custom_call_target="tpu_custom_call" | custom-call | flops 3000000000 | bytes 1000000 | tf_op jit(solution)/shard_map/inner_columns/pallas_call | solution.py:607
  8.2 0.0 collective-permute-done.1.got_ref
  8.2 1.6 %collective-permute-start.3 = (bf16[560,128]{1,0:T(8,128)(2,1)S(1)}, bf16[560,128]{1,0:T(8,128)(2,1)S(1)}, u32[]{:S(2)}, u32[]{:S(2)}) collective-permute-start(bf16[560,128]{1,0:T(8,128)(2,1)S(1)} %collective-permute-done.1.got_ref), channel_id=1, source_target_pairs={{0,1},{1,0},{2,3},{3,2},{4,5},{5,4},{6,7},{7,6},{8,9},{9,8},{10,11... | collective-permute-start | bytes 430088 | tf_op jit(solution)/shard_map/ppermute | solution.py:543
  9.8 0.7 %late_columns.1.late_ref = bf16[128,256]{1,0:T(8,128)(2,1)S(1)} custom-call(f32[552,384]{1,0:T(8,128)S(1)} %get-tuple-element.78.match, f32[552,384]{1,0:T(8,128)S(1)} %get-tuple-element.79.first, f32[8,384]{1,0:T(8,128)S(1)} %get-tuple-element.72.table_ref, bf16[256,256]{1,0:T(8,128)(2,1)S(1)} %get-tuple-element.73.spread_ref, ...), custom_call_target="tpu_custom_call" | custom-call | flops 2000000000 | bytes 1000000 | tf_op jit(solution)/shard_map/late_columns/pallas_call | solution.py:653
  10.5 0.3 %collective-permute-done.3.swapped_ref = bf16[560,128]{1,0:T(8,128)(2,1)S(1)} collective-permute-done((bf16[560,128]{1,0:T(8,128)(2,1)S(1)}, bf16[560,128]{1,0:T(8,128)(2,1)S(1)}, u32[]{:S(2)}, u32[]{:S(2)}) %collective-permute-start.3) | collective-permute-done | bytes 143392 | tf_op jit(solution)/shard_map/ppermute | solution.py:543
  10.8 3.0 %outer_columns.1 = bf16[8,8,4,256]{3,2,1,0:T(4,128)(2,1)} custom-call(bf16[4,256,128]{2,1,0:T(8,128)(2,1)S(1)} %get-tuple-element.69.cols_ref, bf16[256,128]{1,0:T(8,128)(2,1)S(1)} %get-tuple-element.70.ref_cols_ref, s32[8,128]{1,0:T(8,128)S(1)} %get-tuple-element.71.word_ref, f32[8,384]{1,0:T(8,128)S(1)} %get-tuple-element.72.table_ref, ...), custom_call_target="tpu_custom_call" | custom-call | tf_op jit(solution)/shard_map/outer_columns/pallas_call | solution.py:665
  (4 shorter events, 0.1 us)
Async XLA Ops:
  0.0 2.3 %collective-permute-start = (bf16[4,16,4,256]{3,2,1,0:T(4,128)(2,1)}, bf16[4,16,4,256]{3,2,1,0:T(4,128)(2,1)S(1)}, u32[]{:S(2)}, u32[]{:S(2)}) collective-permute-start(bf16[4,16,4,256]{3,2,1,0:T(4,128)(2,1)} %refs_0_.1), channel_id=1, source_target_pairs={{0,1},{1,0},{2,3},{3,2},{4,5},{5,4},{6,7},{7,6},{8,9},{9,8},{10,11... | collective-permute-start | bytes 393224 | tf_op jit(solution)/shard_map/ppermute | solution.py:543
  2.3 2.5 %copy-start = (bf16[8,8,3,3,3]{1,0,4,3,2:T(8,128)(2,1)S(1)}, bf16[8,8,3,3,3]{1,0,4,3,2:T(8,128)(2,1)}, u32[]{:S(2)}) copy-start(bf16[8,8,3,3,3]{1,0,4,3,2:T(8,128)(2,1)} %param.13) | copy-start | bytes 10372
  2.3 2.5 %copy-start.1 = (bf16[8,8,3,3,3]{1,0,4,3,2:T(8,128)(2,1)S(1)}, bf16[8,8,3,3,3]{1,0,4,3,2:T(8,128)(2,1)}, u32[]{:S(2)}) copy-start(bf16[8,8,3,3,3]{1,0,4,3,2:T(8,128)(2,1)} %param.11) | copy-start | bytes 10372
  2.7 5.5 %collective-permute-start.1 = (bf16[560,128]{1,0:T(8,128)(2,1)S(1)}, bf16[560,128]{1,0:T(8,128)(2,1)S(1)}, u32[]{:S(2)}, u32[]{:S(2)}) collective-permute-start(bf16[560,128]{1,0:T(8,128)(2,1)S(1)} %pack_other.1), channel_id=1, source_target_pairs={{0,2},{2,4},{4,6},{6,8},{8,10},{10,12},{12,14},{14,16},{16,18},{18... | collective-permute-start | bytes 430088 | tf_op jit(solution)/shard_map/ppermute | solution.py:587
  4.8 1.2 %collective-permute-start.2 = (s32[4,8]{1,0:T(4,128)S(1)}, s32[4,8]{1,0:T(4,128)S(1)}, u32[]{:S(2)}, u32[]{:S(2)}) collective-permute-start(s32[4,8]{1,0:T(4,128)S(1)} %get-tuple-element.48.shifts), channel_id=1, source_target_pairs={{0,1},{1,0},{2,3},{3,2},{4,5},{5,4},{6,7},{7,6},{8,9},{9,8},{10,11... | collective-permute-start | bytes 392 | tf_op jit(solution)/shard_map/ppermute | solution.py:543
  8.2 2.6 %collective-permute-start.3 = (bf16[560,128]{1,0:T(8,128)(2,1)S(1)}, bf16[560,128]{1,0:T(8,128)(2,1)S(1)}, u32[]{:S(2)}, u32[]{:S(2)}) collective-permute-start(bf16[560,128]{1,0:T(8,128)(2,1)S(1)} %collective-permute-done.1.got_ref), channel_id=1, source_target_pairs={{0,1},{1,0},{2,3},{3,2},{4,5},{5,4},{6,7},{7,6},{8,9},{9,8},{10,11... | collective-permute-start | bytes 430088 | tf_op jit(solution)/shard_map/ppermute | solution.py:543

commit v11 on v10

--- a/solution.py
+++ b/solution.py
@@ -9,6 +9,7 @@
 MAX_SHIFT = 128
 LEAD = MAX_SHIFT + 8
 EDGE = 16
+SPOT = 4
 BATCH = 2
 FAR = -3.0e38
 
@@ -38,6 +39,11 @@
 def columns_of(count, width, start):
     picked = iota((count, width), 0) + start == iota((count, width), 1)
     return picked.astype(jnp.bfloat16)
+
+
+def on_spot(count, width):
+    row = iota((count, width), 0)
+    return (row >= SPOT) & (row < SPOT + 2)
 
 
 def lane_order(half, rows, side):
@@ -94,27 +100,27 @@
     views, half, rows, width = own_ref.shape
     lanes = part_ref.shape[1]
     role, order, *_ = position()
-    pick_ref[...] = columns_of(LEAD, width, edge_start(role, width, LEAD))
+    pick = columns_of(LEAD, width, edge_start(role, width, LEAD))
+    pick_ref[...] = jnp.where(on_spot(LEAD, width), 0.0, pick.astype(jnp.float32)).astype(jnp.bfloat16)
     own_order_ref[...] = lane_order(half, rows, order)
     other_order_ref[...] = lane_order(half, rows, 1 - order)
-    few = columns_of(EDGE, width, edge_start(role, width, EDGE))
+    few = columns_of(EDGE, width, edge_start(role, width, 2) - SPOT).astype(jnp.float32)
+    few = jnp.where(on_spot(EDGE, width), few, 0.0).astype(jnp.bfloat16)
     copies[0].wait()
     for i, pair in enumerate(turned_half(own_ref, pick_ref[...], own_order_ref[...])):
         at = 2 * i * LEAD
         part_ref[at : at + 2 * LEAD] = stacked(pair, lanes).astype(jnp.bfloat16)
     for copy in copies[1:]:
         copy.wait()
-    part_ref[views * LEAD :] = turned_ref(ref_ref, few).astype(jnp.bfloat16)
+    part_ref[0:EDGE] = part_ref[0:EDGE] + turned_ref(ref_ref, few).astype(jnp.bfloat16)
 
 
 def pack_other_body(part_ref, pick_ref, other_order_ref, other_ref, packet_ref):
-    views = other_ref.shape[0]
     lanes = packet_ref.shape[1]
     for i, pair in enumerate(turned_half(other_ref, pick_ref[...], other_order_ref[...])):
         at = 2 * i * LEAD
         both = part_ref[at : at + 2 * LEAD].astype(jnp.float32) + stacked(pair, lanes)
         packet_ref[at : at + 2 * LEAD] = both.astype(jnp.bfloat16)
-    packet_ref[views * LEAD :] = part_ref[views * LEAD :]
 
 
 def lane_table(values_ref, rows, lane):
@@ -488,9 +494,10 @@
             src[v + k, 0:LEAD] = pair[k * LEAD : (k + 1) * LEAD]
             src[v + k, LEAD : LEAD + width] = cols_ref[v + k].astype(jnp.float32)
             src[v + k, LEAD + width :] = ends[k * LEAD : k * LEAD + EDGE]
-    wide[0:EDGE] = left[views * LEAD :].astype(jnp.float32)
+    wide[EDGE - 8 : EDGE] = pltpu.roll(left[0:EDGE].astype(jnp.float32)[0:8], 6 - SPOT, 0)
     wide[EDGE : EDGE + width] = ref_cols_ref[...].astype(jnp.float32)
-    wide[EDGE + width :] = jnp.where(is_last_tile, 0.0, right[views * LEAD :].astype(jnp.float32))
+    ends = pltpu.roll(right[0:EDGE].astype(jnp.float32)[0:8], 8 - SPOT, 0)
+    wide[EDGE + width : EDGE + width + 8] = jnp.where(is_last_tile, 0.0, ends)
     main = MAX_SHIFT + 8
     tall = main + 8
     none = jnp.zeros((1, match.shape[1]), jnp.float32)
@@ -558,7 +565,7 @@
         half = full.shape[1] // 2
         own, other = full[:, :half], full[:, half:]
 
-    packet_shape = shape((views * LEAD + EDGE, lanes), bf16)
+    packet_shape = shape((views * LEAD, lanes), bf16)
     order_shape = shape((lanes, 2 * lanes), bf16)
     staged = (own, ref_feat, shifts, bias_one, bias_two, view_head)
     *staged, part, pick, own_order, other_order = pl.pallas_call(

time: 13.9 us -> 13.9 us (level)
  no operation moved by 1% of the time
where the time goes in v11:
time: 13.9 us; the launch traced here: 13.7 us
  Pallas kernels  7.89 us (57%)
  starting transfers between devices  4.31 us (31%)
  waiting for transfers between devices  1.03 us (7%)
  local copies, waits for them, and re-layouts  0.39 us (3%)
    pallas_call x1, Pallas kernels, per_device(): pl.pallas_call(outer_body, out_shape=shape((GROUPS, planes, rows, width),...  3 us
    pallas_call x1, Pallas kernels, per_device(): pl.pallas_call(inner_body, out_shape=[shape((views, width, lanes), bf16),...  2.22 us
    ppermute x3, starting transfers between devices, swap_planes(): return lax.ppermute(value, 'plane', [(0, 1), (1, 0)])  2.21 us
    ppermute x1, starting transfers between devices, per_device(): got = lax.ppermute(packet, ('tile', 'plane'), pairs)  2.11 us
    pallas_call x1, Pallas kernels, per_device(): pl.pallas_call(pack_own_body, out_shape=[shape(x.shape, x.dtype) for x in...  1.61 us
    ppermute x3, waiting for transfers between devices, swap_planes(): return lax.ppermute(value, 'plane', [(0, 1), (1, 0)])  1.02 us
    pallas_call x1, Pallas kernels, per_device(): pl.pallas_call(late_body, out_shape=shape((late_rows, out_lanes), bf16),...  0.69 us
    pallas_call x1, Pallas kernels, per_device(): pl.pallas_call(pack_other_body, out_shape=packet_shape, in_specs=[whole(v...  0.38 us
  transfers between devices with their start and end apart: 4, of which 2 were waited for; matrix products, arithmetic and copies ran while one was open for 3% of the time, Pallas kernels for 33%

profile of v11, /device:TPU:25, one launch (start us, length us, event | category | flops | bytes accessed | tf_op | source)
XLA Modules:
  0.0 13.7 jit_solution(5533230412844749379)
XLA Ops:
  0.0 0.7 %collective-permute-start = (bf16[4,16,4,256]{3,2,1,0:T(4,128)(2,1)}, bf16[4,16,4,256]{3,2,1,0:T(4,128)(2,1)S(1)}, u32[]{:S(2)}, u32[]{:S(2)}) collective-permute-start(bf16[4,16,4,256]{3,2,1,0:T(4,128)(2,1)} %refs_0_.1), channel_id=1, source_target_pairs={{0,1},{1,0},{2,3},{3,2},{4,5},{5,4},{6,7},{7,6},{8,9},{9,8},{10,11... | collective-permute-start | bytes 393224 | tf_op jit(solution)/shard_map/ppermute | solution.py:550
  0.7 1.6 %pack_own.1 = (bf16[4,16,4,256]{3,2,1,0:T(4,128)(2,1)S(1)}, bf16[32,4,256]{2,1,0:T(4,128)(2,1)S(1)}, s32[4,8]{1,0:T(4,128)S(1)}, f32[8]{0:T(128)S(1)}, f32[8]{0:...) custom-call(bf16[4,16,4,256]{3,2,1,0:T(4,128)(2,1)} %refs_0_.1, ...), custom_call_target="tpu_custom_call" | custom-call | tf_op jit(solution)/shard_map/pack_own/pallas_call | solution.py:571
  2.3 0.0 collective-permute-done.other_ref
  2.3 0.0 copy-start
  2.3 0.0 copy-start.1
  2.3 0.4 %pack_other.1 = bf16[544,128]{1,0:T(8,128)(2,1)S(1)} custom-call(bf16[544,128]{1,0:T(8,128)(2,1)S(1)} %get-tuple-element.43.part_ref, bf16[136,256]{1,0:T(8,128)(2,1)S(1)} %get-tuple-element.44.pick_ref, bf16[128,256]{1,0:T(8,128)(2,1)S(1)} %get-tuple-element.45.other_order_ref, bf16[4,16,4,256]{3,2,1,0:T(4,128)(2,1)S(1)} %collective-permute-done.other_ref), custom_call_target="tpu_custom_call" | custom-call | tf_op jit(solution)/shard_map/pack_other/pallas_call | solution.py:582
  2.7 2.1 %collective-permute-start.1 = (bf16[544,128]{1,0:T(8,128)(2,1)S(1)}, bf16[544,128]{1,0:T(8,128)(2,1)S(1)}, u32[]{:S(2)}, u32[]{:S(2)}) collective-permute-start(bf16[544,128]{1,0:T(8,128)(2,1)S(1)} %pack_other.1), channel_id=1, source_target_pairs={{0,2},{2,4},{4,6},{6,8},{8,10},{10,12},{12,14},{14,16},{16,18},{18... | collective-permute-start | bytes 417800 | tf_op jit(solution)/shard_map/ppermute | solution.py:594
  4.8 0.0 collective-permute-start.2
  4.8 0.0 copy-done
  4.8 0.0 copy-done.1
  4.9 0.1 stack_reshape.7
  5.0 0.1 stack_reshape.6
  5.2 0.1 copy.17.taps_ref
  5.3 0.7 %collective-permute-done.2.before.after = s32[4,8]{1,0:T(4,128)S(1)} collective-permute-done((s32[4,8]{1,0:T(4,128)S(1)}, s32[4,8]{1,0:T(4,128)S(1)}, u32[]{:S(2)}, u32[]{:S(2)}) %collective-permute-start.2) | collective-permute-done | bytes 160 | tf_op jit(solution)/shard_map/ppermute | solution.py:550
  6.0 2.2 %inner_columns.1 = (bf16[4,256,128]{2,1,0:T(8,128)(2,1)S(1)}, bf16[256,128]{1,0:T(8,128)(2,1)S(1)}, s32[8,128]{1,0:T(8,128)S(1)}, f32[8,384]{1,0:T(8,128)S(1)}, ...) custom-call(s32[4,8]{1,0:T(4,128)S(1)} %get-tuple-element.48.shifts,, ...), custom_call_target="tpu_custom_call" | custom-call | flops 3000000000 | bytes 1000000 | tf_op jit(solution)/shard_map/inner_columns/pallas_call | solution.py:614
  8.2 0.0 collective-permute-done.1.got_ref
  8.2 1.5 %collective-permute-start.3 = (bf16[544,128]{1,0:T(8,128)(2,1)S(1)}, bf16[544,128]{1,0:T(8,128)(2,1)S(1)}, u32[]{:S(2)}, u32[]{:S(2)}) collective-permute-start(bf16[544,128]{1,0:T(8,128)(2,1)S(1)} %collective-permute-done.1.got_ref), channel_id=1, source_target_pairs={{0,1},{1,0},{2,3},{3,2},{4,5},{5,4},{6,7},{7,6},{8,9},{9,8},{10,11... | collective-permute-start | bytes 417800 | tf_op jit(solution)/shard_map/ppermute | solution.py:550
  9.7 0.7 %late_columns.1.late_ref = bf16[128,256]{1,0:T(8,128)(2,1)S(1)} custom-call(f32[552,384]{1,0:T(8,128)S(1)} %get-tuple-element.78.match, f32[552,384]{1,0:T(8,128)S(1)} %get-tuple-element.79.first, f32[8,384]{1,0:T(8,128)S(1)} %get-tuple-element.72.table_ref, bf16[256,256]{1,0:T(8,128)(2,1)S(1)} %get-tuple-element.73.spread_ref, ...), custom_call_target="tpu_custom_call" | custom-call | flops 2000000000 | bytes 1000000 | tf_op jit(solution)/shard_map/late_columns/pallas_call | solution.py:660
  10.4 0.3 %collective-permute-done.3.swapped_ref = bf16[544,128]{1,0:T(8,128)(2,1)S(1)} collective-permute-done((bf16[544,128]{1,0:T(8,128)(2,1)S(1)}, bf16[544,128]{1,0:T(8,128)(2,1)S(1)}, u32[]{:S(2)}, u32[]{:S(2)}) %collective-permute-start.3) | collective-permute-done | bytes 139296 | tf_op jit(solution)/shard_map/ppermute | solution.py:550
  10.7 3.0 %outer_columns.1 = bf16[8,8,4,256]{3,2,1,0:T(4,128)(2,1)} custom-call(bf16[4,256,128]{2,1,0:T(8,128)(2,1)S(1)} %get-tuple-element.69.cols_ref, bf16[256,128]{1,0:T(8,128)(2,1)S(1)} %get-tuple-element.70.ref_cols_ref, s32[8,128]{1,0:T(8,128)S(1)} %get-tuple-element.71.word_ref, f32[8,384]{1,0:T(8,128)S(1)} %get-tuple-element.72.table_ref, ...), custom_call_target="tpu_custom_call" | custom-call | tf_op jit(solution)/shard_map/outer_columns/pallas_call | solution.py:672
  (4 shorter events, 0.1 us)
Async XLA Ops:
  0.0 2.3 %collective-permute-start = (bf16[4,16,4,256]{3,2,1,0:T(4,128)(2,1)}, bf16[4,16,4,256]{3,2,1,0:T(4,128)(2,1)S(1)}, u32[]{:S(2)}, u32[]{:S(2)}) collective-permute-start(bf16[4,16,4,256]{3,2,1,0:T(4,128)(2,1)} %refs_0_.1), channel_id=1, source_target_pairs={{0,1},{1,0},{2,3},{3,2},{4,5},{5,4},{6,7},{7,6},{8,9},{9,8},{10,11... | collective-permute-start | bytes 393224 | tf_op jit(solution)/shard_map/ppermute | solution.py:550
  2.3 2.5 %copy-start = (bf16[8,8,3,3,3]{1,0,4,3,2:T(8,128)(2,1)S(1)}, bf16[8,8,3,3,3]{1,0,4,3,2:T(8,128)(2,1)}, u32[]{:S(2)}) copy-start(bf16[8,8,3,3,3]{1,0,4,3,2:T(8,128)(2,1)} %param.13) | copy-start | bytes 10372
  2.3 2.5 %copy-start.1 = (bf16[8,8,3,3,3]{1,0,4,3,2:T(8,128)(2,1)S(1)}, bf16[8,8,3,3,3]{1,0,4,3,2:T(8,128)(2,1)}, u32[]{:S(2)}) copy-start(bf16[8,8,3,3,3]{1,0,4,3,2:T(8,128)(2,1)} %param.11) | copy-start | bytes 10372
  2.7 5.5 %collective-permute-start.1 = (bf16[544,128]{1,0:T(8,128)(2,1)S(1)}, bf16[544,128]{1,0:T(8,128)(2,1)S(1)}, u32[]{:S(2)}, u32[]{:S(2)}) collective-permute-start(bf16[544,128]{1,0:T(8,128)(2,1)S(1)} %pack_other.1), channel_id=1, source_target_pairs={{0,2},{2,4},{4,6},{6,8},{8,10},{10,12},{12,14},{14,16},{16,18},{18... | collective-permute-start | bytes 417800 | tf_op jit(solution)/shard_map/ppermute | solution.py:594
  4.8 1.2 %collective-permute-start.2 = (s32[4,8]{1,0:T(4,128)S(1)}, s32[4,8]{1,0:T(4,128)S(1)}, u32[]{:S(2)}, u32[]{:S(2)}) collective-permute-start(s32[4,8]{1,0:T(4,128)S(1)} %get-tuple-element.48.shifts), channel_id=1, source_target_pairs={{0,1},{1,0},{2,3},{3,2},{4,5},{5,4},{6,7},{7,6},{8,9},{9,8},{10,11... | collective-permute-start | bytes 392 | tf_op jit(solution)/shard_map/ppermute | solution.py:550
  8.2 2.5 %collective-permute-start.3 = (bf16[544,128]{1,0:T(8,128)(2,1)S(1)}, bf16[544,128]{1,0:T(8,128)(2,1)S(1)}, u32[]{:S(2)}, u32[]{:S(2)}) collective-permute-start(bf16[544,128]{1,0:T(8,128)(2,1)S(1)} %collective-permute-done.1.got_ref), channel_id=1, source_target_pairs={{0,1},{1,0},{2,3},{3,2},{4,5},{5,4},{6,7},{7,6},{8,9},{9,8},{10,11... | collective-permute-start | bytes 417800 | tf_op jit(solution)/shard_map/ppermute | solution.py:550

commit v12 on v10

--- a/solution.py
+++ b/solution.py
@@ -38,6 +38,23 @@
 def columns_of(count, width, start):
     picked = iota((count, width), 0) + start == iota((count, width), 1)
     return picked.astype(jnp.bfloat16)
+
+
+def edge_columns(width, role):
+    row = iota((LEAD, width), 0)
+    base = edge_start(role, width, MAX_SHIFT)
+    column = jnp.where(row < MAX_SHIFT, base + row, base - 4 + row % 4)
+    column = jnp.where((row >= MAX_SHIFT) & (row % 4 < 2), -1, column)
+    return (column == iota((LEAD, width), 1)).astype(jnp.bfloat16)
+
+
+def laid_out(pairs, lanes):
+    blocks, tails = [], []
+    for pair in pairs:
+        a, b = pair[:, 0:lanes], pair[:, lanes:]
+        blocks += [a[0:MAX_SHIFT], b[0:MAX_SHIFT]]
+        tails.append(jnp.where(iota((8, lanes), 0) < 4, a[MAX_SHIFT:], b[MAX_SHIFT:]))
+    return blocks, jnp.concatenate(tails, axis=0)
 
 
 def lane_order(half, rows, side):
@@ -74,10 +91,6 @@
 
 def edge_start(role, width, count):
     return jnp.where(role == 0, width - count, 0)
-
-
-def stacked(pair, lanes):
-    return jnp.concatenate([pair[:, 0:lanes], pair[:, lanes:]], axis=0)
 
 
 def pack_own_body(*refs):
@@ -94,27 +107,32 @@
     views, half, rows, width = own_ref.shape
     lanes = part_ref.shape[1]
     role, order, *_ = position()
-    pick_ref[...] = columns_of(LEAD, width, edge_start(role, width, LEAD))
+    pick_ref[...] = edge_columns(width, role)
     own_order_ref[...] = lane_order(half, rows, order)
     other_order_ref[...] = lane_order(half, rows, 1 - order)
-    few = columns_of(EDGE, width, edge_start(role, width, EDGE))
+    few = columns_of(EDGE, width, edge_start(role, width, 2)).astype(jnp.float32)
+    few = jnp.where(iota((EDGE, width), 0) < 2, few, 0.0).astype(jnp.bfloat16)
     copies[0].wait()
-    for i, pair in enumerate(turned_half(own_ref, pick_ref[...], own_order_ref[...])):
-        at = 2 * i * LEAD
-        part_ref[at : at + 2 * LEAD] = stacked(pair, lanes).astype(jnp.bfloat16)
+    pairs = turned_half(own_ref, pick_ref[...], own_order_ref[...])
+    blocks, tails = laid_out(pairs, lanes)
+    for v, block in enumerate(blocks):
+        part_ref[v * MAX_SHIFT : (v + 1) * MAX_SHIFT] = block.astype(jnp.bfloat16)
     for copy in copies[1:]:
         copy.wait()
-    part_ref[views * LEAD :] = turned_ref(ref_ref, few).astype(jnp.bfloat16)
+    extra = turned_ref(ref_ref, few)[0:8]
+    tails = jnp.concatenate([tails[0:8] + extra, tails[8:]], axis=0)
+    part_ref[views * MAX_SHIFT :] = tails.astype(jnp.bfloat16)
 
 
 def pack_other_body(part_ref, pick_ref, other_order_ref, other_ref, packet_ref):
-    views = other_ref.shape[0]
     lanes = packet_ref.shape[1]
-    for i, pair in enumerate(turned_half(other_ref, pick_ref[...], other_order_ref[...])):
-        at = 2 * i * LEAD
-        both = part_ref[at : at + 2 * LEAD].astype(jnp.float32) + stacked(pair, lanes)
-        packet_ref[at : at + 2 * LEAD] = both.astype(jnp.bfloat16)
-    packet_ref[views * LEAD :] = part_ref[views * LEAD :]
+    pairs = turned_half(other_ref, pick_ref[...], other_order_ref[...])
+    blocks, tails = laid_out(pairs, lanes)
+    for v, block in enumerate(blocks):
+        rows = pl.ds(v * MAX_SHIFT, MAX_SHIFT)
+        packet_ref[rows] = (part_ref[rows].astype(jnp.float32) + block).astype(jnp.bfloat16)
+    at = len(blocks) * MAX_SHIFT
+    packet_ref[at:] = (part_ref[at:].astype(jnp.float32) + tails).astype(jnp.bfloat16)
 
 
 def lane_table(values_ref, rows, lane):
@@ -480,17 +498,18 @@
     left = jnp.where(order == 0, got_ref[...], swapped_ref[...])
     left = jnp.where(is_first_tile, jnp.zeros_like(left), left)
     right = jnp.where(order == 0, swapped_ref[...], got_ref[...])
-    for v in range(0, views, 2):
-        at = v * LEAD
-        pair = left[at : at + 2 * LEAD].astype(jnp.float32)
-        ends = right[at : at + LEAD + 24].astype(jnp.float32)
-        for k in range(2):
-            src[v + k, 0:LEAD] = pair[k * LEAD : (k + 1) * LEAD]
-            src[v + k, LEAD : LEAD + width] = cols_ref[v + k].astype(jnp.float32)
-            src[v + k, LEAD + width :] = ends[k * LEAD : k * LEAD + EDGE]
-    wide[0:EDGE] = left[views * LEAD :].astype(jnp.float32)
+    left_tails = left[views * MAX_SHIFT :].astype(jnp.float32)
+    right_tails = right[views * MAX_SHIFT :].astype(jnp.float32)
+    for v in range(views):
+        at = v * MAX_SHIFT
+        tail = left_tails[v // 2 * 8 : v // 2 * 8 + 8]
+        src[v, 0:8] = tail if v % 2 else pltpu.roll(tail, 4, 0)
+        src[v, 8:LEAD] = left[at : at + MAX_SHIFT].astype(jnp.float32)
+        src[v, LEAD : LEAD + width] = cols_ref[v].astype(jnp.float32)
+        src[v, LEAD + width :] = right[at : at + EDGE].astype(jnp.float32)
+    wide[EDGE - 8 : EDGE] = pltpu.roll(left_tails[0:8], 6, 0)
     wide[EDGE : EDGE + width] = ref_cols_ref[...].astype(jnp.float32)
-    wide[EDGE + width :] = jnp.where(is_last_tile, 0.0, right[views * LEAD :].astype(jnp.float32))
+    wide[EDGE + width : EDGE + width + 8] = jnp.where(is_last_tile, 0.0, right_tails[0:8])
     main = MAX_SHIFT + 8
     tall = main + 8
     none = jnp.zeros((1, match.shape[1]), jnp.float32)
@@ -558,7 +577,7 @@
         half = full.shape[1] // 2
         own, other = full[:, :half], full[:, half:]
 
-    packet_shape = shape((views * LEAD + EDGE, lanes), bf16)
+    packet_shape = shape((views * MAX_SHIFT + views * 4, lanes), bf16)
     order_shape = shape((lanes, 2 * lanes), bf16)
     staged = (own, ref_feat, shifts, bias_one, bias_two, view_head)
     *staged, part, pick, own_order, other_order = pl.pallas_call(

time: 13.9 us -> 13.8 us (level)
  no operation moved by 1% of the time
where the time goes in v12:
time: 13.8 us; the launch traced here: 13.7 us
  Pallas kernels  7.92 us (57%)
  starting transfers between devices  4.27 us (31%)
  waiting for transfers between devices  1 us (7%)
  local copies, waits for them, and re-layouts  0.39 us (3%)
    pallas_call x1, Pallas kernels, per_device(): pl.pallas_call(outer_body, out_shape=shape((GROUPS, planes, rows, width),...  3.02 us
    pallas_call x1, Pallas kernels, per_device(): pl.pallas_call(inner_body, out_shape=[shape((views, width, lanes), bf16),...  2.21 us
    ppermute x3, starting transfers between devices, swap_planes(): return lax.ppermute(value, 'plane', [(0, 1), (1, 0)])  2.17 us
    ppermute x1, starting transfers between devices, per_device(): got = lax.ppermute(packet, ('tile', 'plane'), pairs)  2.11 us
    pallas_call x1, Pallas kernels, per_device(): pl.pallas_call(pack_own_body, out_shape=[shape(x.shape, x.dtype) for x in...  1.61 us
    ppermute x3, waiting for transfers between devices, swap_planes(): return lax.ppermute(value, 'plane', [(0, 1), (1, 0)])  1 us
    pallas_call x1, Pallas kernels, per_device(): pl.pallas_call(late_body, out_shape=shape((late_rows, out_lanes), bf16),...  0.71 us
    pallas_call x1, Pallas kernels, per_device(): pl.pallas_call(pack_other_body, out_shape=packet_shape, in_specs=[whole(v...  0.38 us
  transfers between devices with their start and end apart: 4, of which 2 were waited for; matrix products, arithmetic and copies ran while one was open for 3% of the time, Pallas kernels for 33%

profile of v12, /device:TPU:25, one launch (start us, length us, event | category | flops | bytes accessed | tf_op | source)
XLA Modules:
  0.0 13.7 jit_solution(1363444554458434173)
XLA Ops:
  0.0 0.7 %collective-permute-start = (bf16[4,16,4,256]{3,2,1,0:T(4,128)(2,1)}, bf16[4,16,4,256]{3,2,1,0:T(4,128)(2,1)S(1)}, u32[]{:S(2)}, u32[]{:S(2)}) collective-permute-start(bf16[4,16,4,256]{3,2,1,0:T(4,128)(2,1)} %refs_0_.1), channel_id=1, source_target_pairs={{0,1},{1,0},{2,3},{3,2},{4,5},{5,4},{6,7},{7,6},{8,9},{9,8},{10,11... | collective-permute-start | bytes 393224 | tf_op jit(solution)/shard_map/ppermute | solution.py:562
  0.7 1.6 %pack_own.1 = (bf16[4,16,4,256]{3,2,1,0:T(4,128)(2,1)S(1)}, bf16[32,4,256]{2,1,0:T(4,128)(2,1)S(1)}, s32[4,8]{1,0:T(4,128)S(1)}, f32[8]{0:T(128)S(1)}, f32[8]{0:...) custom-call(bf16[4,16,4,256]{3,2,1,0:T(4,128)(2,1)} %refs_0_.1, ...), custom_call_target="tpu_custom_call" | custom-call | tf_op jit(solution)/shard_map/pack_own/pallas_call | solution.py:583
  2.3 0.0 collective-permute-done.other_ref
  2.3 0.0 copy-start
  2.3 0.0 copy-start.1
  2.3 0.4 %pack_other.1 = bf16[528,128]{1,0:T(8,128)(2,1)S(1)} custom-call(bf16[528,128]{1,0:T(8,128)(2,1)S(1)} %get-tuple-element.43.part_ref, bf16[136,256]{1,0:T(8,128)(2,1)S(1)} %get-tuple-element.44.pick_ref, bf16[128,256]{1,0:T(8,128)(2,1)S(1)} %get-tuple-element.45.other_order_ref, bf16[4,16,4,256]{3,2,1,0:T(4,128)(2,1)S(1)} %collective-permute-done.other_ref), custom_call_target="tpu_custom_call" | custom-call | tf_op jit(solution)/shard_map/pack_other/pallas_call | solution.py:594
  2.7 2.1 %collective-permute-start.1 = (bf16[528,128]{1,0:T(8,128)(2,1)S(1)}, bf16[528,128]{1,0:T(8,128)(2,1)S(1)}, u32[]{:S(2)}, u32[]{:S(2)}) collective-permute-start(bf16[528,128]{1,0:T(8,128)(2,1)S(1)} %pack_other.1), channel_id=1, source_target_pairs={{0,2},{2,4},{4,6},{6,8},{8,10},{10,12},{12,14},{14,16},{16,18},{18... | collective-permute-start | bytes 405512 | tf_op jit(solution)/shard_map/ppermute | solution.py:606
  4.8 0.0 collective-permute-start.2
  4.8 0.0 copy-done
  4.8 0.0 copy-done.1
  4.9 0.1 stack_reshape.7
  5.0 0.1 stack_reshape.6
  5.1 0.1 copy.17.taps_ref
  5.3 0.7 %collective-permute-done.2.before.after = s32[4,8]{1,0:T(4,128)S(1)} collective-permute-done((s32[4,8]{1,0:T(4,128)S(1)}, s32[4,8]{1,0:T(4,128)S(1)}, u32[]{:S(2)}, u32[]{:S(2)}) %collective-permute-start.2) | collective-permute-done | bytes 160 | tf_op jit(solution)/shard_map/ppermute | solution.py:562
  6.0 2.2 %inner_columns.1 = (bf16[4,256,128]{2,1,0:T(8,128)(2,1)S(1)}, bf16[256,128]{1,0:T(8,128)(2,1)S(1)}, s32[8,128]{1,0:T(8,128)S(1)}, f32[8,384]{1,0:T(8,128)S(1)}, ...) custom-call(s32[4,8]{1,0:T(4,128)S(1)} %get-tuple-element.48.shifts,, ...), custom_call_target="tpu_custom_call" | custom-call | flops 3000000000 | bytes 1000000 | tf_op jit(solution)/shard_map/inner_columns/pallas_call | solution.py:626
  8.2 0.0 collective-permute-done.1.got_ref
  8.2 1.5 %collective-permute-start.3 = (bf16[528,128]{1,0:T(8,128)(2,1)S(1)}, bf16[528,128]{1,0:T(8,128)(2,1)S(1)}, u32[]{:S(2)}, u32[]{:S(2)}) collective-permute-start(bf16[528,128]{1,0:T(8,128)(2,1)S(1)} %collective-permute-done.1.got_ref), channel_id=1, source_target_pairs={{0,1},{1,0},{2,3},{3,2},{4,5},{5,4},{6,7},{7,6},{8,9},{9,8},{10,11... | collective-permute-start | bytes 405512 | tf_op jit(solution)/shard_map/ppermute | solution.py:562
  9.7 0.7 %late_columns.1.late_ref = bf16[128,256]{1,0:T(8,128)(2,1)S(1)} custom-call(f32[552,384]{1,0:T(8,128)S(1)} %get-tuple-element.78.match, f32[552,384]{1,0:T(8,128)S(1)} %get-tuple-element.79.first, f32[8,384]{1,0:T(8,128)S(1)} %get-tuple-element.72.table_ref, bf16[256,256]{1,0:T(8,128)(2,1)S(1)} %get-tuple-element.73.spread_ref, ...), custom_call_target="tpu_custom_call" | custom-call | flops 2000000000 | bytes 1000000 | tf_op jit(solution)/shard_map/late_columns/pallas_call | solution.py:672
  10.4 0.3 %collective-permute-done.3.swapped_ref = bf16[528,128]{1,0:T(8,128)(2,1)S(1)} collective-permute-done((bf16[528,128]{1,0:T(8,128)(2,1)S(1)}, bf16[528,128]{1,0:T(8,128)(2,1)S(1)}, u32[]{:S(2)}, u32[]{:S(2)}) %collective-permute-start.3) | collective-permute-done | bytes 135200 | tf_op jit(solution)/shard_map/ppermute | solution.py:562
  10.7 3.0 %outer_columns.1 = bf16[8,8,4,256]{3,2,1,0:T(4,128)(2,1)} custom-call(bf16[4,256,128]{2,1,0:T(8,128)(2,1)S(1)} %get-tuple-element.69.cols_ref, bf16[256,128]{1,0:T(8,128)(2,1)S(1)} %get-tuple-element.70.ref_cols_ref, s32[8,128]{1,0:T(8,128)S(1)} %get-tuple-element.71.word_ref, f32[8,384]{1,0:T(8,128)S(1)} %get-tuple-element.72.table_ref, ...), custom_call_target="tpu_custom_call" | custom-call | tf_op jit(solution)/shard_map/outer_columns/pallas_call | solution.py:684
  (4 shorter events, 0.1 us)
Async XLA Ops:
  0.0 2.3 %collective-permute-start = (bf16[4,16,4,256]{3,2,1,0:T(4,128)(2,1)}, bf16[4,16,4,256]{3,2,1,0:T(4,128)(2,1)S(1)}, u32[]{:S(2)}, u32[]{:S(2)}) collective-permute-start(bf16[4,16,4,256]{3,2,1,0:T(4,128)(2,1)} %refs_0_.1), channel_id=1, source_target_pairs={{0,1},{1,0},{2,3},{3,2},{4,5},{5,4},{6,7},{7,6},{8,9},{9,8},{10,11... | collective-permute-start | bytes 393224 | tf_op jit(solution)/shard_map/ppermute | solution.py:562
  2.3 2.5 %copy-start = (bf16[8,8,3,3,3]{1,0,4,3,2:T(8,128)(2,1)S(1)}, bf16[8,8,3,3,3]{1,0,4,3,2:T(8,128)(2,1)}, u32[]{:S(2)}) copy-start(bf16[8,8,3,3,3]{1,0,4,3,2:T(8,128)(2,1)} %param.13) | copy-start | bytes 10372
  2.3 2.5 %copy-start.1 = (bf16[8,8,3,3,3]{1,0,4,3,2:T(8,128)(2,1)S(1)}, bf16[8,8,3,3,3]{1,0,4,3,2:T(8,128)(2,1)}, u32[]{:S(2)}) copy-start(bf16[8,8,3,3,3]{1,0,4,3,2:T(8,128)(2,1)} %param.11) | copy-start | bytes 10372
  2.7 5.5 %collective-permute-start.1 = (bf16[528,128]{1,0:T(8,128)(2,1)S(1)}, bf16[528,128]{1,0:T(8,128)(2,1)S(1)}, u32[]{:S(2)}, u32[]{:S(2)}) collective-permute-start(bf16[528,128]{1,0:T(8,128)(2,1)S(1)} %pack_other.1), channel_id=1, source_target_pairs={{0,2},{2,4},{4,6},{6,8},{8,10},{10,12},{12,14},{14,16},{16,18},{18... | collective-permute-start | bytes 405512 | tf_op jit(solution)/shard_map/ppermute | solution.py:606
  4.8 1.2 %collective-permute-start.2 = (s32[4,8]{1,0:T(4,128)S(1)}, s32[4,8]{1,0:T(4,128)S(1)}, u32[]{:S(2)}, u32[]{:S(2)}) collective-permute-start(s32[4,8]{1,0:T(4,128)S(1)} %get-tuple-element.48.shifts), channel_id=1, source_target_pairs={{0,1},{1,0},{2,3},{3,2},{4,5},{5,4},{6,7},{7,6},{8,9},{9,8},{10,11... | collective-permute-start | bytes 392 | tf_op jit(solution)/shard_map/ppermute | solution.py:562
  8.2 2.5 %collective-permute-start.3 = (bf16[528,128]{1,0:T(8,128)(2,1)S(1)}, bf16[528,128]{1,0:T(8,128)(2,1)S(1)}, u32[]{:S(2)}, u32[]{:S(2)}) collective-permute-start(bf16[528,128]{1,0:T(8,128)(2,1)S(1)} %collective-permute-done.1.got_ref), channel_id=1, source_target_pairs={{0,1},{1,0},{2,3},{3,2},{4,5},{5,4},{6,7},{7,6},{8,9},{9,8},{10,11... | collective-permute-start | bytes 405512 | tf_op jit(solution)/shard_map/ppermute | solution.py:562

commit v13 on v12

--- a/solution.py
+++ b/solution.py
@@ -9,7 +9,7 @@
 MAX_SHIFT = 128
 LEAD = MAX_SHIFT + 8
 EDGE = 16
-BATCH = 2
+BATCH = 1
 FAR = -3.0e38
 
 
@@ -40,11 +40,11 @@
     return picked.astype(jnp.bfloat16)
 
 
-def edge_columns(width, role):
+def edge_columns(width, role, dropped):
     row = iota((LEAD, width), 0)
     base = edge_start(role, width, MAX_SHIFT)
     column = jnp.where(row < MAX_SHIFT, base + row, base - 4 + row % 4)
-    column = jnp.where((row >= MAX_SHIFT) & (row % 4 < 2), -1, column)
+    column = jnp.where(((row >= MAX_SHIFT) & (row % 4 < 2)) | dropped, -1, column)
     return (column == iota((LEAD, width), 1)).astype(jnp.bfloat16)
 
 
@@ -106,12 +106,14 @@
     own_ref, ref_ref = targets[:2]
     views, half, rows, width = own_ref.shape
     lanes = part_ref.shape[1]
-    role, order, *_ = position()
-    pick_ref[...] = edge_columns(width, role)
+    role, order, is_first_tile, is_last_tile, *_ = position()
+    dropped = (is_first_tile & (role != 0)) | (is_last_tile & (role == 0))
+    pick_ref[...] = edge_columns(width, role, dropped)
     own_order_ref[...] = lane_order(half, rows, order)
     other_order_ref[...] = lane_order(half, rows, 1 - order)
     few = columns_of(EDGE, width, edge_start(role, width, 2)).astype(jnp.float32)
-    few = jnp.where(iota((EDGE, width), 0) < 2, few, 0.0).astype(jnp.bfloat16)
+    kept = (iota((EDGE, width), 0) < 2) & ~dropped
+    few = jnp.where(kept, few, 0.0).astype(jnp.bfloat16)
     copies[0].wait()
     pairs = turned_half(own_ref, pick_ref[...], own_order_ref[...])
     blocks, tails = laid_out(pairs, lanes)
@@ -496,7 +498,6 @@
 
     near = read_shifts(views, planes, word_ref)
     left = jnp.where(order == 0, got_ref[...], swapped_ref[...])
-    left = jnp.where(is_first_tile, jnp.zeros_like(left), left)
     right = jnp.where(order == 0, swapped_ref[...], got_ref[...])
     left_tails = left[views * MAX_SHIFT :].astype(jnp.float32)
     right_tails = right[views * MAX_SHIFT :].astype(jnp.float32)
@@ -509,7 +510,7 @@
         src[v, LEAD + width :] = right[at : at + EDGE].astype(jnp.float32)
     wide[EDGE - 8 : EDGE] = pltpu.roll(left_tails[0:8], 6, 0)
     wide[EDGE : EDGE + width] = ref_cols_ref[...].astype(jnp.float32)
-    wide[EDGE + width : EDGE + width + 8] = jnp.where(is_last_tile, 0.0, right_tails[0:8])
+    wide[EDGE + width : EDGE + width + 8] = right_tails[0:8]
     main = MAX_SHIFT + 8
     tall = main + 8
     none = jnp.zeros((1, match.shape[1]), jnp.float32)

time: 13.8 us -> 13.8 us (level)
  no operation moved by 1% of the time
where the time goes in v13:
time: 13.8 us; the launch traced here: 13.6 us
  Pallas kernels  7.87 us (57%)
  starting transfers between devices  4.27 us (31%)
  waiting for transfers between devices  1 us (7%)
  local copies, waits for them, and re-layouts  0.39 us (3%)
    pallas_call x1, Pallas kernels, per_device(): pl.pallas_call(outer_body, out_shape=shape((GROUPS, planes, rows, width),...  2.96 us
    pallas_call x1, Pallas kernels, per_device(): pl.pallas_call(inner_body, out_shape=[shape((views, width, lanes), bf16),...  2.22 us
    ppermute x3, starting transfers between devices, swap_planes(): return lax.ppermute(value, 'plane', [(0, 1), (1, 0)])  2.16 us
    ppermute x1, starting transfers between devices, per_device(): got = lax.ppermute(packet, ('tile', 'plane'), pairs)  2.11 us
    pallas_call x1, Pallas kernels, per_device(): pl.pallas_call(pack_own_body, out_shape=[shape(x.shape, x.dtype) for x in...  1.61 us
    ppermute x3, waiting for transfers between devices, swap_planes(): return lax.ppermute(value, 'plane', [(0, 1), (1, 0)])  1 us
    pallas_call x1, Pallas kernels, per_device(): pl.pallas_call(late_body, out_shape=shape((late_rows, out_lanes), bf16),...  0.71 us
    pallas_call x1, Pallas kernels, per_device(): pl.pallas_call(pack_other_body, out_shape=packet_shape, in_specs=[whole(v...  0.38 us
  transfers between devices with their start and end apart: 4, of which 2 were waited for; matrix products, arithmetic and copies ran while one was open for 3% of the time, Pallas kernels for 33%

profile of v13, /device:TPU:25, one launch (start us, length us, event | category | flops | bytes accessed | tf_op | source)
XLA Modules:
  0.0 13.6 jit_solution(13389265703939335144)
XLA Ops:
  0.0 0.7 %collective-permute-start = (bf16[4,16,4,256]{3,2,1,0:T(4,128)(2,1)}, bf16[4,16,4,256]{3,2,1,0:T(4,128)(2,1)S(1)}, u32[]{:S(2)}, u32[]{:S(2)}) collective-permute-start(bf16[4,16,4,256]{3,2,1,0:T(4,128)(2,1)} %refs_0_.1), channel_id=1, source_target_pairs={{0,1},{1,0},{2,3},{3,2},{4,5},{5,4},{6,7},{7,6},{8,9},{9,8},{10,11... | collective-permute-start | bytes 393224 | tf_op jit(solution)/shard_map/ppermute | solution.py:563
  0.7 1.6 %pack_own.1 = (bf16[4,16,4,256]{3,2,1,0:T(4,128)(2,1)S(1)}, bf16[32,4,256]{2,1,0:T(4,128)(2,1)S(1)}, s32[4,8]{1,0:T(4,128)S(1)}, f32[8]{0:T(128)S(1)}, f32[8]{0:...) custom-call(bf16[4,16,4,256]{3,2,1,0:T(4,128)(2,1)} %refs_0_.1, ...), custom_call_target="tpu_custom_call" | custom-call | tf_op jit(solution)/shard_map/pack_own/pallas_call | solution.py:584
  2.3 0.0 collective-permute-done.other_ref
  2.3 0.0 copy-start
  2.3 0.0 copy-start.1
  2.3 0.4 %pack_other.1 = bf16[528,128]{1,0:T(8,128)(2,1)S(1)} custom-call(bf16[528,128]{1,0:T(8,128)(2,1)S(1)} %get-tuple-element.43.part_ref, bf16[136,256]{1,0:T(8,128)(2,1)S(1)} %get-tuple-element.44.pick_ref, bf16[128,256]{1,0:T(8,128)(2,1)S(1)} %get-tuple-element.45.other_order_ref, bf16[4,16,4,256]{3,2,1,0:T(4,128)(2,1)S(1)} %collective-permute-done.other_ref), custom_call_target="tpu_custom_call" | custom-call | tf_op jit(solution)/shard_map/pack_other/pallas_call | solution.py:595
  2.7 2.1 %collective-permute-start.1 = (bf16[528,128]{1,0:T(8,128)(2,1)S(1)}, bf16[528,128]{1,0:T(8,128)(2,1)S(1)}, u32[]{:S(2)}, u32[]{:S(2)}) collective-permute-start(bf16[528,128]{1,0:T(8,128)(2,1)S(1)} %pack_other.1), channel_id=1, source_target_pairs={{0,2},{2,4},{4,6},{6,8},{8,10},{10,12},{12,14},{14,16},{16,18},{18... | collective-permute-start | bytes 405512 | tf_op jit(solution)/shard_map/ppermute | solution.py:607
  4.8 0.0 collective-permute-start.2
  4.8 0.0 copy-done
  4.8 0.0 copy-done.1
  4.9 0.1 stack_reshape.7
  5.0 0.1 stack_reshape.6
  5.1 0.1 copy.17.taps_ref
  5.3 0.7 %collective-permute-done.2.before.after = s32[4,8]{1,0:T(4,128)S(1)} collective-permute-done((s32[4,8]{1,0:T(4,128)S(1)}, s32[4,8]{1,0:T(4,128)S(1)}, u32[]{:S(2)}, u32[]{:S(2)}) %collective-permute-start.2) | collective-permute-done | bytes 160 | tf_op jit(solution)/shard_map/ppermute | solution.py:563
  6.0 2.2 %inner_columns.1 = (bf16[4,256,128]{2,1,0:T(8,128)(2,1)S(1)}, bf16[256,128]{1,0:T(8,128)(2,1)S(1)}, s32[8,128]{1,0:T(8,128)S(1)}, f32[8,384]{1,0:T(8,128)S(1)}, ...) custom-call(s32[4,8]{1,0:T(4,128)S(1)} %get-tuple-element.48.shifts,, ...), custom_call_target="tpu_custom_call" | custom-call | flops 3000000000 | bytes 1000000 | tf_op jit(solution)/shard_map/inner_columns/pallas_call | solution.py:627
  8.2 0.0 collective-permute-done.1.got_ref
  8.2 1.5 %collective-permute-start.3 = (bf16[528,128]{1,0:T(8,128)(2,1)S(1)}, bf16[528,128]{1,0:T(8,128)(2,1)S(1)}, u32[]{:S(2)}, u32[]{:S(2)}) collective-permute-start(bf16[528,128]{1,0:T(8,128)(2,1)S(1)} %collective-permute-done.1.got_ref), channel_id=1, source_target_pairs={{0,1},{1,0},{2,3},{3,2},{4,5},{5,4},{6,7},{7,6},{8,9},{9,8},{10,11... | collective-permute-start | bytes 405512 | tf_op jit(solution)/shard_map/ppermute | solution.py:563
  9.7 0.7 %late_columns.1.late_ref = bf16[128,256]{1,0:T(8,128)(2,1)S(1)} custom-call(f32[552,384]{1,0:T(8,128)S(1)} %get-tuple-element.78.match, f32[552,384]{1,0:T(8,128)S(1)} %get-tuple-element.79.first, f32[8,384]{1,0:T(8,128)S(1)} %get-tuple-element.72.table_ref, bf16[256,256]{1,0:T(8,128)(2,1)S(1)} %get-tuple-element.73.spread_ref, ...), custom_call_target="tpu_custom_call" | custom-call | flops 2000000000 | bytes 1000000 | tf_op jit(solution)/shard_map/late_columns/pallas_call | solution.py:673
  10.4 0.3 %collective-permute-done.3.swapped_ref = bf16[528,128]{1,0:T(8,128)(2,1)S(1)} collective-permute-done((bf16[528,128]{1,0:T(8,128)(2,1)S(1)}, bf16[528,128]{1,0:T(8,128)(2,1)S(1)}, u32[]{:S(2)}, u32[]{:S(2)}) %collective-permute-start.3) | collective-permute-done | bytes 135200 | tf_op jit(solution)/shard_map/ppermute | solution.py:563
  10.7 3.0 %outer_columns.1 = bf16[8,8,4,256]{3,2,1,0:T(4,128)(2,1)} custom-call(bf16[4,256,128]{2,1,0:T(8,128)(2,1)S(1)} %get-tuple-element.69.cols_ref, bf16[256,128]{1,0:T(8,128)(2,1)S(1)} %get-tuple-element.70.ref_cols_ref, s32[8,128]{1,0:T(8,128)S(1)} %get-tuple-element.71.word_ref, f32[8,384]{1,0:T(8,128)S(1)} %get-tuple-element.72.table_ref, ...), custom_call_target="tpu_custom_call" | custom-call | tf_op jit(solution)/shard_map/outer_columns/pallas_call | solution.py:685
  (4 shorter events, 0.1 us)
Async XLA Ops:
  0.0 2.3 %collective-permute-start = (bf16[4,16,4,256]{3,2,1,0:T(4,128)(2,1)}, bf16[4,16,4,256]{3,2,1,0:T(4,128)(2,1)S(1)}, u32[]{:S(2)}, u32[]{:S(2)}) collective-permute-start(bf16[4,16,4,256]{3,2,1,0:T(4,128)(2,1)} %refs_0_.1), channel_id=1, source_target_pairs={{0,1},{1,0},{2,3},{3,2},{4,5},{5,4},{6,7},{7,6},{8,9},{9,8},{10,11... | collective-permute-start | bytes 393224 | tf_op jit(solution)/shard_map/ppermute | solution.py:563
  2.3 2.5 %copy-start = (bf16[8,8,3,3,3]{1,0,4,3,2:T(8,128)(2,1)S(1)}, bf16[8,8,3,3,3]{1,0,4,3,2:T(8,128)(2,1)}, u32[]{:S(2)}) copy-start(bf16[8,8,3,3,3]{1,0,4,3,2:T(8,128)(2,1)} %param.13) | copy-start | bytes 10372
  2.3 2.5 %copy-start.1 = (bf16[8,8,3,3,3]{1,0,4,3,2:T(8,128)(2,1)S(1)}, bf16[8,8,3,3,3]{1,0,4,3,2:T(8,128)(2,1)}, u32[]{:S(2)}) copy-start(bf16[8,8,3,3,3]{1,0,4,3,2:T(8,128)(2,1)} %param.11) | copy-start | bytes 10372
  2.7 5.5 %collective-permute-start.1 = (bf16[528,128]{1,0:T(8,128)(2,1)S(1)}, bf16[528,128]{1,0:T(8,128)(2,1)S(1)}, u32[]{:S(2)}, u32[]{:S(2)}) collective-permute-start(bf16[528,128]{1,0:T(8,128)(2,1)S(1)} %pack_other.1), channel_id=1, source_target_pairs={{0,2},{2,4},{4,6},{6,8},{8,10},{10,12},{12,14},{14,16},{16,18},{18... | collective-permute-start | bytes 405512 | tf_op jit(solution)/shard_map/ppermute | solution.py:607
  4.8 1.2 %collective-permute-start.2 = (s32[4,8]{1,0:T(4,128)S(1)}, s32[4,8]{1,0:T(4,128)S(1)}, u32[]{:S(2)}, u32[]{:S(2)}) collective-permute-start(s32[4,8]{1,0:T(4,128)S(1)} %get-tuple-element.48.shifts), channel_id=1, source_target_pairs={{0,1},{1,0},{2,3},{3,2},{4,5},{5,4},{6,7},{7,6},{8,9},{9,8},{10,11... | collective-permute-start | bytes 392 | tf_op jit(solution)/shard_map/ppermute | solution.py:563
  8.2 2.5 %collective-permute-start.3 = (bf16[528,128]{1,0:T(8,128)(2,1)S(1)}, bf16[528,128]{1,0:T(8,128)(2,1)S(1)}, u32[]{:S(2)}, u32[]{:S(2)}) collective-permute-start(bf16[528,128]{1,0:T(8,128)(2,1)S(1)} %collective-permute-done.1.got_ref), channel_id=1, source_target_pairs={{0,1},{1,0},{2,3},{3,2},{4,5},{5,4},{6,7},{7,6},{8,9},{9,8},{10,11... | collective-permute-start | bytes 405512 | tf_op jit(solution)/shard_map/ppermute | solution.py:563

commit v14 on v12

--- a/solution.py
+++ b/solution.py
@@ -117,11 +117,12 @@
     blocks, tails = laid_out(pairs, lanes)
     for v, block in enumerate(blocks):
         part_ref[v * MAX_SHIFT : (v + 1) * MAX_SHIFT] = block.astype(jnp.bfloat16)
-    for copy in copies[1:]:
-        copy.wait()
+    copies[1].wait()
     extra = turned_ref(ref_ref, few)[0:8]
     tails = jnp.concatenate([tails[0:8] + extra, tails[8:]], axis=0)
     part_ref[views * MAX_SHIFT :] = tails.astype(jnp.bfloat16)
+    for copy in copies[2:]:
+        copy.wait()
 
 
 def pack_other_body(part_ref, pick_ref, other_order_ref, other_ref, packet_ref):

time: 13.8 us -> 13.8 us (level)
  no operation moved by 1% of the time
where the time goes in v14:
time: 13.8 us; the launch traced here: 13.7 us
  Pallas kernels  7.9 us (57%)
  starting transfers between devices  4.27 us (31%)
  waiting for transfers between devices  1 us (7%)
  local copies, waits for them, and re-layouts  0.39 us (3%)
    pallas_call x1, Pallas kernels, per_device(): pl.pallas_call(outer_body, out_shape=shape((GROUPS, planes, rows, width),...  3 us
    pallas_call x1, Pallas kernels, per_device(): pl.pallas_call(inner_body, out_shape=[shape((views, width, lanes), bf16),...  2.21 us
    ppermute x3, starting transfers between devices, swap_planes(): return lax.ppermute(value, 'plane', [(0, 1), (1, 0)])  2.17 us
    ppermute x1, starting transfers between devices, per_device(): got = lax.ppermute(packet, ('tile', 'plane'), pairs)  2.11 us
    pallas_call x1, Pallas kernels, per_device(): pl.pallas_call(pack_own_body, out_shape=[shape(x.shape, x.dtype) for x in...  1.61 us
    ppermute x3, waiting for transfers between devices, swap_planes(): return lax.ppermute(value, 'plane', [(0, 1), (1, 0)])  1 us
    pallas_call x1, Pallas kernels, per_device(): pl.pallas_call(late_body, out_shape=shape((late_rows, out_lanes), bf16),...  0.71 us
    pallas_call x1, Pallas kernels, per_device(): pl.pallas_call(pack_other_body, out_shape=packet_shape, in_specs=[whole(v...  0.38 us
  transfers between devices with their start and end apart: 4, of which 2 were waited for; matrix products, arithmetic and copies ran while one was open for 3% of the time, Pallas kernels for 33%

profile of v14, /device:TPU:25, one launch (start us, length us, event | category | flops | bytes accessed | tf_op | source)
XLA Modules:
  0.0 13.7 jit_solution(4569598903177163985)
XLA Ops:
  0.0 0.7 %collective-permute-start = (bf16[4,16,4,256]{3,2,1,0:T(4,128)(2,1)}, bf16[4,16,4,256]{3,2,1,0:T(4,128)(2,1)S(1)}, u32[]{:S(2)}, u32[]{:S(2)}) collective-permute-start(bf16[4,16,4,256]{3,2,1,0:T(4,128)(2,1)} %refs_0_.1), channel_id=1, source_target_pairs={{0,1},{1,0},{2,3},{3,2},{4,5},{5,4},{6,7},{7,6},{8,9},{9,8},{10,11... | collective-permute-start | bytes 393224 | tf_op jit(solution)/shard_map/ppermute | solution.py:563
  0.7 1.6 %pack_own.1 = (bf16[4,16,4,256]{3,2,1,0:T(4,128)(2,1)S(1)}, bf16[32,4,256]{2,1,0:T(4,128)(2,1)S(1)}, s32[4,8]{1,0:T(4,128)S(1)}, f32[8]{0:T(128)S(1)}, f32[8]{0:...) custom-call(bf16[4,16,4,256]{3,2,1,0:T(4,128)(2,1)} %refs_0_.1, ...), custom_call_target="tpu_custom_call" | custom-call | tf_op jit(solution)/shard_map/pack_own/pallas_call | solution.py:584
  2.3 0.0 collective-permute-done.other_ref
  2.3 0.0 copy-start
  2.3 0.0 copy-start.1
  2.3 0.4 %pack_other.1 = bf16[528,128]{1,0:T(8,128)(2,1)S(1)} custom-call(bf16[528,128]{1,0:T(8,128)(2,1)S(1)} %get-tuple-element.43.part_ref, bf16[136,256]{1,0:T(8,128)(2,1)S(1)} %get-tuple-element.44.pick_ref, bf16[128,256]{1,0:T(8,128)(2,1)S(1)} %get-tuple-element.45.other_order_ref, bf16[4,16,4,256]{3,2,1,0:T(4,128)(2,1)S(1)} %collective-permute-done.other_ref), custom_call_target="tpu_custom_call" | custom-call | tf_op jit(solution)/shard_map/pack_other/pallas_call | solution.py:595
  2.7 2.1 %collective-permute-start.1 = (bf16[528,128]{1,0:T(8,128)(2,1)S(1)}, bf16[528,128]{1,0:T(8,128)(2,1)S(1)}, u32[]{:S(2)}, u32[]{:S(2)}) collective-permute-start(bf16[528,128]{1,0:T(8,128)(2,1)S(1)} %pack_other.1), channel_id=1, source_target_pairs={{0,2},{2,4},{4,6},{6,8},{8,10},{10,12},{12,14},{14,16},{16,18},{18... | collective-permute-start | bytes 405512 | tf_op jit(solution)/shard_map/ppermute | solution.py:607
  4.8 0.0 collective-permute-start.2
  4.8 0.0 copy-done
  4.8 0.0 copy-done.1
  4.9 0.1 stack_reshape.7
  5.0 0.1 stack_reshape.6
  5.1 0.1 copy.17.taps_ref
  5.3 0.7 %collective-permute-done.2.before.after = s32[4,8]{1,0:T(4,128)S(1)} collective-permute-done((s32[4,8]{1,0:T(4,128)S(1)}, s32[4,8]{1,0:T(4,128)S(1)}, u32[]{:S(2)}, u32[]{:S(2)}) %collective-permute-start.2) | collective-permute-done | bytes 160 | tf_op jit(solution)/shard_map/ppermute | solution.py:563
  6.0 2.2 %inner_columns.1 = (bf16[4,256,128]{2,1,0:T(8,128)(2,1)S(1)}, bf16[256,128]{1,0:T(8,128)(2,1)S(1)}, s32[8,128]{1,0:T(8,128)S(1)}, f32[8,384]{1,0:T(8,128)S(1)}, ...) custom-call(s32[4,8]{1,0:T(4,128)S(1)} %get-tuple-element.48.shifts,, ...), custom_call_target="tpu_custom_call" | custom-call | flops 3000000000 | bytes 1000000 | tf_op jit(solution)/shard_map/inner_columns/pallas_call | solution.py:627
  8.2 0.0 collective-permute-done.1.got_ref
  8.2 1.5 %collective-permute-start.3 = (bf16[528,128]{1,0:T(8,128)(2,1)S(1)}, bf16[528,128]{1,0:T(8,128)(2,1)S(1)}, u32[]{:S(2)}, u32[]{:S(2)}) collective-permute-start(bf16[528,128]{1,0:T(8,128)(2,1)S(1)} %collective-permute-done.1.got_ref), channel_id=1, source_target_pairs={{0,1},{1,0},{2,3},{3,2},{4,5},{5,4},{6,7},{7,6},{8,9},{9,8},{10,11... | collective-permute-start | bytes 405512 | tf_op jit(solution)/shard_map/ppermute | solution.py:563
  9.7 0.7 %late_columns.1.late_ref = bf16[128,256]{1,0:T(8,128)(2,1)S(1)} custom-call(f32[552,384]{1,0:T(8,128)S(1)} %get-tuple-element.78.match, f32[552,384]{1,0:T(8,128)S(1)} %get-tuple-element.79.first, f32[8,384]{1,0:T(8,128)S(1)} %get-tuple-element.72.table_ref, bf16[256,256]{1,0:T(8,128)(2,1)S(1)} %get-tuple-element.73.spread_ref, ...), custom_call_target="tpu_custom_call" | custom-call | flops 2000000000 | bytes 1000000 | tf_op jit(solution)/shard_map/late_columns/pallas_call | solution.py:673
  10.4 0.3 %collective-permute-done.3.swapped_ref = bf16[528,128]{1,0:T(8,128)(2,1)S(1)} collective-permute-done((bf16[528,128]{1,0:T(8,128)(2,1)S(1)}, bf16[528,128]{1,0:T(8,128)(2,1)S(1)}, u32[]{:S(2)}, u32[]{:S(2)}) %collective-permute-start.3) | collective-permute-done | bytes 135200 | tf_op jit(solution)/shard_map/ppermute | solution.py:563
  10.7 3.0 %outer_columns.1 = bf16[8,8,4,256]{3,2,1,0:T(4,128)(2,1)} custom-call(bf16[4,256,128]{2,1,0:T(8,128)(2,1)S(1)} %get-tuple-element.69.cols_ref, bf16[256,128]{1,0:T(8,128)(2,1)S(1)} %get-tuple-element.70.ref_cols_ref, s32[8,128]{1,0:T(8,128)S(1)} %get-tuple-element.71.word_ref, f32[8,384]{1,0:T(8,128)S(1)} %get-tuple-element.72.table_ref, ...), custom_call_target="tpu_custom_call" | custom-call | tf_op jit(solution)/shard_map/outer_columns/pallas_call | solution.py:685
  (4 shorter events, 0.1 us)
Async XLA Ops:
  0.0 2.3 %collective-permute-start = (bf16[4,16,4,256]{3,2,1,0:T(4,128)(2,1)}, bf16[4,16,4,256]{3,2,1,0:T(4,128)(2,1)S(1)}, u32[]{:S(2)}, u32[]{:S(2)}) collective-permute-start(bf16[4,16,4,256]{3,2,1,0:T(4,128)(2,1)} %refs_0_.1), channel_id=1, source_target_pairs={{0,1},{1,0},{2,3},{3,2},{4,5},{5,4},{6,7},{7,6},{8,9},{9,8},{10,11... | collective-permute-start | bytes 393224 | tf_op jit(solution)/shard_map/ppermute | solution.py:563
  2.3 2.5 %copy-start = (bf16[8,8,3,3,3]{1,0,4,3,2:T(8,128)(2,1)S(1)}, bf16[8,8,3,3,3]{1,0,4,3,2:T(8,128)(2,1)}, u32[]{:S(2)}) copy-start(bf16[8,8,3,3,3]{1,0,4,3,2:T(8,128)(2,1)} %param.13) | copy-start | bytes 10372
  2.3 2.5 %copy-start.1 = (bf16[8,8,3,3,3]{1,0,4,3,2:T(8,128)(2,1)S(1)}, bf16[8,8,3,3,3]{1,0,4,3,2:T(8,128)(2,1)}, u32[]{:S(2)}) copy-start(bf16[8,8,3,3,3]{1,0,4,3,2:T(8,128)(2,1)} %param.11) | copy-start | bytes 10372
  2.7 5.5 %collective-permute-start.1 = (bf16[528,128]{1,0:T(8,128)(2,1)S(1)}, bf16[528,128]{1,0:T(8,128)(2,1)S(1)}, u32[]{:S(2)}, u32[]{:S(2)}) collective-permute-start(bf16[528,128]{1,0:T(8,128)(2,1)S(1)} %pack_other.1), channel_id=1, source_target_pairs={{0,2},{2,4},{4,6},{6,8},{8,10},{10,12},{12,14},{14,16},{16,18},{18... | collective-permute-start | bytes 405512 | tf_op jit(solution)/shard_map/ppermute | solution.py:607
  4.8 1.2 %collective-permute-start.2 = (s32[4,8]{1,0:T(4,128)S(1)}, s32[4,8]{1,0:T(4,128)S(1)}, u32[]{:S(2)}, u32[]{:S(2)}) collective-permute-start(s32[4,8]{1,0:T(4,128)S(1)} %get-tuple-element.48.shifts), channel_id=1, source_target_pairs={{0,1},{1,0},{2,3},{3,2},{4,5},{5,4},{6,7},{7,6},{8,9},{9,8},{10,11... | collective-permute-start | bytes 392 | tf_op jit(solution)/shard_map/ppermute | solution.py:563
  8.2 2.5 %collective-permute-start.3 = (bf16[528,128]{1,0:T(8,128)(2,1)S(1)}, bf16[528,128]{1,0:T(8,128)(2,1)S(1)}, u32[]{:S(2)}, u32[]{:S(2)}) collective-permute-start(bf16[528,128]{1,0:T(8,128)(2,1)S(1)} %collective-permute-done.1.got_ref), channel_id=1, source_target_pairs={{0,1},{1,0},{2,3},{3,2},{4,5},{5,4},{6,7},{7,6},{8,9},{9,8},{10,11... | collective-permute-start | bytes 405512 | tf_op jit(solution)/shard_map/ppermute | solution.py:563

commit v15 on v12

--- a/solution.py
+++ b/solution.py
@@ -517,7 +517,7 @@
     def filled(v):
         at = v * tall
         pieces = [
-            (at + r, LEAD - 2 + r, EDGE - 2 + r, min(48, main - r)) for r in range(0, main, 48)
+            (at + r, LEAD - 2 + r, EDGE - 2 + r, min(24, main - r)) for r in range(0, main, 24)
         ]
         pieces += [(at + main, LEAD + width - 4, EDGE + width - 4, 8)]
         fill(pieces, near[v], src.at[v], wide, match, table_ref, block)

time: 13.8 us -> 13.8 us (level)
  no operation moved by 1% of the time
where the time goes in v15:
time: 13.8 us; the launch traced here: 13.7 us
  Pallas kernels  7.91 us (57%)
  starting transfers between devices  4.27 us (31%)
  waiting for transfers between devices  1 us (7%)
  local copies, waits for them, and re-layouts  0.39 us (3%)
    pallas_call x1, Pallas kernels, per_device(): pl.pallas_call(outer_body, out_shape=shape((GROUPS, planes, rows, width),...  3.01 us
    pallas_call x1, Pallas kernels, per_device(): pl.pallas_call(inner_body, out_shape=[shape((views, width, lanes), bf16),...  2.22 us
    ppermute x3, starting transfers between devices, swap_planes(): return lax.ppermute(value, 'plane', [(0, 1), (1, 0)])  2.16 us
    ppermute x1, starting transfers between devices, per_device(): got = lax.ppermute(packet, ('tile', 'plane'), pairs)  2.11 us
    pallas_call x1, Pallas kernels, per_device(): pl.pallas_call(pack_own_body, out_shape=[shape(x.shape, x.dtype) for x in...  1.61 us
    ppermute x3, waiting for transfers between devices, swap_planes(): return lax.ppermute(value, 'plane', [(0, 1), (1, 0)])  1 us
    pallas_call x1, Pallas kernels, per_device(): pl.pallas_call(late_body, out_shape=shape((late_rows, out_lanes), bf16),...  0.71 us
    pallas_call x1, Pallas kernels, per_device(): pl.pallas_call(pack_other_body, out_shape=packet_shape, in_specs=[whole(v...  0.38 us
  transfers between devices with their start and end apart: 4, of which 2 were waited for; matrix products, arithmetic and copies ran while one was open for 3% of the time, Pallas kernels for 33%

profile of v15, /device:TPU:25, one launch (start us, length us, event | category | flops | bytes accessed | tf_op | source)
XLA Modules:
  0.0 13.7 jit_solution(11703072865457764334)
XLA Ops:
  0.0 0.7 %collective-permute-start = (bf16[4,16,4,256]{3,2,1,0:T(4,128)(2,1)}, bf16[4,16,4,256]{3,2,1,0:T(4,128)(2,1)S(1)}, u32[]{:S(2)}, u32[]{:S(2)}) collective-permute-start(bf16[4,16,4,256]{3,2,1,0:T(4,128)(2,1)} %refs_0_.1), channel_id=1, source_target_pairs={{0,1},{1,0},{2,3},{3,2},{4,5},{5,4},{6,7},{7,6},{8,9},{9,8},{10,11... | collective-permute-start | bytes 393224 | tf_op jit(solution)/shard_map/ppermute | solution.py:562
  0.7 1.6 %pack_own.1 = (bf16[4,16,4,256]{3,2,1,0:T(4,128)(2,1)S(1)}, bf16[32,4,256]{2,1,0:T(4,128)(2,1)S(1)}, s32[4,8]{1,0:T(4,128)S(1)}, f32[8]{0:T(128)S(1)}, f32[8]{0:...) custom-call(bf16[4,16,4,256]{3,2,1,0:T(4,128)(2,1)} %refs_0_.1, ...), custom_call_target="tpu_custom_call" | custom-call | tf_op jit(solution)/shard_map/pack_own/pallas_call | solution.py:583
  2.3 0.0 collective-permute-done.other_ref
  2.3 0.0 copy-start
  2.3 0.0 copy-start.1
  2.3 0.4 %pack_other.1 = bf16[528,128]{1,0:T(8,128)(2,1)S(1)} custom-call(bf16[528,128]{1,0:T(8,128)(2,1)S(1)} %get-tuple-element.43.part_ref, bf16[136,256]{1,0:T(8,128)(2,1)S(1)} %get-tuple-element.44.pick_ref, bf16[128,256]{1,0:T(8,128)(2,1)S(1)} %get-tuple-element.45.other_order_ref, bf16[4,16,4,256]{3,2,1,0:T(4,128)(2,1)S(1)} %collective-permute-done.other_ref), custom_call_target="tpu_custom_call" | custom-call | tf_op jit(solution)/shard_map/pack_other/pallas_call | solution.py:594
  2.7 2.1 %collective-permute-start.1 = (bf16[528,128]{1,0:T(8,128)(2,1)S(1)}, bf16[528,128]{1,0:T(8,128)(2,1)S(1)}, u32[]{:S(2)}, u32[]{:S(2)}) collective-permute-start(bf16[528,128]{1,0:T(8,128)(2,1)S(1)} %pack_other.1), channel_id=1, source_target_pairs={{0,2},{2,4},{4,6},{6,8},{8,10},{10,12},{12,14},{14,16},{16,18},{18... | collective-permute-start | bytes 405512 | tf_op jit(solution)/shard_map/ppermute | solution.py:606
  4.8 0.0 collective-permute-start.2
  4.8 0.0 copy-done
  4.8 0.0 copy-done.1
  4.9 0.1 stack_reshape.7
  5.0 0.1 stack_reshape.6
  5.1 0.1 copy.17.taps_ref
  5.3 0.7 %collective-permute-done.2.before.after = s32[4,8]{1,0:T(4,128)S(1)} collective-permute-done((s32[4,8]{1,0:T(4,128)S(1)}, s32[4,8]{1,0:T(4,128)S(1)}, u32[]{:S(2)}, u32[]{:S(2)}) %collective-permute-start.2) | collective-permute-done | bytes 160 | tf_op jit(solution)/shard_map/ppermute | solution.py:562
  6.0 2.2 %inner_columns.1 = (bf16[4,256,128]{2,1,0:T(8,128)(2,1)S(1)}, bf16[256,128]{1,0:T(8,128)(2,1)S(1)}, s32[8,128]{1,0:T(8,128)S(1)}, f32[8,384]{1,0:T(8,128)S(1)}, ...) custom-call(s32[4,8]{1,0:T(4,128)S(1)} %get-tuple-element.48.shifts,, ...), custom_call_target="tpu_custom_call" | custom-call | flops 3000000000 | bytes 1000000 | tf_op jit(solution)/shard_map/inner_columns/pallas_call | solution.py:626
  8.2 0.0 collective-permute-done.1.got_ref
  8.2 1.5 %collective-permute-start.3 = (bf16[528,128]{1,0:T(8,128)(2,1)S(1)}, bf16[528,128]{1,0:T(8,128)(2,1)S(1)}, u32[]{:S(2)}, u32[]{:S(2)}) collective-permute-start(bf16[528,128]{1,0:T(8,128)(2,1)S(1)} %collective-permute-done.1.got_ref), channel_id=1, source_target_pairs={{0,1},{1,0},{2,3},{3,2},{4,5},{5,4},{6,7},{7,6},{8,9},{9,8},{10,11... | collective-permute-start | bytes 405512 | tf_op jit(solution)/shard_map/ppermute | solution.py:562
  9.7 0.7 %late_columns.1.late_ref = bf16[128,256]{1,0:T(8,128)(2,1)S(1)} custom-call(f32[552,384]{1,0:T(8,128)S(1)} %get-tuple-element.78.match, f32[552,384]{1,0:T(8,128)S(1)} %get-tuple-element.79.first, f32[8,384]{1,0:T(8,128)S(1)} %get-tuple-element.72.table_ref, bf16[256,256]{1,0:T(8,128)(2,1)S(1)} %get-tuple-element.73.spread_ref, ...), custom_call_target="tpu_custom_call" | custom-call | flops 2000000000 | bytes 1000000 | tf_op jit(solution)/shard_map/late_columns/pallas_call | solution.py:672
  10.4 0.3 %collective-permute-done.3.swapped_ref = bf16[528,128]{1,0:T(8,128)(2,1)S(1)} collective-permute-done((bf16[528,128]{1,0:T(8,128)(2,1)S(1)}, bf16[528,128]{1,0:T(8,128)(2,1)S(1)}, u32[]{:S(2)}, u32[]{:S(2)}) %collective-permute-start.3) | collective-permute-done | bytes 135200 | tf_op jit(solution)/shard_map/ppermute | solution.py:562
  10.7 3.0 %outer_columns.1 = bf16[8,8,4,256]{3,2,1,0:T(4,128)(2,1)} custom-call(bf16[4,256,128]{2,1,0:T(8,128)(2,1)S(1)} %get-tuple-element.69.cols_ref, bf16[256,128]{1,0:T(8,128)(2,1)S(1)} %get-tuple-element.70.ref_cols_ref, s32[8,128]{1,0:T(8,128)S(1)} %get-tuple-element.71.word_ref, f32[8,384]{1,0:T(8,128)S(1)} %get-tuple-element.72.table_ref, ...), custom_call_target="tpu_custom_call" | custom-call | tf_op jit(solution)/shard_map/outer_columns/pallas_call | solution.py:684
  (4 shorter events, 0.1 us)
Async XLA Ops:
  0.0 2.3 %collective-permute-start = (bf16[4,16,4,256]{3,2,1,0:T(4,128)(2,1)}, bf16[4,16,4,256]{3,2,1,0:T(4,128)(2,1)S(1)}, u32[]{:S(2)}, u32[]{:S(2)}) collective-permute-start(bf16[4,16,4,256]{3,2,1,0:T(4,128)(2,1)} %refs_0_.1), channel_id=1, source_target_pairs={{0,1},{1,0},{2,3},{3,2},{4,5},{5,4},{6,7},{7,6},{8,9},{9,8},{10,11... | collective-permute-start | bytes 393224 | tf_op jit(solution)/shard_map/ppermute | solution.py:562
  2.3 2.5 %copy-start = (bf16[8,8,3,3,3]{1,0,4,3,2:T(8,128)(2,1)S(1)}, bf16[8,8,3,3,3]{1,0,4,3,2:T(8,128)(2,1)}, u32[]{:S(2)}) copy-start(bf16[8,8,3,3,3]{1,0,4,3,2:T(8,128)(2,1)} %param.13) | copy-start | bytes 10372
  2.3 2.5 %copy-start.1 = (bf16[8,8,3,3,3]{1,0,4,3,2:T(8,128)(2,1)S(1)}, bf16[8,8,3,3,3]{1,0,4,3,2:T(8,128)(2,1)}, u32[]{:S(2)}) copy-start(bf16[8,8,3,3,3]{1,0,4,3,2:T(8,128)(2,1)} %param.11) | copy-start | bytes 10372
  2.7 5.5 %collective-permute-start.1 = (bf16[528,128]{1,0:T(8,128)(2,1)S(1)}, bf16[528,128]{1,0:T(8,128)(2,1)S(1)}, u32[]{:S(2)}, u32[]{:S(2)}) collective-permute-start(bf16[528,128]{1,0:T(8,128)(2,1)S(1)} %pack_other.1), channel_id=1, source_target_pairs={{0,2},{2,4},{4,6},{6,8},{8,10},{10,12},{12,14},{14,16},{16,18},{18... | collective-permute-start | bytes 405512 | tf_op jit(solution)/shard_map/ppermute | solution.py:606
  4.8 1.2 %collective-permute-start.2 = (s32[4,8]{1,0:T(4,128)S(1)}, s32[4,8]{1,0:T(4,128)S(1)}, u32[]{:S(2)}, u32[]{:S(2)}) collective-permute-start(s32[4,8]{1,0:T(4,128)S(1)} %get-tuple-element.48.shifts), channel_id=1, source_target_pairs={{0,1},{1,0},{2,3},{3,2},{4,5},{5,4},{6,7},{7,6},{8,9},{9,8},{10,11... | collective-permute-start | bytes 392 | tf_op jit(solution)/shard_map/ppermute | solution.py:562
  8.2 2.5 %collective-permute-start.3 = (bf16[528,128]{1,0:T(8,128)(2,1)S(1)}, bf16[528,128]{1,0:T(8,128)(2,1)S(1)}, u32[]{:S(2)}, u32[]{:S(2)}) collective-permute-start(bf16[528,128]{1,0:T(8,128)(2,1)S(1)} %collective-permute-done.1.got_ref), channel_id=1, source_target_pairs={{0,1},{1,0},{2,3},{3,2},{4,5},{5,4},{6,7},{7,6},{8,9},{9,8},{10,11... | collective-permute-start | bytes 405512 | tf_op jit(solution)/shard_map/ppermute | solution.py:562
